TPU v7x, 32 devices: a whole 2x2x4 slice. The times are simulated.
32 devices in a mesh: blk: 8 (over y, x, core), shard: 4 (over z).
Axes of the slice: x: 2, y: 2, z: 4, core: 2. Of those that a mesh axis runs over, the one named last changes fastest.
Arguments:
- queries: bfloat16 [2048, 2560], P('blk', 'shard'), may hold values from -256 to 256
- key_rows: bfloat16 [2048, 2560], P('blk', 'shard'), may hold values from -6 to 6
- values: bfloat16 [2048, 2560], P('blk', 'shard'), may hold values from -6 to 6
- segment_ids: int32 [8, 256], P('blk'), may hold values from 0 to 3, never falling along the last dimension, each value on 1 to 128 neighbouring positions
- residual: bfloat16 [2048, 2560], P('blk', 'shard'), may hold values from -6 to 6
- out_weight: bfloat16 [2560, 2560], P('shard', 'blk'), may hold values from -0.125 to 0.125
- cotangent: bfloat16 [2048, 2560], P('blk', 'shard'), may hold values from -6 to 6
Outputs:
- layer_out: bfloat16 [2048, 2560], P('blk', 'shard')
- weight_grad: float32 [2560, 2560], P('blk', 'shard')
- query_grad: bfloat16 [2048, 2560], P('blk', 'shard')
- key_grad: bfloat16 [2048, 2560], P('blk', 'shard')
- value_grad: bfloat16 [2048, 2560], P('blk', 'shard')
Inputs may be any that keep to these rules, and one draw needn't show every extreme that they name: `segment_ids`: in each worker's row the document numbers never fall, and each document has 1 to 128 tokens.
All inputs are finite; a program needn't handle non-finite values.
Results may differ from a plain program's by a relative error of at most 0.0059.
Values may be sent and summed in bfloat16 or wider, within the bound.
No kernel may reach another device: no remote copies, remote signals or barrier semaphores. Data moves between devices by JAX's collectives and lax.ppermute only.
A program may use at most 128 MiB of HBM per device.

v0:
```python
import math

import jax
import jax.numpy as jnp
from jax import lax
from jax.sharding import PartitionSpec as P

HEAD = 128


masked_fill = -1e30


def attention_probs(q_three, k_three, seg_row):
    count = q_three.shape[0]
    scores = jnp.einsum("qhd,khd->hqk", q_three, k_three, preferred_element_type=jnp.float32)
    scores = scores * (1.0 / math.sqrt(HEAD))
    places = jnp.arange(count, dtype=jnp.int32)
    allowed = (places[None, :] <= places[:, None]) & (seg_row[None, :] == seg_row[:, None])
    scores = jnp.where(allowed[None], scores, masked_fill)
    highest = jnp.max(scores, axis=-1, keepdims=True)
    weights = jnp.exp(scores - highest)
    return weights / jnp.sum(weights, axis=-1, keepdims=True)


def per_device(queries, key_rows, values, segment_ids, residual, out_weight, cotangent):
    count = queries.shape[0]
    q_three = queries.reshape(count, -1, HEAD)
    k_three = key_rows.reshape(count, -1, HEAD)
    v_three = values.reshape(count, -1, HEAD)
    seg_row = segment_ids[0]
    probs = attention_probs(q_three, k_three, seg_row)
    p_low = probs.astype(jnp.bfloat16)
    context = jnp.einsum("hqk,khd->qhd", p_low, v_three, preferred_element_type=jnp.float32)
    context = context.reshape(count, -1).astype(jnp.bfloat16)
    contract_cols = (((1,), (1,)), ((), ()))
    contract_rows = (((0,), (0,)), ((), ()))
    weight_rows = lax.all_gather(out_weight, "blk", axis=1, tiled=True)
    partial_value = jnp.dot(context, weight_rows, preferred_element_type=jnp.float32)
    summed = lax.psum_scatter(partial_value, "shard", scatter_dimension=1, tiled=True)
    layer_out = (residual.astype(jnp.float32) + summed).astype(jnp.bfloat16)
    full_cot = lax.all_gather(cotangent, "shard", axis=1, tiled=True)
    d_context = lax.dot_general(
        full_cot, weight_rows, contract_cols, preferred_element_type=jnp.float32
    )
    d_context = d_context.astype(jnp.bfloat16)
    grad_scale = 1.0 / math.sqrt(count * lax.axis_size("blk"))
    local_grad = lax.dot_general(
        full_cot, context, contract_rows, preferred_element_type=jnp.float32
    )
    owned = jnp.sum(
        lax.all_to_all(local_grad[None], "blk", split_axis=1, concat_axis=0, tiled=True), axis=0
    )
    weight_grad = owned * grad_scale
    dctx_three = d_context.reshape(count, -1, HEAD)
    d_probs = jnp.einsum("qhd,khd->hqk", dctx_three, v_three, preferred_element_type=jnp.float32)
    v_grad = jnp.einsum("hqk,qhd->khd", p_low, dctx_three, preferred_element_type=jnp.float32)
    inner = jnp.sum(probs * d_probs, axis=-1, keepdims=True)
    d_scores = (probs * (d_probs - inner)).astype(jnp.bfloat16)
    scale = 1.0 / math.sqrt(HEAD)
    q_grad = (
        jnp.einsum("hqk,khd->qhd", d_scores, k_three, preferred_element_type=jnp.float32) * scale
    )
    k_grad = (
        jnp.einsum("hqk,qhd->khd", d_scores, q_three, preferred_element_type=jnp.float32) * scale
    )
    return (
        layer_out,
        weight_grad,
        q_grad.reshape(count, -1).astype(jnp.bfloat16),
        k_grad.reshape(count, -1).astype(jnp.bfloat16),
        v_grad.reshape(count, -1).astype(jnp.bfloat16),
    )


def solution(mesh):
    placed = (
        P("blk", "shard"),
        P("blk", "shard"),
        P("blk", "shard"),
        P("blk", None),
        P("blk", "shard"),
        P("shard", "blk"),
        P("blk", "shard"),
    )
    return jax.shard_map(
        per_device,
        mesh=mesh,
        in_specs=placed,
        out_specs=(
            P("blk", "shard"),
            P("blk", "shard"),
            P("blk", "shard"),
            P("blk", "shard"),
            P("blk", "shard"),
        ),
        check_vma=False,
    )
```

profile of v0, /device:TPU:0, one launch (start us, length us, event | category | flops | bytes accessed | tf_op | source)
XLA Modules:
  0.0 169.1 jit_solution(9650711272005702907)
XLA Ops:
  7.2 0.0 copy-start.9
  7.2 0.0 copy-start.10
  7.2 0.0 copy-start.13
  7.2 0.0 all-gather.5.cloned.1.call-start
  7.2 0.7 all-gather.5.cloned.1.call-update
  7.9 0.0 all-gather.3.cloned.1.call-start
  8.0 0.7 all-gather.3.cloned.1.call-update
  8.7 1.1 copy.43
  9.8 0.0 copy-done.9
  9.8 0.0 copy-start.4
  9.8 0.2 copy.44
  10.0 0.0 copy-done.10
  10.0 0.0 copy-start.6
  10.1 0.2 copy.47
  10.2 0.0 copy-start.11
  10.2 0.0 copy-done.13
  10.3 0.1 fusion.8
  10.4 0.6 fusion.12
  11.0 0.0 copy-done.4
  11.0 0.0 copy-done.6
  11.0 0.0 copy-start.2
  11.0 0.0 copy-done.11
  11.0 0.3 convolution_convert_fusion.1
  11.3 0.8 copy-done.2
  12.1 0.0 copy-start.1
  12.1 32.5 %all-gather.5.cloned.1.call-done = bf16[256,2560]{1,0:T(8,128)(2,1)} async-done(((bf16[256,640]{1,0:T(8,128)(2,1)}), bf16[256,2560]{1,0:T(8,128)(2,1)}) %all-gather.5.cloned.1.call-update) | async-done | bytes 1310736 | tf_op jit(solution)/shard_map/all_gather | solution.py:42
  44.6 5.1 %convolution_bitcast_fusion = f32[1,2560,640]{1,2,0:T(8,128)} fusion(bf16[256,640]{0,1:T(8,128)(2,1)S(1)} %bitcast.39, bf16[256,2560]{1,0:T(8,128)(2,1)} %all-gather.5.cloned.1.call-done), kind=kOutput, calls=%fused_computation.1 | convolution fusion | flops 838860800 | bytes 8192000 | tf_op jit(solution)/shard_map/dot_general | solution.py:48
  49.7 0.0 copy-done.1
  49.7 14.2 %copy.49 = f32[1,2560,640]{2,0,1:T(1,128)} copy(f32[1,2560,640]{1,2,0:T(8,128)} %convolution_bitcast_fusion) | data formatting | bytes 13107200 | tf_op jit(solution)/shard_map/broadcast_in_dim | solution.py:52
  63.9 5.0 %all-to-all-start = ((f32[1,2560,640]{2,0,1:T(1,128)}), f32[1,2560,640]{2,0,1:T(1,128)}, u32[]{:S(2)}, u32[]{:S(2)}) async-start(f32[1,2560,640]{2,0,1:T(1,128)} %copy.49), calls=%async_computation.1 | async-start | bytes 13107200 | tf_op jit(solution)/shard_map/all_to_all | solution.py:52
  68.9 0.0 reduce-scatter.2.cloned.1.call-start
  69.0 15.0 %all-gather.3.cloned.1.call-done = bf16[640,2560]{0,1:T(8,128)(2,1)} async-done(((bf16[640,320]{0,1:T(8,128)(2,1)}), bf16[640,2560]{0,1:T(8,128)(2,1)}) %all-gather.3.cloned.1.call-update) | async-done | bytes 3276816 | tf_op jit(solution)/shard_map/all_gather | solution.py:38
  84.0 0.0 copy-start
  84.0 4.9 %fusion.13 = f32[256,2560]{1,0:T(8,128)} fusion(bf16[256,640]{0,1:T(8,128)(2,1)} %bitcast.40, bf16[640,2560]{0,1:T(8,128)(2,1)} %all-gather.3.cloned.1.call-done), kind=kOutput, calls=%fused_computation.26 | convolution fusion | flops 838860800 | bytes 6225920 | tf_op jit(solution)/shard_map/dot_general | solution.py:39
  88.9 0.0 reduce-scatter.2.cloned.1.call-update
  88.9 0.0 copy-done
  88.9 3.2 %convolution_convert_fusion = bf16[256,640]{1,0:T(8,128)(2,1)} fusion(bf16[256,2560]{1,0:T(8,128)(2,1)} %all-gather.5.cloned.1.call-done, bf16[640,2560]{0,1:T(8,128)(2,1)S(1)} %copy-done), kind=kOutput, calls=%fused_computation.10 | convolution fusion | flops 839024640 | bytes 4915200 | tf_op jit(solution)/shard_map/dot_general | solution.py:43
  92.2 1.1 copy.50
  93.3 0.0 copy-start.3
  93.3 0.0 copy-start.12
  93.3 1.8 %convolution_convert_fusion.2 = bf16[5,128,256]{2,1,0:T(8,128)(2,1)S(1)} fusion(bf16[256,5,128]{0,2,1:T(8,128)(2,1)S(1)} %bitcast.49, f32[5,256,256]{1,2,0:T(8,128)} %copy-done.2, f32[5,256]{1,0:T(8,128)S(1)} %get-tuple-element.20), kind=kOutput, calls=%fused_computation.14 | convolution fusion | flops 84705280 | bytes 1971200 | tf_op jit(solution)/shard_map/hqk,qhd->khd/dot_general | solution.py:57
  95.1 0.9 copy.58
  96.0 0.0 copy-done.3
  96.0 0.0 copy-done.12
  96.1 0.4 multiply_reduce_fusion
  96.5 0.0 copy-start.7
  96.5 0.2 multiply_convert_fusion
  96.7 0.7 copy-done.7
  97.4 0.0 copy-start.5
  97.4 0.3 fusion.5
  97.7 0.9 copy.56
  98.6 0.0 copy-done.5
  98.6 0.4 fusion.4
  99.0 0.9 copy.57
  99.9 48.6 %all-to-all-done = f32[1,2560,640]{2,0,1:T(1,128)} async-done(((f32[1,2560,640]{2,0,1:T(1,128)}), f32[1,2560,640]{2,0,1:T(1,128)}, u32[]{:S(2)}, u32[]{:S(2)}) %all-to-all-start) | async-done | bytes 6553632 | tf_op jit(solution)/shard_map/all_to_all | solution.py:52
  148.4 6.1 %copy.67 = f32[1,2560,640]{2,1,0:T(8,128)} copy(f32[1,2560,640]{2,0,1:T(1,128)} %all-to-all-done) | data formatting | bytes 13107200
  154.5 3.3 %reduce_sum.28 = f32[320,640]{1,0:T(8,128)S(1)} reduce(f32[8,320,640]{2,1,0:T(8,128)} %bitcast.38, f32[]{:T(128)} %constant.2.clone.1), dimensions={0}, to_apply=%region_3.4 | reduce | flops 1433600 | bytes 7372804 | tf_op jit(solution)/shard_map/reduce_sum | solution.py:51
  157.8 0.0 copy-start.8
  157.8 1.0 broadcast_multiply_fusion
  158.8 1.9 %reduce-scatter.2.cloned.1.call-done = f32[256,640]{1,0:T(8,128)} async-done(((f32[256,2560]{1,0:T(8,128)}), f32[256,640]{1,0:T(8,128)}) %reduce-scatter.2.cloned.1.call-update) | async-done | bytes 655376 | tf_op jit(solution)/shard_map/reduce_scatter | solution.py:40
  160.7 0.0 copy-done.8
  160.7 1.9 %add_convert_fusion = bf16[256,640]{1,0:T(8,128)(2,1)} fusion(f32[256,640]{1,0:T(8,128)} %reduce-scatter.2.cloned.1.call-done, bf16[256,640]{1,0:T(8,128)(2,1)S(1)} %copy-done.8), kind=kLoop, calls=%fused_computation.15 | loop fusion | flops 491520 | bytes 1310720 | tf_op jit(solution)/shard_map/convert_element_type | solution.py:41
Async XLA Ops:
  7.2 2.7 %copy-start.9 = (bf16[256,640]{1,0:T(8,128)(2,1)S(1)}, bf16[256,640]{1,0:T(8,128)(2,1)}, u32[]{:S(2)}) copy-start(bf16[256,640]{1,0:T(8,128)(2,1)} %param.8) | copy-start | bytes 983044
  7.2 2.9 %copy-start.10 = (bf16[256,640]{1,0:T(8,128)(2,1)S(1)}, bf16[256,640]{1,0:T(8,128)(2,1)}, u32[]{:S(2)}) copy-start(bf16[256,640]{1,0:T(8,128)(2,1)} %param.9) | copy-start | bytes 983044
  7.2 3.1 %copy-start.13 = (s32[1,256]{1,0:T(1,128)S(1)}, s32[1,256]{1,0:T(1,128)}, u32[]{:S(2)}) copy-start(s32[1,256]{1,0:T(1,128)} %param.10) | copy-start | bytes 3076
  7.2 37.4 %all-gather.5.cloned.1.call-start = ((), (), s32[]{:S(2)}) async-start(), calls=%async_computation.4 | async-start | bytes 1638400 | tf_op jit(solution)/shard_map/all_gather | solution.py:42
  7.9 76.0 %all-gather.3.cloned.1.call-start = ((), (), s32[]{:S(2)}) async-start(), calls=%async_computation.2 | async-start | bytes 3686400 | tf_op jit(solution)/shard_map/all_gather | solution.py:38
  9.8 1.2 copy-start.4
  10.0 1.0 copy-start.6
  10.2 0.8 copy-start.11
  11.0 1.1 copy-start.2
  12.1 37.6 %copy-start.1 = (bf16[5,256,128]{1,2,0:T(8,128)(2,1)}, bf16[5,256,128]{1,2,0:T(8,128)(2,1)S(1)}, u32[]{:S(2)}) copy-start(bf16[5,256,128]{1,2,0:T(8,128)(2,1)S(1)} %convolution_convert_fusion.1) | copy-start | bytes 983044
  63.9 84.5 %all-to-all-start = ((f32[1,2560,640]{2,0,1:T(1,128)}), f32[1,2560,640]{2,0,1:T(1,128)}, u32[]{:S(2)}, u32[]{:S(2)}) async-start(f32[1,2560,640]{2,0,1:T(1,128)} %copy.49), calls=%async_computation.1 | async-start | bytes 13107200 | tf_op jit(solution)/shard_map/all_to_all | solution.py:52
  68.9 91.7 %reduce-scatter.2.cloned.1.call-start = ((), (), s32[]{:S(2)}) async-start(), calls=%async_computation.3 | async-start | bytes 3276800 | tf_op jit(solution)/shard_map/reduce_scatter | solution.py:40
  84.0 4.9 %copy-start = (bf16[640,2560]{0,1:T(8,128)(2,1)S(1)}, bf16[640,2560]{0,1:T(8,128)(2,1)}, u32[]{:S(2)}) copy-start(bf16[640,2560]{0,1:T(8,128)(2,1)} %all-gather.3.cloned.1.call-done) | copy-start | bytes 9830404
  93.3 2.7 %copy-start.3 = (f32[5,256,256]{1,2,0:T(8,128)S(1)}, f32[5,256,256]{1,2,0:T(8,128)}, u32[]{:S(2)}) copy-start(f32[5,256,256]{1,2,0:T(8,128)} %copy-done.2) | copy-start | bytes 3932164
  93.3 2.7 %copy-start.12 = (bf16[256,640]{0,1:T(8,128)(2,1)S(1)}, bf16[256,640]{0,1:T(8,128)(2,1)}, u32[]{:S(2)}) copy-start(bf16[256,640]{0,1:T(8,128)(2,1)} %copy-done.11) | copy-start | bytes 983044
  96.5 1.0 copy-start.7
  97.4 1.2 copy-start.5
  157.8 2.9 %copy-start.8 = (bf16[256,640]{1,0:T(8,128)(2,1)S(1)}, bf16[256,640]{1,0:T(8,128)(2,1)}, u32[]{:S(2)}) copy-start(bf16[256,640]{1,0:T(8,128)(2,1)} %param.11) | copy-start | bytes 983044
Sparse Core Ops, SparseCore 0:
  9.6 34.9 all-gather.4
  46.5 37.4 all-gather.2
  89.0 71.5 reduce-scatter.1
where the time goes:
time: 170 us; the launch traced here: 169 us
  waiting for transfers between devices  99.4 us (58%)
  local copies, waits for them, and re-layouts  27.2 us (16%)
  matrix products  16.9 us (10%)
  between operations  14 us (8%)
  other arithmetic  6.43 us (4%)
  starting transfers between devices  5.16 us (3%)
    all_to_all x1, waiting for transfers between devices, per_device(): lax.all_to_all(local_grad[None], 'blk', split_axis=1, concat_axis=0, tile...  48.6 us
    all_gather x1, waiting for transfers between devices, per_device(): full_cot = lax.all_gather(cotangent, 'shard', axis=1, tiled=True)  32.5 us
    all_gather x1, waiting for transfers between devices, per_device(): weight_rows = lax.all_gather(out_weight, 'blk', axis=1, tiled=True)  15 us
    broadcast_in_dim x1, local copies, waits for them, and re-layouts, per_device(): local_grad[None]  14.2 us
    unnamed x35, local copies, waits for them, and re-layouts  11.8 us
    dot_general x1, matrix products, per_device(): lax.dot_general(full_cot, context, contract_rows, preferred_element_type=...  5.05 us
    all_to_all x1, starting transfers between devices, per_device(): lax.all_to_all(local_grad[None], 'blk', split_axis=1, concat_axis=0, tile...  5.04 us
    dot_general x1, matrix products, per_device(): jnp.dot(context, weight_rows, preferred_element_type=jnp.float32)  4.92 us
  transfers between devices with their start and end apart: 4, of which 4 were waited for; matrix products, arithmetic and copies ran while one was open for 28% of the time, Pallas kernels for 0%

commit v1 on v0

v1 whole, which is shorter than its diff:
```python
import math

import jax
import jax.numpy as jnp
from jax import lax
from jax.experimental import pallas as pl
from jax.experimental.pallas import tpu as pltpu
from jax.sharding import PartitionSpec as P

HEAD = 128
MASKED = -1e30
F32 = jnp.float32
BF16 = jnp.bfloat16
NT = (((1,), (1,)), ((), ()))
NN = (((1,), (0,)), ((), ()))
TN = (((0,), (0,)), ((), ()))


def dot(a, b, dims):
    return lax.dot_general(a, b, dims, preferred_element_type=F32)


def call(kernel, outs, *args, flops=0):
    size = sum(math.prod(o.shape) * o.dtype.itemsize for o in (*outs, *args))
    return pl.pallas_call(
        kernel,
        out_shape=tuple(outs),
        in_specs=[pl.BlockSpec(memory_space=pltpu.VMEM)] * len(args),
        out_specs=tuple([pl.BlockSpec(memory_space=pltpu.VMEM)] * len(outs)),
        compiler_params=pltpu.CompilerParams(vmem_limit_bytes=40 * 1024 * 1024),
        cost_estimate=pl.CostEstimate(flops=flops, bytes_accessed=size, transcendentals=0),
    )(*args)


def shape(*dims, dtype=BF16):
    return jax.ShapeDtypeStruct(dims, dtype)


def visible_mask(seg_ref):
    count = seg_ref.shape[1]
    seg = jnp.broadcast_to(seg_ref[...].astype(F32), (count, count))
    rows = lax.broadcasted_iota(jnp.int32, (count, count), 0)
    cols = lax.broadcasted_iota(jnp.int32, (count, count), 1)
    return (cols <= rows) & (seg == seg.T)


def head_probs(q, k, allowed):
    scores = dot(q, k, NT) * (1.0 / math.sqrt(HEAD))
    scores = jnp.where(allowed, scores, MASKED)
    weights = jnp.exp(scores - jnp.max(scores, axis=-1, keepdims=True))
    return weights / jnp.sum(weights, axis=-1, keepdims=True)


def forward_kernel(q_ref, k_ref, v_ref, seg_ref, ctx_ref):
    allowed = visible_mask(seg_ref)
    for h in range(q_ref.shape[1] // HEAD):
        at = pl.ds(h * HEAD, HEAD)
        probs = head_probs(q_ref[:, at], k_ref[:, at], allowed).astype(BF16)
        ctx_ref[:, at] = dot(probs, v_ref[:, at], NN).astype(BF16)


def backward_kernel(q_ref, k_ref, v_ref, seg_ref, mine_ref, other_ref, dq_ref, dk_ref, dv_ref):
    allowed = visible_mask(seg_ref)
    scale = 1.0 / math.sqrt(HEAD)
    for h in range(q_ref.shape[1] // HEAD):
        at = pl.ds(h * HEAD, HEAD)
        q, k, v = q_ref[:, at], k_ref[:, at], v_ref[:, at]
        probs = head_probs(q, k, allowed)
        d_ctx = (mine_ref[:, at] + other_ref[:, at].astype(F32)).astype(BF16)
        d_probs = dot(d_ctx, v, NT)
        dv_ref[:, at] = dot(probs.astype(BF16), d_ctx, TN).astype(BF16)
        inner = jnp.sum(probs * d_probs, axis=-1, keepdims=True)
        d_scores = (probs * (d_probs - inner)).astype(BF16)
        dq_ref[:, at] = (dot(d_scores, k, NN) * scale).astype(BF16)
        dk_ref[:, at] = (dot(d_scores, q, TN) * scale).astype(BF16)


def plane_slot(plane, group):
    return plane ^ (lax.axis_index("blk") // group)


def unit_kernel(own_ref, other_ref, unit_ref):
    half, count = unit_ref.shape[0], own_ref.shape[0]
    core = lax.rem(lax.axis_index("blk"), 2)
    own, other = own_ref[...].T, other_ref[...].T
    for side in range(2):

        @pl.when(core == side)
        def _():
            rows = slice(side * half, (side + 1) * half)
            unit_ref[:, :count] = own[rows]
            unit_ref[:, count:] = other[rows]


def make_unit(own, other, strips):
    count, width = own.shape
    half = width // 2
    if strips == 1:
        return call(unit_kernel, (shape(half, 2 * count),), own, other)[0]
    core = lax.rem(lax.axis_index("blk"), 2)
    both = jnp.concatenate([own, other], axis=0).T.reshape(strips, 2, half // strips, 2 * count)
    return lax.dynamic_index_in_dim(both, core, 1, keepdims=False).reshape(half, 2 * count)


def project_kernel(sign, away, group, has_past, *refs):
    w_ref, own_ref, other_ref = refs[:3]
    past_ref, out_ref = (refs[3], refs[4]) if has_past else (None, refs[3])
    planes, count = w_ref.shape[0], own_ref.shape[0]
    z = lax.axis_index("shard")
    plane = z + sign * away

    @pl.when((plane >= 0) & (plane < planes))
    def _():
        w = w_ref[plane_slot(plane, group)]
        for i, ctx_ref in enumerate((own_ref, other_ref)):
            at = pl.ds(i * count, count)
            part = dot(w, ctx_ref[...], NT)
            if has_past:
                before = z - sign
                live = (before >= 0) & (before < planes)
                part = part + jnp.where(live, past_ref[:, at].astype(F32), 0.0)
            out_ref[:, at] = part.astype(BF16)


def project(sign, away, group, w, own, other, past):
    args = (w, own, other) + (() if past is None else (past,))
    out = shape(w.shape[1], 2 * own.shape[0])

    def kernel(*refs):
        project_kernel(sign, away, group, past is not None, *refs)

    return call(kernel, (out,), *args, flops=2 * math.prod(out.shape) * w.shape[2])[0]


def last_project_kernel(group, w_ref, own_ref, other_ref, up_ref, down_ref, keep_ref, send_ref):
    planes, count = w_ref.shape[0], own_ref.shape[0]
    z = lax.axis_index("shard")
    w = w_ref[plane_slot(z, group)]
    for i, (ctx_ref, out_ref) in enumerate(((own_ref, keep_ref), (other_ref, send_ref))):
        at = pl.ds(i * count, count)
        part = dot(w, ctx_ref[...], NT)
        part = part + jnp.where(z > 0, up_ref[:, at].astype(F32), 0.0)
        out_ref[...] = part + jnp.where(z < planes - 1, down_ref[:, at].astype(F32), 0.0)


def layer_out_kernel(residual_ref, keep_ref, other_ref, out_ref):
    half = keep_ref.shape[0]
    core = lax.rem(lax.axis_index("blk"), 2)
    keep, other = keep_ref[...], other_ref[...]
    for side, order in enumerate(((keep, other), (other, keep))):

        @pl.when(core == side)
        def _():
            total = jnp.concatenate(order, axis=0).T
            out_ref[...] = (residual_ref[...].astype(F32) + total).astype(BF16)


def make_layer_out(residual, keep, other, strips):
    count, width = residual.shape
    if strips == 1:
        return call(layer_out_kernel, (shape(count, width),), residual, keep, other)[0]
    core = lax.rem(lax.axis_index("blk"), 2)
    pair = jnp.stack([keep, other]).reshape(2, strips, -1, count)
    pair = jnp.where(core == 0, pair, pair[::-1])
    total = pair.transpose(1, 0, 2, 3).reshape(width, count)
    return (residual.astype(F32) + total.T).astype(BF16)


def for_each_plane(unit_refs, planes, body):
    z = lax.axis_index("shard")
    steps = [0] + [-k for k in range(1, planes)] + list(range(1, planes))
    for step, unit_ref in zip(steps, unit_refs):
        if step == 0:
            body(z, unit_ref)
        else:
            plane = z + step
            pl.when((plane >= 0) & (plane < planes))(lambda p=plane, u=unit_ref: body(p, u))


def d_context_kernel(group, *refs):
    *unit_refs, w_ref, mine_ref, send_ref, total = refs
    count = mine_ref.shape[0]
    total[...] = jnp.zeros_like(total)

    def body(plane, unit_ref):
        total[...] += dot(unit_ref[...], w_ref[plane_slot(plane, group)], TN)

    for_each_plane(unit_refs, w_ref.shape[0], body)
    mine_ref[...] = total[:count]
    send_ref[...] = total[count:].astype(BF16)


def weight_grad_kernel(group, planes, *refs):
    *unit_refs, own_ref, other_ref, send_a, send_b, keep_a, keep_b = refs
    count, rows = own_ref.shape[0], send_a.shape[1]

    def body(plane, unit_ref):
        slot = plane_slot(plane, group)
        part = dot(unit_ref[:, :count], own_ref[...], NN)
        part = part + dot(unit_ref[:, count:], other_ref[...], NN)
        low, high = slot & 1, slot >> 1
        first, second = part[:rows], part[rows:]

        @pl.when(low == 1)
        def _():
            send_a[high] = first.astype(BF16)

        @pl.when(low == 0)
        def _():
            keep_a[high] = first

        @pl.when(high == 1)
        def _():
            send_b[low] = second.astype(BF16)

        @pl.when(high == 0)
        def _():
            keep_b[low] = second

    for_each_plane(unit_refs, planes, body)


def half_sum_kernel(keep_a, keep_b, from_a, from_b, send_a, send_b, left_a, left_b):
    send_a[...] = (keep_a[1] + from_a[1].astype(F32)).astype(BF16)
    send_b[...] = (keep_b[1] + from_b[1].astype(F32)).astype(BF16)
    left_a[...] = keep_a[0] + from_a[0].astype(F32)
    left_b[...] = keep_b[0] + from_b[0].astype(F32)


def grad_sum_kernel(scale, left_a, left_b, from_a, from_b, out_ref):
    rows = left_a.shape[0]
    out_ref[:rows] = (left_a[...] + from_a[...].astype(F32)) * scale
    out_ref[rows:] = (left_b[...] + from_b[...].astype(F32)) * scale


def solution(mesh):
    blk, planes = mesh.shape["blk"], mesh.shape["shard"]
    chips = blk // 2
    strips = chips // planes

    def swap(value, bit):
        return lax.ppermute(value, "blk", [(i, i ^ bit) for i in range(blk)])

    def pass_up(value, first, last):
        return lax.ppermute(value, "shard", [(i, i + 1) for i in range(first, last)])

    def pass_down(value, first, last):
        return lax.ppermute(value, "shard", [(i, i - 1) for i in range(first, last, -1)])

    def per_device(queries, key_rows, values, segment_ids, residual, out_weight, cotangent):
        count = queries.shape[0]
        width = queries.shape[1]
        half = width // 2
        position = lax.axis_index("blk") // 2
        group = 2 * strips

        w_own = out_weight.T
        bit = 1
        while bit < strips:
            there = swap(w_own, 2 * bit)
            upper = (position // bit) % 2
            w_own = jnp.concatenate(
                [jnp.where(upper, there, w_own), jnp.where(upper, w_own, there)], axis=0
            )
            bit *= 2
        cut = half // 2
        a_own, b_own = w_own[:cut], w_own[cut:]
        a_one = swap(a_own, group)
        b_two = swap(b_own, 2 * group)
        cot_other = swap(cotangent, 1)
        a_pair = jnp.stack([a_own, a_one])
        b_pair = jnp.stack([b_own, b_two])
        a_high = swap(a_pair, 2 * group)
        b_low = swap(b_pair, group)
        w_all = jnp.concatenate(
            [
                jnp.concatenate([a_pair, a_high], axis=0),
                jnp.stack([b_own, b_low[0], b_two, b_low[1]]),
            ],
            axis=1,
        )

        unit = make_unit(cotangent, cot_other, strips)
        ups, downs, last = [unit], [unit], planes - 1
        for k in range(1, planes):
            ups.append(pass_up(ups[-1], k - 1, last))
            downs.append(pass_down(downs[-1], last - k + 1, 0))
        units = [unit, *ups[1:], *downs[1:]]

        ctx = call(
            forward_kernel,
            (shape(count, width),),
            queries,
            key_rows,
            values,
            segment_ids,
            flops=4 * count * count * width,
        )[0]
        ctx_other = swap(ctx, 1)

        up = down = None
        for away in range(planes - 1, 0, -1):
            up = project(1, away, group, w_all, ctx, ctx_other, up)
            down = project(-1, away, group, w_all, ctx, ctx_other, down)
            up = pass_up(up, 0, planes - away)
            down = pass_down(down, last, away - 1)

        def last_project(*refs):
            last_project_kernel(group, *refs)

        keep, send = call(
            last_project,
            (shape(half, count, dtype=F32),) * 2,
            w_all,
            ctx,
            ctx_other,
            up,
            down,
            flops=4 * half * count * width,
        )
        layer_out = make_layer_out(residual, keep, swap(send, 1), strips)

        def d_context(*refs):
            d_context_kernel(group, *refs)

        mine, send = pl.pallas_call(
            d_context,
            out_shape=(shape(count, width, dtype=F32), shape(count, width)),
            in_specs=[pl.BlockSpec(memory_space=pltpu.VMEM)] * (len(units) + 1),
            out_specs=(pl.BlockSpec(memory_space=pltpu.VMEM),) * 2,
            scratch_shapes=[pltpu.VMEM((2 * count, width), F32)],
            compiler_params=pltpu.CompilerParams(vmem_limit_bytes=40 * 1024 * 1024),
            cost_estimate=pl.CostEstimate(
                flops=4 * count * width * half * planes, bytes_accessed=1 << 23, transcendentals=0
            ),
        )(*units, w_all)
        d_ctx_other = swap(send, 1)

        def weight_parts(*refs):
            weight_grad_kernel(group, planes, *refs)

        send_a, send_b, keep_a, keep_b = call(
            weight_parts,
            (shape(2, cut, width),) * 2 + (shape(2, cut, width, dtype=F32),) * 2,
            *units,
            ctx,
            ctx_other,
            flops=4 * count * width * half * planes,
        )
        from_a, from_b = swap(send_a, group), swap(send_b, 2 * group)
        send_a, send_b, left_a, left_b = call(
            half_sum_kernel,
            (shape(cut, width),) * 2 + (shape(cut, width, dtype=F32),) * 2,
            keep_a,
            keep_b,
            from_a,
            from_b,
        )
        from_a, from_b = swap(send_a, 2 * group), swap(send_b, group)
        grad_scale = 1.0 / math.sqrt(count * blk)

        def grad_sum(*refs):
            grad_sum_kernel(grad_scale, *refs)

        total = call(
            grad_sum, (shape(half, width, dtype=F32),), left_a, left_b, from_a, from_b
        )[0]
        bit = strips // 2
        while bit >= 1:
            lower, upper = jnp.split(total, 2, axis=0)
            right = (position // bit) % 2
            sent = jnp.where(right, lower, upper)
            total = jnp.where(right, upper, lower) + swap(sent, 2 * bit)
            bit //= 2

        d_queries, d_keys, d_values = call(
            backward_kernel,
            (shape(count, width),) * 3,
            queries,
            key_rows,
            values,
            segment_ids,
            mine,
            d_ctx_other,
            flops=10 * count * count * width,
        )
        return layer_out, total, d_queries, d_keys, d_values

    spread = P("blk", "shard")
    return jax.shard_map(
        per_device,
        mesh=mesh,
        in_specs=(spread, spread, spread, P("blk", None), spread, P("shard", "blk"), spread),
        out_specs=(spread,) * 5,
        check_vma=False,
    )
```

time: 170 us -> 73.2 us (0.43)
  waiting for transfers between devices: 99.4 us -> 20 us
  starting transfers between devices: 5.16 us -> 36.4 us
  local copies, waits for them, and re-layouts: 27.2 us -> 1.25 us
  matrix products: 16.9 us -> 0 us
  Pallas kernels: 0 us -> 13.7 us
  between operations: 14 us -> 1.01 us
  other arithmetic: 6.43 us -> 0.26 us
    all_to_all x1 -> x0, waiting for transfers between devices: 48.6 us -> none  [per_device(): lax.all_to_all(local_grad[None], 'blk', split_axis=1, concat_axis=0, tile...]
    all_gather x2 -> x0, waiting for transfers between devices: 47.5 us -> none  [the longest x1 32.5 us: per_device(): full_cot = lax.all_gather(cotangent, 'shard', axis=1, tiled=True)]
    ppermute x0 -> x24, starting transfers between devices: none -> 36.4 us  [the longest x6 17.8 us: pass_up(): lax.ppermute(value, 'shard', [(i, i + 1) for i in range(first, last)])]
    ppermute x0 -> x24, waiting for transfers between devices: none -> 20 us  [the longest x12 8.7 us: swap(): return lax.ppermute(value, 'blk', [(i, i ^ bit) for i in range(blk)])]
    dot_general x8 -> x0, matrix products: 16.3 us -> none  [the longest x1 5.05 us: per_device(): lax.dot_general(full_cot, context, contract_rows, preferred_element_type=...]
    broadcast_in_dim x1 -> x0, local copies, waits for them, and re-layouts: 14.2 us -> none  [per_device(): local_grad[None]]
    pallas_call x0 -> x15, Pallas kernels: none -> 13.7 us  [the longest x14 11 us: call(): pl.pallas_call(kernel, out_shape=tuple(outs), in_specs=[pl.BlockSpec(memo...]
    unnamed x35 -> x12, local copies, waits for them, and re-layouts: 11.8 us -> 0.02 us
  transfers between devices with their start and end apart: 4 -> 24, of which waited for: 4 -> 8; matrix products, arithmetic and copies ran while one was open for 28% -> 0% of each run, Pallas kernels for 0% -> 17%
where the time goes in v1:
time: 73.2 us; the launch traced here: 72.6 us
  starting transfers between devices  36.4 us (50%)
  waiting for transfers between devices  20 us (27%)
  Pallas kernels  13.7 us (19%)
  local copies, waits for them, and re-layouts  1.25 us (2%)
  between operations  1.01 us (1%)
    ppermute x6, starting transfers between devices, pass_up(): lax.ppermute(value, 'shard', [(i, i + 1) for i in range(first, last)])  17.8 us
    ppermute x12, starting transfers between devices, swap(): return lax.ppermute(value, 'blk', [(i, i ^ bit) for i in range(blk)])  12.1 us
    pallas_call x14, Pallas kernels, call(): pl.pallas_call(kernel, out_shape=tuple(outs), in_specs=[pl.BlockSpec(memo...  11 us
    ppermute x12, waiting for transfers between devices, swap(): return lax.ppermute(value, 'blk', [(i, i ^ bit) for i in range(blk)])  8.7 us
    ppermute x6, waiting for transfers between devices, pass_up(): lax.ppermute(value, 'shard', [(i, i + 1) for i in range(first, last)])  8.65 us
    ppermute x6, starting transfers between devices, pass_down(): lax.ppermute(value, 'shard', [(i, i - 1) for i in range(first, last, -1)])  6.53 us
    ppermute x6, waiting for transfers between devices, pass_down(): lax.ppermute(value, 'shard', [(i, i - 1) for i in range(first, last, -1)])  2.66 us
    pallas_call x1, Pallas kernels, per_device(): pl.pallas_call(d_context, out_shape=(shape(count, width, dtype=F32), shap...  2.61 us
  transfers between devices with their start and end apart: 24, of which 8 were waited for; matrix products, arithmetic and copies ran while one was open for 0% of the time, Pallas kernels for 17%

profile of v1, /device:TPU:0, one launch (start us, length us, event | category | flops | bytes accessed | tf_op | source)
XLA Modules:
  0.0 72.6 jit_solution(1015826786069537121)
XLA Ops:
  0.6 0.0 copy-start.4
  0.6 0.0 copy-start.5
  0.7 1.2 %slice_bitcast_fusion.1 = (bf16[1,160,640]{2,1,0:T(8,128)(2,1)S(1)}, bf16[1,160,640]{2,1,0:T(8,128)(2,1)S(1)}, bf16[160,640]{1,0:T(8,128)(2,1)S(1)}, bf16[160,640]{1,0:T(8,128)(2,1)S(1)}) fusion(bf16[320,640]{1,0:T(8,128)(2,1)} %bitcast.11), kind=kLoop, calls=%fused_computation.4 | loop fusion | bytes 1228800 | tf_op jit(solution)/shard_map/stack | solution.py:271
  1.9 3.0 %collective-permute-start.2 = (bf16[160,640]{1,0:T(8,128)(2,1)S(1)}, bf16[160,640]{1,0:T(8,128)(2,1)S(1)}, u32[]{:S(2)}, u32[]{:S(2)}) collective-permute-start(bf16[160,640]{1,0:T(8,128)(2,1)S(1)} %get-tuple-element.37), channel_id=1, source_target_pairs={{0,16},{4,20},{8,24},{12,28},{16,0},{20,4},{24,8},{28,12},{1,17},{... | collective-permute-start | bytes 614408 | tf_op jit(solution)/shard_map/ppermute | solution.py:242
  4.9 1.5 %collective-permute-start = (bf16[160,640]{1,0:T(8,128)(2,1)S(1)}, bf16[160,640]{1,0:T(8,128)(2,1)S(1)}, u32[]{:S(2)}, u32[]{:S(2)}) collective-permute-start(bf16[160,640]{1,0:T(8,128)(2,1)S(1)} %get-tuple-element.38), channel_id=1, source_target_pairs={{0,8},{4,12},{8,0},{12,4},{16,24},{20,28},{24,16},{28,20},{1,9},{5... | collective-permute-start | bytes 614408 | tf_op jit(solution)/shard_map/ppermute | solution.py:242
  6.4 3.6 %collective-permute-done.2 = bf16[160,640]{1,0:T(8,128)(2,1)S(1)} collective-permute-done((bf16[160,640]{1,0:T(8,128)(2,1)S(1)}, bf16[160,640]{1,0:T(8,128)(2,1)S(1)}, u32[]{:S(2)}, u32[]{:S(2)}) %collective-permute-start.2) | collective-permute-done | bytes 204832 | tf_op jit(solution)/shard_map/ppermute | solution.py:242
  10.0 1.8 %collective-permute-start.3 = (bf16[2,160,640]{2,1,0:T(8,128)(2,1)S(1)}, bf16[2,160,640]{2,1,0:T(8,128)(2,1)S(1)}, u32[]{:S(2)}, u32[]{:S(2)}) collective-permute-start(bf16[2,160,640]{2,1,0:T(8,128)(2,1)S(1)} %pad_maximum_fusion.1), channel_id=1, source_target_pairs={{0,8},{4,12},{8,0},{12,4},{16,24},{20,28},{24,16},{28,20},{1,9},{5... | collective-permute-start | bytes 1228808 | tf_op jit(solution)/shard_map/ppermute | solution.py:242
  11.8 0.0 collective-permute-start.12
  11.8 0.0 collective-permute-done
  11.9 1.6 %collective-permute-start.1 = (bf16[2,160,640]{2,1,0:T(8,128)(2,1)S(1)}, bf16[2,160,640]{2,1,0:T(8,128)(2,1)S(1)}, u32[]{:S(2)}, u32[]{:S(2)}) collective-permute-start(bf16[2,160,640]{2,1,0:T(8,128)(2,1)S(1)} %pad_maximum_fusion), channel_id=1, source_target_pairs={{0,16},{4,20},{8,24},{12,28},{16,0},{20,4},{24,8},{28,12},{1,17},{... | collective-permute-start | bytes 1228808 | tf_op jit(solution)/shard_map/ppermute | solution.py:242
  13.5 1.3 %shard_map.110.refs_1_.refs_7_ = bf16[256,640]{1,0:T(8,128)(2,1)S(1)} custom-call(bf16[256,640]{1,0:T(8,128)(2,1)S(1)} %copy-done, bf16[256,640]{1,0:T(8,128)(2,1)S(1)} %copy-done.1, bf16[256,640]{1,0:T(8,128)(2,1)S(1)} %copy-done.2, s32[1,256]{1,0:T(1,128)S(1)} %copy-done.5), custom_call_target="tpu_custom_call" | custom-call | flops 167772160 | bytes 1311744 | tf_op jit(solution)/shard_map/pallas_call | solution.py:25
  14.7 0.3 collective-permute-start.4
  15.0 0.0 collective-permute-done.12.other_ref
  15.0 0.2 shard_map.119.refs_0_
  15.3 1.3 %collective-permute-start.16 = (bf16[320,512]{1,0:T(8,128)(2,1)S(1)}, bf16[320,512]{1,0:T(8,128)(2,1)S(1)}, u32[]{:S(2)}, u32[]{:S(2)}) collective-permute-start(bf16[320,512]{1,0:T(8,128)(2,1)S(1)} %shard_map.119.refs_0_), channel_id=1, source_target_pairs={{3,2},{2,1},{1,0},{7,6},{6,5},{5,4},{11,10},{10,9},{9,8},{15,14},{... | collective-permute-start | bytes 983048 | tf_op jit(solution)/shard_map/ppermute | solution.py:248
  16.6 4.6 %collective-permute-start.13 = (bf16[320,512]{1,0:T(8,128)(2,1)S(1)}, bf16[320,512]{1,0:T(8,128)(2,1)S(1)}, u32[]{:S(2)}, u32[]{:S(2)}) collective-permute-start(bf16[320,512]{1,0:T(8,128)(2,1)S(1)} %shard_map.119.refs_0_), channel_id=1, source_target_pairs={{0,1},{1,2},{2,3},{4,5},{5,6},{6,7},{8,9},{9,10},{10,11},{12,13},{... | collective-permute-start | bytes 983048 | tf_op jit(solution)/shard_map/ppermute | solution.py:245
  21.2 0.0 collective-permute-done.3
  21.2 2.6 %collective-permute-done.1 = bf16[2,160,640]{2,1,0:T(8,128)(2,1)S(1)} collective-permute-done((bf16[2,160,640]{2,1,0:T(8,128)(2,1)S(1)}, bf16[2,160,640]{2,1,0:T(8,128)(2,1)S(1)}, u32[]{:S(2)}, u32[]{:S(2)}) %collective-permute-start.1) | collective-permute-done | bytes 409632 | tf_op jit(solution)/shard_map/ppermute | solution.py:242
  23.8 0.2 maximum_maximum_fusion.refs_0_.refs_7_
  24.0 0.0 collective-permute-done.4.refs_2_.refs_8_
  24.0 0.5 shard_map.111
  24.5 3.1 %collective-permute-start.5 = (bf16[320,512]{1,0:T(8,128)(2,1)S(1)}, bf16[320,512]{1,0:T(8,128)(2,1)S(1)}, u32[]{:S(2)}, u32[]{:S(2)}) collective-permute-start(bf16[320,512]{1,0:T(8,128)(2,1)S(1)} %shard_map.111), channel_id=1, source_target_pairs={{0,1},{4,5},{8,9},{12,13},{16,17},{20,21},{24,25},{28,29}} | collective-permute-start | bytes 983048 | tf_op jit(solution)/shard_map/ppermute | solution.py:245
  27.5 0.7 collective-permute-start.8
  28.2 0.0 collective-permute-done.16.refs_4_
  28.2 1.3 %collective-permute-start.17 = (bf16[320,512]{1,0:T(8,128)(2,1)S(1)}, bf16[320,512]{1,0:T(8,128)(2,1)S(1)}, u32[]{:S(2)}, u32[]{:S(2)}) collective-permute-start(bf16[320,512]{1,0:T(8,128)(2,1)S(1)} %collective-permute-done.16.refs_4_), channel_id=1, source_target_pairs={{2,1},{1,0},{6,5},{5,4},{10,9},{9,8},{14,13},{13,12},{18,17},{17,1... | collective-permute-start | bytes 983048 | tf_op jit(solution)/shard_map/ppermute | solution.py:248
  29.5 0.0 collective-permute-done.13.refs_1_
  29.6 0.7 collective-permute-start.14
  30.2 5.0 %collective-permute-done.5.refs_3_ = bf16[320,512]{1,0:T(8,128)(2,1)S(1)} collective-permute-done((bf16[320,512]{1,0:T(8,128)(2,1)S(1)}, bf16[320,512]{1,0:T(8,128)(2,1)S(1)}, u32[]{:S(2)}, u32[]{:S(2)}) %collective-permute-start.5) | collective-permute-done | bytes 327712 | tf_op jit(solution)/shard_map/ppermute | solution.py:245
  35.3 0.4 shard_map.112
  35.7 4.4 %collective-permute-start.6 = (bf16[320,512]{1,0:T(8,128)(2,1)S(1)}, bf16[320,512]{1,0:T(8,128)(2,1)S(1)}, u32[]{:S(2)}, u32[]{:S(2)}) collective-permute-start(bf16[320,512]{1,0:T(8,128)(2,1)S(1)} %shard_map.112), channel_id=1, source_target_pairs={{0,1},{1,2},{4,5},{5,6},{8,9},{9,10},{12,13},{13,14},{16,17},{17,1... | collective-permute-start | bytes 983048 | tf_op jit(solution)/shard_map/ppermute | solution.py:245
  40.2 0.0 collective-permute-done.8.refs_3_
  40.2 0.7 collective-permute-start.9
  40.9 0.0 collective-permute-done.17.refs_5_
  40.9 1.3 %collective-permute-start.18 = (bf16[320,512]{1,0:T(8,128)(2,1)S(1)}, bf16[320,512]{1,0:T(8,128)(2,1)S(1)}, u32[]{:S(2)}, u32[]{:S(2)}) collective-permute-start(bf16[320,512]{1,0:T(8,128)(2,1)S(1)} %collective-permute-done.17.refs_5_), channel_id=1, source_target_pairs={{1,0},{5,4},{9,8},{13,12},{17,16},{21,20},{25,24},{29,28}} | collective-permute-start | bytes 983048 | tf_op jit(solution)/shard_map/ppermute | solution.py:248
  42.2 0.0 collective-permute-done.14.refs_2_
  42.2 0.7 collective-permute-start.15
  42.9 3.6 %collective-permute-done.6.refs_3_ = bf16[320,512]{1,0:T(8,128)(2,1)S(1)} collective-permute-done((bf16[320,512]{1,0:T(8,128)(2,1)S(1)}, bf16[320,512]{1,0:T(8,128)(2,1)S(1)}, u32[]{:S(2)}, u32[]{:S(2)}) %collective-permute-start.6) | collective-permute-done | bytes 327712 | tf_op jit(solution)/shard_map/ppermute | solution.py:245
  46.5 0.4 shard_map.113
  46.9 4.4 %collective-permute-start.7 = (bf16[320,512]{1,0:T(8,128)(2,1)S(1)}, bf16[320,512]{1,0:T(8,128)(2,1)S(1)}, u32[]{:S(2)}, u32[]{:S(2)}) collective-permute-start(bf16[320,512]{1,0:T(8,128)(2,1)S(1)} %shard_map.113), channel_id=1, source_target_pairs={{0,1},{1,2},{2,3},{4,5},{5,6},{6,7},{8,9},{9,10},{10,11},{12,13},{... | collective-permute-start | bytes 983048 | tf_op jit(solution)/shard_map/ppermute | solution.py:245
  51.4 0.0 collective-permute-done.9.refs_3_
  51.4 1.3 %collective-permute-start.10 = (bf16[320,512]{1,0:T(8,128)(2,1)S(1)}, bf16[320,512]{1,0:T(8,128)(2,1)S(1)}, u32[]{:S(2)}, u32[]{:S(2)}) collective-permute-start(bf16[320,512]{1,0:T(8,128)(2,1)S(1)} %shard_map.116), channel_id=1, source_target_pairs={{3,2},{2,1},{1,0},{7,6},{6,5},{5,4},{11,10},{10,9},{9,8},{15,14},{... | collective-permute-start | bytes 983048 | tf_op jit(solution)/shard_map/ppermute | solution.py:248
  52.7 0.0 collective-permute-done.18.refs_6_
  52.7 0.0 collective-permute-done.15.refs_3_
  52.7 1.9 %shard_map.120 = (bf16[2,160,640]{2,1,0:T(8,128)(2,1)S(1)}, bf16[2,160,640]{2,1,0:T(8,128)(2,1)S(1)}, f32[2,160,640]{2,1,0:T(8,128)S(1)}, f32[2,160,640]{2,1,0:T(8,128)S(1)}) custom-call(bf16[320,512]{1,0:T(8,128)(2,1)S(1)} %shard_map.119.refs_0_, bf16[320,512]{1,0:T(8,128)(2,1)S(1)} %collective-permute-done.13.refs_1_, ...), custom_call_target="tpu_custom_call" | custom-call | flops 838860800 | bytes 5406720 | tf_op jit(solution)/shard_map/pallas_call | solution.py:25
  54.6 0.5 collective-permute-start.19
  55.2 1.3 %collective-permute-start.20 = (bf16[2,160,640]{2,1,0:T(8,128)(2,1)S(1)}, bf16[2,160,640]{2,1,0:T(8,128)(2,1)S(1)}, u32[]{:S(2)}, u32[]{:S(2)}) collective-permute-start(bf16[2,160,640]{2,1,0:T(8,128)(2,1)S(1)} %get-tuple-element.25), channel_id=1, source_target_pairs={{0,16},{4,20},{8,24},{12,28},{16,0},{20,4},{24,8},{28,12},{1,17},{... | collective-permute-start | bytes 1228808 | tf_op jit(solution)/shard_map/ppermute | solution.py:242
  56.4 2.6 %shard_map.123 = (f32[256,640]{1,0:T(8,128)S(1)}, bf16[256,640]{1,0:T(8,128)(2,1)S(1)}) custom-call(bf16[320,512]{1,0:T(8,128)(2,1)S(1)} %shard_map.119.refs_0_, bf16[320,512]{1,0:T(8,128)(2,1)S(1)} %collective-permute-done.13.refs_1_, bf16[320,512]{1,0:T(8,128)(2,1)S(1)} %collective-permute-done.14.refs_2_, ...), custom_call_target="tpu_custom_call" | custom-call | flops 838860800 | bytes 8388608 | tf_op jit(solution)/shard_map/pallas_call | solution.py:326
  59.0 0.1 collective-permute-start.23
  59.1 0.0 collective-permute-done.7.refs_3_
  59.1 2.7 %collective-permute-done.10.refs_4_ = bf16[320,512]{1,0:T(8,128)(2,1)S(1)} collective-permute-done((bf16[320,512]{1,0:T(8,128)(2,1)S(1)}, bf16[320,512]{1,0:T(8,128)(2,1)S(1)}, u32[]{:S(2)}, u32[]{:S(2)}) %collective-permute-start.10) | collective-permute-done | bytes 327712 | tf_op jit(solution)/shard_map/ppermute | solution.py:248
  61.8 0.5 shard_map.117
  62.2 0.1 collective-permute-start.11
  62.3 1.8 %collective-permute-done.19.from_a = bf16[2,160,640]{2,1,0:T(8,128)(2,1)S(1)} collective-permute-done((bf16[2,160,640]{2,1,0:T(8,128)(2,1)S(1)}, bf16[2,160,640]{2,1,0:T(8,128)(2,1)S(1)}, u32[]{:S(2)}, u32[]{:S(2)}) %collective-permute-start.19) | collective-permute-done | bytes 409632 | tf_op jit(solution)/shard_map/ppermute | solution.py:242
  64.1 0.1 collective-permute-done.20.from_b
  64.2 0.1 shard_map.121
  64.3 1.5 %collective-permute-start.21 = (bf16[160,640]{1,0:T(8,128)(2,1)S(1)}, bf16[160,640]{1,0:T(8,128)(2,1)S(1)}, u32[]{:S(2)}, u32[]{:S(2)}) collective-permute-start(bf16[160,640]{1,0:T(8,128)(2,1)S(1)} %get-tuple-element.28), channel_id=1, source_target_pairs={{0,16},{4,20},{8,24},{12,28},{16,0},{20,4},{24,8},{28,12},{1,17},{... | collective-permute-start | bytes 614408 | tf_op jit(solution)/shard_map/ppermute | solution.py:242
  65.8 0.5 collective-permute-start.22
  66.3 0.0 collective-permute-done.23.other_ref
  66.3 3.7 %shard_map.124 = (bf16[256,640]{1,0:T(8,128)(2,1)}, bf16[256,640]{1,0:T(8,128)(2,1)}, bf16[256,640]{1,0:T(8,128)(2,1)}) custom-call(bf16[256,640]{1,0:T(8,128)(2,1)S(1)} %copy-done, bf16[256,640]{1,0:T(8,128)(2,1)S(1)} %copy-done.1, bf16[256,640]{1,0:T(8,128)(2,1)S(1)} %copy-done.2, s32[1,256]{1,0:T(1,128)S(1)} %copy-done.5, ...), custom_call_target="tpu_custom_call" | custom-call | flops 419430400 | bytes 2950144 | tf_op jit(solution)/shard_map/pallas_call | solution.py:25
  70.0 0.0 collective-permute-done.11.other_ref
  70.0 1.0 %shard_map.118 = bf16[256,640]{1,0:T(8,128)(2,1)} custom-call(bf16[256,640]{1,0:T(8,128)(2,1)S(1)} %copy-done.3, f32[320,256]{1,0:T(8,128)S(1)} %get-tuple-element.20.keep_ref, f32[320,256]{1,0:T(8,128)S(1)} %collective-permute-done.11.other_ref), custom_call_target="tpu_custom_call" | custom-call | bytes 1310720 | tf_op jit(solution)/shard_map/pallas_call | solution.py:25
  71.0 0.0 collective-permute-done.21.refs_2_
  71.0 0.6 collective-permute-done.22.refs_3_
  71.6 1.0 %shard_map.122 = f32[320,640]{1,0:T(8,128)} custom-call(f32[160,640]{1,0:T(8,128)S(1)} %get-tuple-element.26.refs_0_, f32[160,640]{1,0:T(8,128)S(1)} %get-tuple-element.27.refs_1_, bf16[160,640]{1,0:T(8,128)(2,1)S(1)} %collective-permute-done.21.refs_2_, bf16[160,640]{1,0:T(8,128)(2,1)S(1)} %collective-permute-done.22.refs_3_), custom_call_target="tpu_custom_call" | custom-call | bytes 2048000 | tf_op jit(solution)/shard_map/pallas_call | solution.py:25
  (16 shorter events, 0.2 us)
Async XLA Ops:
  0.6 11.2 %copy-start.4 = (bf16[256,640]{1,0:T(8,128)(2,1)S(1)}, bf16[256,640]{1,0:T(8,128)(2,1)}, u32[]{:S(2)}) copy-start(bf16[256,640]{1,0:T(8,128)(2,1)} %own_ref.1) | copy-start | bytes 983044
  0.6 12.8 %copy-start.5 = (s32[1,256]{1,0:T(1,128)S(1)}, s32[1,256]{1,0:T(1,128)}, u32[]{:S(2)}) copy-start(s32[1,256]{1,0:T(1,128)} %seg_ref.3) | copy-start | bytes 3076
  0.7 12.8 %copy-start.2 = (bf16[256,640]{1,0:T(8,128)(2,1)S(1)}, bf16[256,640]{1,0:T(8,128)(2,1)}, u32[]{:S(2)}) copy-start(bf16[256,640]{1,0:T(8,128)(2,1)} %v_ref.3) | copy-start | bytes 983044
  0.7 12.8 %copy-start.1 = (bf16[256,640]{1,0:T(8,128)(2,1)S(1)}, bf16[256,640]{1,0:T(8,128)(2,1)}, u32[]{:S(2)}) copy-start(bf16[256,640]{1,0:T(8,128)(2,1)} %k_ref.3) | copy-start | bytes 983044
  0.7 12.8 %copy-start = (bf16[256,640]{1,0:T(8,128)(2,1)S(1)}, bf16[256,640]{1,0:T(8,128)(2,1)}, u32[]{:S(2)}) copy-start(bf16[256,640]{1,0:T(8,128)(2,1)} %q_ref.3) | copy-start | bytes 983044
  1.9 8.1 %collective-permute-start.2 = (bf16[160,640]{1,0:T(8,128)(2,1)S(1)}, bf16[160,640]{1,0:T(8,128)(2,1)S(1)}, u32[]{:S(2)}, u32[]{:S(2)}) collective-permute-start(bf16[160,640]{1,0:T(8,128)(2,1)S(1)} %get-tuple-element.37), channel_id=1, source_target_pairs={{0,16},{4,20},{8,24},{12,28},{16,0},{20,4},{24,8},{28,12},{1,17},{... | collective-permute-start | bytes 614408 | tf_op jit(solution)/shard_map/ppermute | solution.py:242
  4.9 6.9 %collective-permute-start = (bf16[160,640]{1,0:T(8,128)(2,1)S(1)}, bf16[160,640]{1,0:T(8,128)(2,1)S(1)}, u32[]{:S(2)}, u32[]{:S(2)}) collective-permute-start(bf16[160,640]{1,0:T(8,128)(2,1)S(1)} %get-tuple-element.38), channel_id=1, source_target_pairs={{0,8},{4,12},{8,0},{12,4},{16,24},{20,28},{24,16},{28,20},{1,9},{5... | collective-permute-start | bytes 614408 | tf_op jit(solution)/shard_map/ppermute | solution.py:242
  10.0 11.1 %collective-permute-start.3 = (bf16[2,160,640]{2,1,0:T(8,128)(2,1)S(1)}, bf16[2,160,640]{2,1,0:T(8,128)(2,1)S(1)}, u32[]{:S(2)}, u32[]{:S(2)}) collective-permute-start(bf16[2,160,640]{2,1,0:T(8,128)(2,1)S(1)} %pad_maximum_fusion.1), channel_id=1, source_target_pairs={{0,8},{4,12},{8,0},{12,4},{16,24},{20,28},{24,16},{28,20},{1,9},{5... | collective-permute-start | bytes 1228808 | tf_op jit(solution)/shard_map/ppermute | solution.py:242
  11.8 3.2 %collective-permute-start.12 = (bf16[256,640]{1,0:T(8,128)(2,1)S(1)}, bf16[256,640]{1,0:T(8,128)(2,1)S(1)}, u32[]{:S(2)}, u32[]{:S(2)}) collective-permute-start(bf16[256,640]{1,0:T(8,128)(2,1)S(1)} %copy-done.4), channel_id=1, source_target_pairs={{0,4},{4,0},{8,12},{12,8},{16,20},{20,16},{24,28},{28,24},{1,5},{5... | collective-permute-start | bytes 983048 | tf_op jit(solution)/shard_map/ppermute | solution.py:242
  11.9 11.9 %collective-permute-start.1 = (bf16[2,160,640]{2,1,0:T(8,128)(2,1)S(1)}, bf16[2,160,640]{2,1,0:T(8,128)(2,1)S(1)}, u32[]{:S(2)}, u32[]{:S(2)}) collective-permute-start(bf16[2,160,640]{2,1,0:T(8,128)(2,1)S(1)} %pad_maximum_fusion), channel_id=1, source_target_pairs={{0,16},{4,20},{8,24},{12,28},{16,0},{20,4},{24,8},{28,12},{1,17},{... | collective-permute-start | bytes 1228808 | tf_op jit(solution)/shard_map/ppermute | solution.py:242
  14.7 9.2 %collective-permute-start.4 = (bf16[256,640]{1,0:T(8,128)(2,1)S(1)}, bf16[256,640]{1,0:T(8,128)(2,1)S(1)}, u32[]{:S(2)}, u32[]{:S(2)}) collective-permute-start(bf16[256,640]{1,0:T(8,128)(2,1)S(1)} %shard_map.110.refs_1_.refs_7_), channel_id=1, source_target_pairs={{0,4},{4,0},{8,12},{12,8},{16,20},{20,16},{24,28},{28,24},{1,5},{5... | collective-permute-start | bytes 983048 | tf_op jit(solution)/shard_map/ppermute | solution.py:242
  15.3 13.0 %collective-permute-start.16 = (bf16[320,512]{1,0:T(8,128)(2,1)S(1)}, bf16[320,512]{1,0:T(8,128)(2,1)S(1)}, u32[]{:S(2)}, u32[]{:S(2)}) collective-permute-start(bf16[320,512]{1,0:T(8,128)(2,1)S(1)} %shard_map.119.refs_0_), channel_id=1, source_target_pairs={{3,2},{2,1},{1,0},{7,6},{6,5},{5,4},{11,10},{10,9},{9,8},{15,14},{... | collective-permute-start | bytes 983048 | tf_op jit(solution)/shard_map/ppermute | solution.py:248
  16.6 13.0 %collective-permute-start.13 = (bf16[320,512]{1,0:T(8,128)(2,1)S(1)}, bf16[320,512]{1,0:T(8,128)(2,1)S(1)}, u32[]{:S(2)}, u32[]{:S(2)}) collective-permute-start(bf16[320,512]{1,0:T(8,128)(2,1)S(1)} %shard_map.119.refs_0_), channel_id=1, source_target_pairs={{0,1},{1,2},{2,3},{4,5},{5,6},{6,7},{8,9},{9,10},{10,11},{12,13},{... | collective-permute-start | bytes 983048 | tf_op jit(solution)/shard_map/ppermute | solution.py:245
  24.5 10.8 %collective-permute-start.5 = (bf16[320,512]{1,0:T(8,128)(2,1)S(1)}, bf16[320,512]{1,0:T(8,128)(2,1)S(1)}, u32[]{:S(2)}, u32[]{:S(2)}) collective-permute-start(bf16[320,512]{1,0:T(8,128)(2,1)S(1)} %shard_map.111), channel_id=1, source_target_pairs={{0,1},{4,5},{8,9},{12,13},{16,17},{20,21},{24,25},{28,29}} | collective-permute-start | bytes 983048 | tf_op jit(solution)/shard_map/ppermute | solution.py:245
  27.5 12.6 %collective-permute-start.8 = (bf16[320,512]{1,0:T(8,128)(2,1)S(1)}, bf16[320,512]{1,0:T(8,128)(2,1)S(1)}, u32[]{:S(2)}, u32[]{:S(2)}) collective-permute-start(bf16[320,512]{1,0:T(8,128)(2,1)S(1)} %shard_map.114), channel_id=1, source_target_pairs={{3,2},{7,6},{11,10},{15,14},{19,18},{23,22},{27,26},{31,30}} | collective-permute-start | bytes 983048 | tf_op jit(solution)/shard_map/ppermute | solution.py:248
  28.2 12.6 %collective-permute-start.17 = (bf16[320,512]{1,0:T(8,128)(2,1)S(1)}, bf16[320,512]{1,0:T(8,128)(2,1)S(1)}, u32[]{:S(2)}, u32[]{:S(2)}) collective-permute-start(bf16[320,512]{1,0:T(8,128)(2,1)S(1)} %collective-permute-done.16.refs_4_), channel_id=1, source_target_pairs={{2,1},{1,0},{6,5},{5,4},{10,9},{9,8},{14,13},{13,12},{18,17},{17,1... | collective-permute-start | bytes 983048 | tf_op jit(solution)/shard_map/ppermute | solution.py:248
  29.6 12.6 %collective-permute-start.14 = (bf16[320,512]{1,0:T(8,128)(2,1)S(1)}, bf16[320,512]{1,0:T(8,128)(2,1)S(1)}, u32[]{:S(2)}, u32[]{:S(2)}) collective-permute-start(bf16[320,512]{1,0:T(8,128)(2,1)S(1)} %collective-permute-done.13.refs_1_), channel_id=1, source_target_pairs={{1,2},{2,3},{5,6},{6,7},{9,10},{10,11},{13,14},{14,15},{17,18},{18... | collective-permute-start | bytes 983048 | tf_op jit(solution)/shard_map/ppermute | solution.py:245
  35.7 10.7 %collective-permute-start.6 = (bf16[320,512]{1,0:T(8,128)(2,1)S(1)}, bf16[320,512]{1,0:T(8,128)(2,1)S(1)}, u32[]{:S(2)}, u32[]{:S(2)}) collective-permute-start(bf16[320,512]{1,0:T(8,128)(2,1)S(1)} %shard_map.112), channel_id=1, source_target_pairs={{0,1},{1,2},{4,5},{5,6},{8,9},{9,10},{12,13},{13,14},{16,17},{17,1... | collective-permute-start | bytes 983048 | tf_op jit(solution)/shard_map/ppermute | solution.py:245
  40.2 11.2 %collective-permute-start.9 = (bf16[320,512]{1,0:T(8,128)(2,1)S(1)}, bf16[320,512]{1,0:T(8,128)(2,1)S(1)}, u32[]{:S(2)}, u32[]{:S(2)}) collective-permute-start(bf16[320,512]{1,0:T(8,128)(2,1)S(1)} %shard_map.115), channel_id=1, source_target_pairs={{3,2},{2,1},{7,6},{6,5},{11,10},{10,9},{15,14},{14,13},{19,18},{18... | collective-permute-start | bytes 983048 | tf_op jit(solution)/shard_map/ppermute | solution.py:248
  40.9 11.8 %collective-permute-start.18 = (bf16[320,512]{1,0:T(8,128)(2,1)S(1)}, bf16[320,512]{1,0:T(8,128)(2,1)S(1)}, u32[]{:S(2)}, u32[]{:S(2)}) collective-permute-start(bf16[320,512]{1,0:T(8,128)(2,1)S(1)} %collective-permute-done.17.refs_5_), channel_id=1, source_target_pairs={{1,0},{5,4},{9,8},{13,12},{17,16},{21,20},{25,24},{29,28}} | collective-permute-start | bytes 983048 | tf_op jit(solution)/shard_map/ppermute | solution.py:248
  42.2 10.5 %collective-permute-start.15 = (bf16[320,512]{1,0:T(8,128)(2,1)S(1)}, bf16[320,512]{1,0:T(8,128)(2,1)S(1)}, u32[]{:S(2)}, u32[]{:S(2)}) collective-permute-start(bf16[320,512]{1,0:T(8,128)(2,1)S(1)} %collective-permute-done.14.refs_2_), channel_id=1, source_target_pairs={{2,3},{6,7},{10,11},{14,15},{18,19},{22,23},{26,27},{30,31}} | collective-permute-start | bytes 983048 | tf_op jit(solution)/shard_map/ppermute | solution.py:245
  46.9 12.2 %collective-permute-start.7 = (bf16[320,512]{1,0:T(8,128)(2,1)S(1)}, bf16[320,512]{1,0:T(8,128)(2,1)S(1)}, u32[]{:S(2)}, u32[]{:S(2)}) collective-permute-start(bf16[320,512]{1,0:T(8,128)(2,1)S(1)} %shard_map.113), channel_id=1, source_target_pairs={{0,1},{1,2},{2,3},{4,5},{5,6},{6,7},{8,9},{9,10},{10,11},{12,13},{... | collective-permute-start | bytes 983048 | tf_op jit(solution)/shard_map/ppermute | solution.py:245
  51.4 10.4 %collective-permute-start.10 = (bf16[320,512]{1,0:T(8,128)(2,1)S(1)}, bf16[320,512]{1,0:T(8,128)(2,1)S(1)}, u32[]{:S(2)}, u32[]{:S(2)}) collective-permute-start(bf16[320,512]{1,0:T(8,128)(2,1)S(1)} %shard_map.116), channel_id=1, source_target_pairs={{3,2},{2,1},{1,0},{7,6},{6,5},{5,4},{11,10},{10,9},{9,8},{15,14},{... | collective-permute-start | bytes 983048 | tf_op jit(solution)/shard_map/ppermute | solution.py:248
  54.6 9.5 %collective-permute-start.19 = (bf16[2,160,640]{2,1,0:T(8,128)(2,1)S(1)}, bf16[2,160,640]{2,1,0:T(8,128)(2,1)S(1)}, u32[]{:S(2)}, u32[]{:S(2)}) collective-permute-start(bf16[2,160,640]{2,1,0:T(8,128)(2,1)S(1)} %get-tuple-element.24), channel_id=1, source_target_pairs={{0,8},{4,12},{8,0},{12,4},{16,24},{20,28},{24,16},{28,20},{1,9},{5... | collective-permute-start | bytes 1228808 | tf_op jit(solution)/shard_map/ppermute | solution.py:242
  55.2 9.0 %collective-permute-start.20 = (bf16[2,160,640]{2,1,0:T(8,128)(2,1)S(1)}, bf16[2,160,640]{2,1,0:T(8,128)(2,1)S(1)}, u32[]{:S(2)}, u32[]{:S(2)}) collective-permute-start(bf16[2,160,640]{2,1,0:T(8,128)(2,1)S(1)} %get-tuple-element.25), channel_id=1, source_target_pairs={{0,16},{4,20},{8,24},{12,28},{16,0},{20,4},{24,8},{28,12},{1,17},{... | collective-permute-start | bytes 1228808 | tf_op jit(solution)/shard_map/ppermute | solution.py:242
  59.0 7.3 %collective-permute-start.23 = (bf16[256,640]{1,0:T(8,128)(2,1)S(1)}, bf16[256,640]{1,0:T(8,128)(2,1)S(1)}, u32[]{:S(2)}, u32[]{:S(2)}) collective-permute-start(bf16[256,640]{1,0:T(8,128)(2,1)S(1)} %get-tuple-element.31), channel_id=1, source_target_pairs={{0,4},{4,0},{8,12},{12,8},{16,20},{20,16},{24,28},{28,24},{1,5},{5... | collective-permute-start | bytes 983048 | tf_op jit(solution)/shard_map/ppermute | solution.py:242
  62.2 7.8 %collective-permute-start.11 = (f32[320,256]{1,0:T(8,128)S(1)}, f32[320,256]{1,0:T(8,128)S(1)}, u32[]{:S(2)}, u32[]{:S(2)}) collective-permute-start(f32[320,256]{1,0:T(8,128)S(1)} %get-tuple-element.21), channel_id=1, source_target_pairs={{0,4},{4,0},{8,12},{12,8},{16,20},{20,16},{24,28},{28,24},{1,5},{5... | collective-permute-start | bytes 983048 | tf_op jit(solution)/shard_map/ppermute | solution.py:242
  64.2 5.8 %copy-start.3 = (bf16[256,640]{1,0:T(8,128)(2,1)S(1)}, bf16[256,640]{1,0:T(8,128)(2,1)}, u32[]{:S(2)}) copy-start(bf16[256,640]{1,0:T(8,128)(2,1)} %residual_ref.1) | copy-start | bytes 983044
  64.3 6.6 %collective-permute-start.21 = (bf16[160,640]{1,0:T(8,128)(2,1)S(1)}, bf16[160,640]{1,0:T(8,128)(2,1)S(1)}, u32[]{:S(2)}, u32[]{:S(2)}) collective-permute-start(bf16[160,640]{1,0:T(8,128)(2,1)S(1)} %get-tuple-element.28), channel_id=1, source_target_pairs={{0,16},{4,20},{8,24},{12,28},{16,0},{20,4},{24,8},{28,12},{1,17},{... | collective-permute-start | bytes 614408 | tf_op jit(solution)/shard_map/ppermute | solution.py:242
  65.8 5.8 %collective-permute-start.22 = (bf16[160,640]{1,0:T(8,128)(2,1)S(1)}, bf16[160,640]{1,0:T(8,128)(2,1)S(1)}, u32[]{:S(2)}, u32[]{:S(2)}) collective-permute-start(bf16[160,640]{1,0:T(8,128)(2,1)S(1)} %get-tuple-element.29), channel_id=1, source_target_pairs={{0,8},{4,12},{8,0},{12,4},{16,24},{20,28},{24,16},{28,20},{1,9},{5... | collective-permute-start | bytes 614408 | tf_op jit(solution)/shard_map/ppermute | solution.py:242

commit v2 on v1

v2 whole, which is shorter than its diff:
```python
import math

import jax
import jax.numpy as jnp
from jax import lax
from jax.experimental import pallas as pl
from jax.experimental.pallas import tpu as pltpu
from jax.sharding import PartitionSpec as P

HEAD = 128
MASKED = -1e30
F32 = jnp.float32
BF16 = jnp.bfloat16
NT = (((1,), (1,)), ((), ()))
NN = (((1,), (0,)), ((), ()))
TN = (((0,), (0,)), ((), ()))


def dot(a, b, dims):
    return lax.dot_general(a, b, dims, preferred_element_type=F32)


def call(kernel, outs, *args, flops=0):
    size = sum(math.prod(o.shape) * o.dtype.itemsize for o in (*outs, *args))
    return pl.pallas_call(
        kernel,
        out_shape=tuple(outs),
        in_specs=[pl.BlockSpec(memory_space=pltpu.VMEM)] * len(args),
        out_specs=tuple([pl.BlockSpec(memory_space=pltpu.VMEM)] * len(outs)),
        compiler_params=pltpu.CompilerParams(vmem_limit_bytes=40 * 1024 * 1024),
        cost_estimate=pl.CostEstimate(flops=flops, bytes_accessed=size, transcendentals=0),
    )(*args)


def shape(*dims, dtype=BF16):
    return jax.ShapeDtypeStruct(dims, dtype)


def visible_mask(seg_ref):
    count = seg_ref.shape[1]
    seg = jnp.broadcast_to(seg_ref[...].astype(F32), (count, count))
    rows = lax.broadcasted_iota(jnp.int32, (count, count), 0)
    cols = lax.broadcasted_iota(jnp.int32, (count, count), 1)
    return (cols <= rows) & (seg == seg.T)


def head_probs(q, k, allowed):
    scores = dot(q, k, NT) * (1.0 / math.sqrt(HEAD))
    scores = jnp.where(allowed, scores, MASKED)
    weights = jnp.exp(scores - jnp.max(scores, axis=-1, keepdims=True))
    return weights / jnp.sum(weights, axis=-1, keepdims=True)


def forward_kernel(q_ref, k_ref, v_ref, seg_ref, ctx_ref, probs_ref):
    allowed = visible_mask(seg_ref)
    for h in range(q_ref.shape[1] // HEAD):
        at = pl.ds(h * HEAD, HEAD)
        probs = head_probs(q_ref[:, at], k_ref[:, at], allowed)
        probs_ref[h] = probs
        ctx_ref[:, at] = dot(probs.astype(BF16), v_ref[:, at], NN).astype(BF16)


def backward_kernel(q_ref, k_ref, v_ref, probs_ref, mine_ref, other_ref, dq_ref, dk_ref, dv_ref):
    scale = 1.0 / math.sqrt(HEAD)
    for h in range(q_ref.shape[1] // HEAD):
        at = pl.ds(h * HEAD, HEAD)
        q, k, v = q_ref[:, at], k_ref[:, at], v_ref[:, at]
        probs = probs_ref[h]
        d_ctx = (mine_ref[:, at] + other_ref[:, at].astype(F32)).astype(BF16)
        d_probs = dot(d_ctx, v, NT)
        dv_ref[:, at] = dot(probs.astype(BF16), d_ctx, TN).astype(BF16)
        inner = jnp.sum(probs * d_probs, axis=-1, keepdims=True)
        d_scores = (probs * (d_probs - inner)).astype(BF16)
        dq_ref[:, at] = (dot(d_scores, k, NN) * scale).astype(BF16)
        dk_ref[:, at] = (dot(d_scores, q, TN) * scale).astype(BF16)


def plane_slot(plane, group):
    return plane ^ (lax.axis_index("blk") // group)


def unit_kernel(own_ref, other_ref, unit_ref):
    half, count = unit_ref.shape[0], own_ref.shape[0]
    core = lax.rem(lax.axis_index("blk"), 2)
    own, other = own_ref[...].T, other_ref[...].T
    for side in range(2):

        @pl.when(core == side)
        def _():
            rows = slice(side * half, (side + 1) * half)
            unit_ref[:, :count] = own[rows]
            unit_ref[:, count:] = other[rows]


def make_unit(own, other, strips):
    count, width = own.shape
    half = width // 2
    if strips == 1:
        return call(unit_kernel, (shape(half, 2 * count),), own, other)[0]
    core = lax.rem(lax.axis_index("blk"), 2)
    both = jnp.concatenate([own, other], axis=0).T.reshape(strips, 2, half // strips, 2 * count)
    return lax.dynamic_index_in_dim(both, core, 1, keepdims=False).reshape(half, 2 * count)


def is_inner(z):
    return (z == 1) | (z == 2)


def project_part(w_ref, ctx_ref, plane, group):
    return dot(w_ref[plane_slot(plane, group)], ctx_ref[...], NT)


def first_message_kernel(group, w_ref, own_ref, other_ref, passing_ref, out_ref):
    count = own_ref.shape[0]
    z = lax.axis_index("shard")

    @pl.when(is_inner(z))
    def _():
        out_ref[...] = passing_ref[...]

    @pl.when(~is_inner(z))
    def _():
        for i, ctx_ref in enumerate((own_ref, other_ref)):
            part = project_part(w_ref, ctx_ref, z ^ 3, group)
            out_ref[:, pl.ds(i * count, count)] = part.astype(BF16)


def message_kernel(flip, group, w_ref, own_ref, other_ref, past_ref, out_ref):
    count = own_ref.shape[0]
    z = lax.axis_index("shard")
    for i, ctx_ref in enumerate((own_ref, other_ref)):
        at = pl.ds(i * count, count)
        part = project_part(w_ref, ctx_ref, z ^ flip, group)
        past = jnp.where(is_inner(z), past_ref[:, at].astype(F32), 0.0)
        out_ref[:, at] = (part + past).astype(BF16)


def last_project_kernel(group, w_ref, own_ref, other_ref, pair_ref, mid_ref, keep_ref, send_ref):
    count = own_ref.shape[0]
    z = lax.axis_index("shard")
    for i, (ctx_ref, out_ref) in enumerate(((own_ref, keep_ref), (other_ref, send_ref))):
        at = pl.ds(i * count, count)
        part = project_part(w_ref, ctx_ref, z, group) + pair_ref[:, at].astype(F32)
        out_ref[...] = part + jnp.where(is_inner(z), mid_ref[:, at].astype(F32), 0.0)


def layer_out_kernel(residual_ref, keep_ref, other_ref, out_ref):
    half = keep_ref.shape[0]
    core = lax.rem(lax.axis_index("blk"), 2)
    keep, other = keep_ref[...], other_ref[...]
    for side, order in enumerate(((keep, other), (other, keep))):

        @pl.when(core == side)
        def _():
            total = jnp.concatenate(order, axis=0).T
            out_ref[...] = (residual_ref[...].astype(F32) + total).astype(BF16)


def make_layer_out(residual, keep, other, strips):
    count, width = residual.shape
    if strips == 1:
        return call(layer_out_kernel, (shape(count, width),), residual, keep, other)[0]
    core = lax.rem(lax.axis_index("blk"), 2)
    pair = jnp.stack([keep, other]).reshape(2, strips, -1, count)
    pair = jnp.where(core == 0, pair, pair[::-1])
    total = pair.transpose(1, 0, 2, 3).reshape(width, count)
    return (residual.astype(F32) + total.T).astype(BF16)


def early_planes(unit_ref, near_ref, outer_ref, inner_ref, body):
    z = lax.axis_index("shard")
    body(z, unit_ref)
    body(z ^ 1, near_ref)
    pl.when(is_inner(z))(lambda: body(z ^ 2, inner_ref))
    pl.when(~is_inner(z))(lambda: body(z ^ 2, outer_ref))


def late_plane(inner_ref, outer_ref, body):
    z = lax.axis_index("shard")
    pl.when(is_inner(z))(lambda: body(z ^ 3, inner_ref))
    pl.when(~is_inner(z))(lambda: body(z ^ 3, outer_ref))


def d_context_early_kernel(group, *refs):
    *unit_refs, w_ref, total_ref = refs
    total_ref[...] = jnp.zeros_like(total_ref)

    def body(plane, unit_ref):
        total_ref[...] += dot(unit_ref[...], w_ref[plane_slot(plane, group)], TN)

    early_planes(*unit_refs, body)


def d_context_late_kernel(group, *refs):
    inner_ref, outer_ref, w_ref, total_ref, mine_ref, send_ref = refs
    count = mine_ref.shape[0]

    def body(plane, unit_ref):
        part = dot(unit_ref[...], w_ref[plane_slot(plane, group)], TN)
        mine_ref[...] = total_ref[:count] + part[:count]
        send_ref[...] = (total_ref[count:] + part[count:]).astype(BF16)

    late_plane(inner_ref, outer_ref, body)


def weight_part(unit_ref, own_ref, other_ref):
    count = own_ref.shape[0]
    part = dot(unit_ref[:, :count], own_ref[...], NN)
    return part + dot(unit_ref[:, count:], other_ref[...], NN)


def late_slot(group):
    return plane_slot(lax.axis_index("shard") ^ 3, group)


def choose(condition, then, other):
    pl.when(condition)(then)
    pl.when(~condition)(other)


def weight_early_kernel(group, *refs):
    *unit_refs, own_ref, other_ref, send_a, send_b, keep_a, keep_b, rest_a, rest_b = refs
    rows = rest_a.shape[0]
    late = late_slot(group)

    def body(plane, unit_ref):
        slot = plane_slot(plane, group)
        part = weight_part(unit_ref, own_ref, other_ref)

        def place(block, bit, send, keep, rest):
            def into_rest():
                rest[...] = block

            def into_send():
                send[...] = block.astype(BF16)

            def into_keep():
                keep[...] = block

            def early():
                choose((slot & bit) == bit, into_send, into_keep)

            choose(slot == (late ^ bit), into_rest, early)

        place(part[:rows], 1, send_a, keep_a, rest_a)
        place(part[rows:], 2, send_b, keep_b, rest_b)

    early_planes(*unit_refs, body)


def weight_late_kernel(group, *refs):
    inner_ref, outer_ref, own_ref, other_ref, rest_a, rest_b, send_a, send_b, keep_a, keep_b = refs
    rows = rest_a.shape[0]
    late = late_slot(group)

    def body(plane, unit_ref):
        part = weight_part(unit_ref, own_ref, other_ref)

        def place(block, bit, send, keep, rest):
            sends = (late & bit) == bit
            send[...] = jnp.where(sends, block, rest[...]).astype(BF16)
            keep[...] = jnp.where(sends, rest[...], block)

        place(part[:rows], 1, send_a, keep_a, rest_a)
        place(part[rows:], 2, send_b, keep_b, rest_b)

    late_plane(inner_ref, outer_ref, body)


def half_sum_kernel(group, *refs):
    late = late_slot(group)
    send_a, send_b, left_a, left_b = refs[8:]
    for stream, send, left, keeps in ((0, send_a, left_a, 2), (1, send_b, left_b, 1)):
        early_keep, early_from, late_keep, late_from = refs[4 * stream : 4 * stream + 4]
        early_sum = early_keep[...] + early_from[...].astype(F32)
        late_sum = late_keep[...] + late_from[...].astype(F32)
        goes = (late & keeps) == keeps
        send[...] = jnp.where(goes, late_sum, early_sum).astype(BF16)
        left[...] = jnp.where(goes, early_sum, late_sum)


def grad_sum_kernel(scale, left_a, left_b, from_a, from_b, out_ref):
    rows = left_a.shape[0]
    out_ref[:rows] = (left_a[...] + from_a[...].astype(F32)) * scale
    out_ref[rows:] = (left_b[...] + from_b[...].astype(F32)) * scale


def solution(mesh):
    blk, planes = mesh.shape["blk"], mesh.shape["shard"]
    assert planes == 4
    chips = blk // 2
    strips = chips // planes
    group = 2 * strips

    def swap(value, bit):
        return lax.ppermute(value, "blk", [(i, i ^ bit) for i in range(blk)])

    def pair_swap(value):
        return lax.ppermute(value, "shard", [(0, 1), (1, 0), (2, 3), (3, 2)])

    def mid_swap(value):
        pairs = []
        for b in range(blk):
            pairs += [(b * planes + z, b * planes + (3 - z)) for z in (1, 2)]
            pairs += [(b * planes + z, (b ^ 1) * planes + z) for z in (0, 3)]
        return lax.ppermute(value, ("blk", "shard"), pairs)

    def bound(kernel, *static):
        return lambda *refs: kernel(*static, *refs)

    def per_device(queries, key_rows, values, segment_ids, residual, out_weight, cotangent):
        count, width = queries.shape
        half = width // 2
        cut = half // 2
        position = lax.axis_index("blk") // 2
        unit_flops = 4 * half * count * width
        message = shape(half, 2 * count)

        cot_other = swap(cotangent, 1)

        w_own = out_weight.T
        bit = 1
        while bit < strips:
            there = swap(w_own, 2 * bit)
            upper = (position // bit) % 2
            w_own = jnp.concatenate(
                [jnp.where(upper, there, w_own), jnp.where(upper, w_own, there)], axis=0
            )
            bit *= 2
        w_one, w_two = swap(w_own, group), swap(w_own, 2 * group)
        unit = make_unit(cotangent, cot_other, strips)
        near, inner_far = pair_swap(unit), mid_swap(unit)
        ctx, probs = call(
            forward_kernel,
            (shape(count, width), shape(width // HEAD, count, count, dtype=F32)),
            queries,
            key_rows,
            values,
            segment_ids,
            flops=4 * count * count * width,
        )
        ctx_other = swap(ctx, 1)
        near, inner_far, w_one, w_two, ctx = lax.optimization_barrier(
            (near, inner_far, w_one, w_two, ctx)
        )
        w_far = [swap(w_two[:cut], group), swap(w_one[cut:], 2 * group)]
        w_all = jnp.stack([w_own, w_one, w_two, jnp.concatenate(w_far, axis=0)])

        outer_next, inner_next = pair_swap(inner_far), mid_swap(near)
        outer_next, inner_next = lax.optimization_barrier((outer_next, inner_next))
        early = call(
            bound(d_context_early_kernel, group),
            (shape(2 * count, width, dtype=F32),),
            unit,
            near,
            outer_next,
            inner_next,
            w_all,
            flops=3 * unit_flops,
        )[0]

        sources = (w_all, ctx, ctx_other)
        out = call(
            bound(first_message_kernel, group), (message,), *sources, inner_next, flops=unit_flops
        )[0]
        block, rest = shape(cut, width), shape(cut, width, dtype=F32)
        early_send_a, early_send_b, early_keep_a, early_keep_b, rest_a, rest_b = call(
            bound(weight_early_kernel, group),
            (block, block, rest, rest, rest, rest),
            unit,
            near,
            outer_next,
            inner_next,
            ctx,
            ctx_other,
            flops=3 * unit_flops,
        )
        early_from_a, early_from_b = swap(early_send_a, group), swap(early_send_b, 2 * group)
        passed, early, rest_a = lax.optimization_barrier((pair_swap(out), early, rest_a))
        late_send_a, late_send_b, late_keep_a, late_keep_b = call(
            bound(weight_late_kernel, group),
            (block, block, rest, rest),
            inner_far,
            passed,
            ctx,
            ctx_other,
            rest_a,
            rest_b,
            flops=unit_flops,
        )
        late_from_a, late_from_b = swap(late_send_a, group), swap(late_send_b, 2 * group)
        out = call(
            bound(message_kernel, 2, group), (message,), *sources, passed, flops=unit_flops
        )[0]
        from_pair, from_mid = pair_swap(out), mid_swap(out)
        early, late_send_a = lax.optimization_barrier((early, late_send_a))
        mine, send = call(
            bound(d_context_late_kernel, group),
            (shape(count, width, dtype=F32), shape(count, width)),
            inner_far,
            passed,
            w_all,
            early,
            flops=unit_flops,
        )
        d_queries, d_keys, d_values = call(
            backward_kernel,
            (shape(count, width),) * 3,
            queries,
            key_rows,
            values,
            probs,
            mine,
            swap(send, 1),
            flops=10 * count * count * width,
        )
        to_pair = call(
            bound(message_kernel, 1, group), (message,), *sources, from_mid, flops=unit_flops
        )[0]
        to_mid = call(
            bound(message_kernel, 3, group), (message,), *sources, from_pair, flops=unit_flops
        )[0]
        send_a, send_b, left_a, left_b = call(
            bound(half_sum_kernel, group),
            (block, block, rest, rest),
            early_keep_a,
            early_from_a,
            late_keep_a,
            late_from_a,
            early_keep_b,
            early_from_b,
            late_keep_b,
            late_from_b,
        )
        from_a, from_b = swap(send_a, 2 * group), swap(send_b, group)
        total = call(
            bound(grad_sum_kernel, 1.0 / math.sqrt(count * blk)),
            (shape(half, width, dtype=F32),),
            left_a,
            left_b,
            from_a,
            from_b,
        )[0]
        bit = strips // 2
        while bit >= 1:
            lower, upper = jnp.split(total, 2, axis=0)
            right = (position // bit) % 2
            sent = jnp.where(right, lower, upper)
            total = jnp.where(right, upper, lower) + swap(sent, 2 * bit)
            bit //= 2

        from_pair, from_mid, d_queries, total = lax.optimization_barrier(
            (pair_swap(to_pair), mid_swap(to_mid), d_queries, total)
        )
        keep, send = call(
            bound(last_project_kernel, group),
            (shape(half, count, dtype=F32),) * 2,
            *sources,
            from_pair,
            from_mid,
            flops=unit_flops,
        )
        layer_out = make_layer_out(residual, keep, swap(send, 1), strips)

        return layer_out, total, d_queries, d_keys, d_values

    spread = P("blk", "shard")
    return jax.shard_map(
        per_device,
        mesh=mesh,
        in_specs=(spread, spread, spread, P("blk", None), spread, P("shard", "blk"), spread),
        out_specs=(spread,) * 5,
        check_vma=False,
    )
```

time: 73.2 us -> 61.4 us (0.84)
  starting transfers between devices: 36.4 us -> 21.2 us
  local copies, waits for them, and re-layouts: 1.25 us -> 4.63 us
  waiting for transfers between devices: 20 us -> 21.4 us
  Pallas kernels: 13.7 us -> 12.8 us
    ppermute x12 -> x9, starting transfers between devices: 24.3 us -> 9.77 us  [the longest x5 9.21 us: pair_swap(): return lax.ppermute(value, 'shard', [(0, 1), (1, 0), (2, 3), (3, 2)])]
    unnamed x12 -> x20, local copies, waits for them, and re-layouts: 0.02 us -> 4.59 us
    pallas_call x1 -> x0, Pallas kernels: 2.61 us -> none  [per_device(): pl.pallas_call(d_context, out_shape=(shape(count, width, dtype=F32), shap...]
    pallas_call x14 -> x15, Pallas kernels: 11 us -> 12.8 us  [call(): pl.pallas_call(kernel, out_shape=tuple(outs), in_specs=[pl.BlockSpec(memo...]
    another operation x1 -> x0, local copies, waits for them, and re-layouts: 1.19 us -> none  [per_device(): a_pair = jnp.stack([a_own, a_one])]
    ppermute x12 -> x14, waiting for transfers between devices: 8.7 us -> 9.62 us  [swap(): return lax.ppermute(value, 'blk', [(i, i ^ bit) for i in range(blk)])]
    ppermute x12 -> x14, starting transfers between devices: 12.1 us -> 11.4 us  [swap(): return lax.ppermute(value, 'blk', [(i, i ^ bit) for i in range(blk)])]
    ppermute x12 -> x9, waiting for transfers between devices: 11.3 us -> 11.7 us  [the longest x5 11.7 us: pair_swap(): return lax.ppermute(value, 'shard', [(0, 1), (1, 0), (2, 3), (3, 2)])]
  transfers between devices with their start and end apart: 24 -> 23, of which waited for: 8 -> 14; matrix products, arithmetic and copies ran while one was open for 0% -> 0% of each run, Pallas kernels for 17% -> 17%
where the time goes in v2:
time: 61.4 us; the launch traced here: 61.1 us
  waiting for transfers between devices  21.4 us (35%)
  starting transfers between devices  21.2 us (35%)
  Pallas kernels  12.8 us (21%)
  local copies, waits for them, and re-layouts  4.63 us (8%)
  between operations  0.85 us (1%)
    pallas_call x15, Pallas kernels, call(): pl.pallas_call(kernel, out_shape=tuple(outs), in_specs=[pl.BlockSpec(memo...  12.8 us
    ppermute x5, waiting for transfers between devices, pair_swap(): return lax.ppermute(value, 'shard', [(0, 1), (1, 0), (2, 3), (3, 2)])  11.7 us
    ppermute x14, starting transfers between devices, swap(): return lax.ppermute(value, 'blk', [(i, i ^ bit) for i in range(blk)])  11.4 us
    ppermute x14, waiting for transfers between devices, swap(): return lax.ppermute(value, 'blk', [(i, i ^ bit) for i in range(blk)])  9.62 us
    ppermute x5, starting transfers between devices, pair_swap(): return lax.ppermute(value, 'shard', [(0, 1), (1, 0), (2, 3), (3, 2)])  9.21 us
    unnamed x20, local copies, waits for them, and re-layouts  4.59 us
  transfers between devices with their start and end apart: 23, of which 14 were waited for; matrix products, arithmetic and copies ran while one was open for 0% of the time, Pallas kernels for 17%

profile of v2, /device:TPU:0, one launch (start us, length us, event | category | flops | bytes accessed | tf_op | source)
XLA Modules:
  0.0 61.1 jit_solution(3332978658208878002)
XLA Ops:
  0.6 0.5 collective-permute-start
  1.1 2.6 %collective-permute-start.3 = (bf16[320,640]{1,0:T(8,128)(2,1)}, bf16[320,640]{1,0:T(8,128)(2,1)S(1)}, u32[]{:S(2)}, u32[]{:S(2)}) collective-permute-start(bf16[320,640]{1,0:T(8,128)(2,1)} %bitcast.9), channel_id=1, source_target_pairs={{0,8},{4,12},{8,0},{12,4},{16,24},{20,28},{24,16},{28,20},{1,9},{5... | collective-permute-start | bytes 1228808 | tf_op jit(solution)/shard_map/ppermute | solution.py:296
  3.7 1.5 %collective-permute-start.4 = (bf16[320,640]{1,0:T(8,128)(2,1)}, bf16[320,640]{1,0:T(8,128)(2,1)S(1)}, u32[]{:S(2)}, u32[]{:S(2)}) collective-permute-start(bf16[320,640]{1,0:T(8,128)(2,1)} %bitcast.10), channel_id=1, source_target_pairs={{0,16},{4,20},{8,24},{12,28},{16,0},{20,4},{24,8},{28,12},{1,17},{... | collective-permute-start | bytes 1228808 | tf_op jit(solution)/shard_map/ppermute | solution.py:296
  5.2 0.0 collective-permute-done.other_ref
  5.2 1.0 %copy-done.7 = bf16[256,640]{1,0:T(8,128)(2,1)S(1)} copy-done((bf16[256,640]{1,0:T(8,128)(2,1)S(1)}, bf16[256,640]{1,0:T(8,128)(2,1)}, u32[]{:S(2)}) %copy-start.7) | copy-done | bytes 327704
  6.2 0.2 shard_map.110.refs_0_
  6.5 1.6 %collective-permute-start.1 = (bf16[320,512]{1,0:T(8,128)(2,1)S(1)}, bf16[320,512]{1,0:T(8,128)(2,1)S(1)}, u32[]{:S(2)}, u32[]{:S(2)}) collective-permute-start(bf16[320,512]{1,0:T(8,128)(2,1)S(1)} %shard_map.110.refs_0_), channel_id=1, source_target_pairs={{0,1},{1,0},{2,3},{3,2},{4,5},{5,4},{6,7},{7,6},{8,9},{9,8},{10,11... | collective-permute-start | bytes 983048 | tf_op jit(solution)/shard_map/ppermute | solution.py:299
  8.1 0.0 collective-permute-start.2
  8.1 1.0 %copy-done = bf16[256,640]{1,0:T(8,128)(2,1)S(1)} copy-done((bf16[256,640]{1,0:T(8,128)(2,1)S(1)}, bf16[256,640]{1,0:T(8,128)(2,1)}, u32[]{:S(2)}) %copy-start) | copy-done | bytes 327704
  9.1 1.0 %copy-done.2 = bf16[256,640]{1,0:T(8,128)(2,1)S(1)} copy-done((bf16[256,640]{1,0:T(8,128)(2,1)S(1)}, bf16[256,640]{1,0:T(8,128)(2,1)}, u32[]{:S(2)}) %copy-start.2) | copy-done | bytes 327704
  10.1 1.0 %copy-done.4 = bf16[256,640]{1,0:T(8,128)(2,1)S(1)} copy-done((bf16[256,640]{1,0:T(8,128)(2,1)S(1)}, bf16[256,640]{1,0:T(8,128)(2,1)}, u32[]{:S(2)}) %copy-start.4) | copy-done | bytes 327704
  11.0 0.7 %copy-done.8 = s32[1,256]{1,0:T(1,128)S(1)} copy-done((s32[1,256]{1,0:T(1,128)S(1)}, s32[1,256]{1,0:T(1,128)}, u32[]{:S(2)}) %copy-start.8) | copy-done | bytes 1048
  11.7 1.3 %shard_map.111 = (bf16[256,640]{1,0:T(8,128)(2,1)S(1)}, f32[5,256,256]{2,1,0:T(8,128)S(1)}) custom-call(bf16[256,640]{1,0:T(8,128)(2,1)S(1)} %copy-done, bf16[256,640]{1,0:T(8,128)(2,1)S(1)} %copy-done.2, bf16[256,640]{1,0:T(8,128)(2,1)S(1)} %copy-done.4, s32[1,256]{1,0:T(1,128)S(1)} %copy-done.8), custom_call_target="tpu_custom_call" | custom-call | flops 167772160 | bytes 2622464 | tf_op jit(solution)/shard_map/pallas_call | solution.py:25
  13.0 1.0 %collective-permute-done.3 = bf16[320,640]{1,0:T(8,128)(2,1)S(1)} collective-permute-done((bf16[320,640]{1,0:T(8,128)(2,1)}, bf16[320,640]{1,0:T(8,128)(2,1)S(1)}, u32[]{:S(2)}, u32[]{:S(2)}) %collective-permute-start.3) | collective-permute-done | bytes 409632 | tf_op jit(solution)/shard_map/ppermute | solution.py:296
  14.0 1.5 %collective-permute-done.4 = bf16[320,640]{1,0:T(8,128)(2,1)S(1)} collective-permute-done((bf16[320,640]{1,0:T(8,128)(2,1)}, bf16[320,640]{1,0:T(8,128)(2,1)S(1)}, u32[]{:S(2)}, u32[]{:S(2)}) %collective-permute-start.4) | collective-permute-done | bytes 409632 | tf_op jit(solution)/shard_map/ppermute | solution.py:296
  15.5 0.6 collective-permute-done.1.refs_1_
  16.1 0.6 collective-permute-start.5
  16.7 1.5 %collective-permute-start.6 = (bf16[160,640]{1,0:T(8,128)(2,1)S(1)}, bf16[160,640]{1,0:T(8,128)(2,1)S(1)}, u32[]{:S(2)}, u32[]{:S(2)}) collective-permute-start(bf16[160,640]{1,0:T(8,128)(2,1)S(1)} %slice.7), channel_id=1, source_target_pairs={{0,16},{4,20},{8,24},{12,28},{16,0},{20,4},{24,8},{28,12},{1,17},{... | collective-permute-start | bytes 614408 | tf_op jit(solution)/shard_map/ppermute | solution.py:296
  18.2 2.7 %collective-permute-start.8 = (bf16[320,512]{1,0:T(8,128)(2,1)S(1)}, bf16[320,512]{1,0:T(8,128)(2,1)S(1)}, u32[]{:S(2)}, u32[]{:S(2)}) collective-permute-start(bf16[320,512]{1,0:T(8,128)(2,1)S(1)} %collective-permute-done.2.refs_0_), channel_id=1, source_target_pairs={{0,1},{1,0},{2,3},{3,2},{4,5},{5,4},{6,7},{7,6},{8,9},{9,8},{10,11... | collective-permute-start | bytes 983048 | tf_op jit(solution)/shard_map/ppermute | solution.py:299
  20.9 0.0 collective-permute-start.9
  20.9 0.5 collective-permute-start.7
  21.4 0.7 %collective-permute-done.5 = bf16[160,640]{1,0:T(8,128)(2,1)S(1)} collective-permute-done((bf16[160,640]{1,0:T(8,128)(2,1)S(1)}, bf16[160,640]{1,0:T(8,128)(2,1)S(1)}, u32[]{:S(2)}, u32[]{:S(2)}) %collective-permute-start.5) | collective-permute-done | bytes 204832 | tf_op jit(solution)/shard_map/ppermute | solution.py:296
  22.1 0.4 collective-permute-done.6
  22.6 0.2 pad_maximum_fusion.refs_0_.refs_4_.refs_2_
  22.8 4.7 %collective-permute-done.8.refs_2_ = bf16[320,512]{1,0:T(8,128)(2,1)S(1)} collective-permute-done((bf16[320,512]{1,0:T(8,128)(2,1)S(1)}, bf16[320,512]{1,0:T(8,128)(2,1)S(1)}, u32[]{:S(2)}, u32[]{:S(2)}) %collective-permute-start.8) | collective-permute-done | bytes 327712 | tf_op jit(solution)/shard_map/ppermute | solution.py:299
  27.5 0.0 collective-permute-done.9.refs_3_
  27.5 0.0 collective-permute-done.7.refs_2_.refs_5_.refs_3_
  27.5 0.4 shard_map.112
  28.0 1.4 %collective-permute-start.10 = (bf16[320,512]{1,0:T(8,128)(2,1)S(1)}, bf16[320,512]{1,0:T(8,128)(2,1)S(1)}, u32[]{:S(2)}, u32[]{:S(2)}) collective-permute-start(bf16[320,512]{1,0:T(8,128)(2,1)S(1)} %shard_map.112), channel_id=1, source_target_pairs={{0,1},{1,0},{2,3},{3,2},{4,5},{5,4},{6,7},{7,6},{8,9},{9,8},{10,11... | collective-permute-start | bytes 983048 | tf_op jit(solution)/shard_map/ppermute | solution.py:299
  29.4 1.5 %shard_map.113.refs_3_ = f32[512,640]{1,0:T(8,128)S(1)} custom-call(bf16[320,512]{1,0:T(8,128)(2,1)S(1)} %shard_map.110.refs_0_, bf16[320,512]{1,0:T(8,128)(2,1)S(1)} %collective-permute-done.1.refs_1_, bf16[320,512]{1,0:T(8,128)(2,1)S(1)} %collective-permute-done.8.refs_2_, bf16[320,512]{1,0:T(8,128)(2,1)S(1)} %collective-permute-done.9.refs_3_, ...), custom_call_target="tpu_custom_call" | custom-call | flops 629145600 | bytes 4259840 | tf_op jit(solution)/shard_map/pallas_call | solution.py:25
  30.9 1.6 %shard_map.114 = (bf16[160,640]{1,0:T(8,128)(2,1)S(1)}, bf16[160,640]{1,0:T(8,128)(2,1)S(1)}, f32[160,640]{1,0:T(8,128)S(1)}, f32[160,640]{1,0:T(8,128)S(1)}, f3...) custom-call(bf16[320,512]{1,0:T(8,128)(2,1)S(1)} %shard_map.110.refs_0_, ...), custom_call_target="tpu_custom_call" | custom-call | flops 629145600 | bytes 4014080 | tf_op jit(solution)/shard_map/pallas_call | solution.py:25
  32.5 3.3 %collective-permute-done.10.refs_3_.refs_1_ = bf16[320,512]{1,0:T(8,128)(2,1)S(1)} collective-permute-done((bf16[320,512]{1,0:T(8,128)(2,1)S(1)}, bf16[320,512]{1,0:T(8,128)(2,1)S(1)}, u32[]{:S(2)}, u32[]{:S(2)}) %collective-permute-start.10) | collective-permute-done | bytes 327712 | tf_op jit(solution)/shard_map/ppermute | solution.py:299
  35.8 0.4 shard_map.115
  36.3 1.1 %collective-permute-start.13 = (bf16[320,512]{1,0:T(8,128)(2,1)S(1)}, bf16[320,512]{1,0:T(8,128)(2,1)S(1)}, u32[]{:S(2)}, u32[]{:S(2)}) collective-permute-start(bf16[320,512]{1,0:T(8,128)(2,1)S(1)} %shard_map.115), channel_id=1, source_target_pairs={{0,1},{1,0},{2,3},{3,2},{4,5},{5,4},{6,7},{7,6},{8,9},{9,8},{10,11... | collective-permute-start | bytes 983048 | tf_op jit(solution)/shard_map/ppermute | solution.py:299
  37.4 1.0 %collective-permute-start.16 = (bf16[160,640]{1,0:T(8,128)(2,1)S(1)}, bf16[160,640]{1,0:T(8,128)(2,1)S(1)}, u32[]{:S(2)}, u32[]{:S(2)}) collective-permute-start(bf16[160,640]{1,0:T(8,128)(2,1)S(1)} %get-tuple-element.63), channel_id=1, source_target_pairs={{0,8},{4,12},{8,0},{12,4},{16,24},{20,28},{24,16},{28,20},{1,9},{5... | collective-permute-start | bytes 614408 | tf_op jit(solution)/shard_map/ppermute | solution.py:296
  38.4 0.6 %collective-permute-start.18 = (bf16[160,640]{1,0:T(8,128)(2,1)S(1)}, bf16[160,640]{1,0:T(8,128)(2,1)S(1)}, u32[]{:S(2)}, u32[]{:S(2)}) collective-permute-start(bf16[160,640]{1,0:T(8,128)(2,1)S(1)} %get-tuple-element.66), channel_id=1, source_target_pairs={{0,16},{4,20},{8,24},{12,28},{16,0},{20,4},{24,8},{28,12},{1,17},{... | collective-permute-start | bytes 614408 | tf_op jit(solution)/shard_map/ppermute | solution.py:296
  39.0 0.4 shard_map.118
  39.4 0.8 %collective-permute-start.17 = (bf16[160,640]{1,0:T(8,128)(2,1)S(1)}, bf16[160,640]{1,0:T(8,128)(2,1)S(1)}, u32[]{:S(2)}, u32[]{:S(2)}) collective-permute-start(bf16[160,640]{1,0:T(8,128)(2,1)S(1)} %get-tuple-element.57), channel_id=1, source_target_pairs={{0,8},{4,12},{8,0},{12,4},{16,24},{20,28},{24,16},{28,20},{1,9},{5... | collective-permute-start | bytes 614408 | tf_op jit(solution)/shard_map/ppermute | solution.py:296
  40.2 3.2 %collective-permute-done.13.refs_3_ = bf16[320,512]{1,0:T(8,128)(2,1)S(1)} collective-permute-done((bf16[320,512]{1,0:T(8,128)(2,1)S(1)}, bf16[320,512]{1,0:T(8,128)(2,1)S(1)}, u32[]{:S(2)}, u32[]{:S(2)}) %collective-permute-start.13) | collective-permute-done | bytes 327712 | tf_op jit(solution)/shard_map/ppermute | solution.py:299
  43.4 0.2 collective-permute-start.19
  43.6 0.8 %shard_map.119 = (f32[256,640]{1,0:T(8,128)S(1)}, bf16[256,640]{1,0:T(8,128)(2,1)S(1)}) custom-call(bf16[320,512]{1,0:T(8,128)(2,1)S(1)} %collective-permute-done.2.refs_0_, bf16[320,512]{1,0:T(8,128)(2,1)S(1)} %collective-permute-done.10.refs_3_.refs_1_, bf16[4,320,640]{2,1,0:T(8,128)(2,1)S(1)} %pad_maximum_fusion.refs_0_.refs_4_.refs_2_, ...), custom_call_target="tpu_custom_call" | custom-call | flops 209715200 | bytes 4587520 | tf_op jit(solution)/shard_map/pallas_call | solution.py:25
  44.3 0.1 collective-permute-start.15
  44.4 0.5 shard_map.117
  44.9 0.5 shard_map.116
  45.3 0.0 copy-start.1
  45.4 0.0 copy-start.3
  45.4 0.0 copy-start.5
  45.4 0.0 collective-permute-done.16.refs_1_
  45.4 0.6 collective-permute-start.14
  45.9 0.4 collective-permute-done.18.refs_5_
  46.3 2.4 %collective-permute-start.12 = (bf16[320,512]{1,0:T(8,128)(2,1)S(1)}, bf16[320,512]{1,0:T(8,128)(2,1)S(1)}, u32[]{:S(2)}, u32[]{:S(2)}) collective-permute-start(bf16[320,512]{1,0:T(8,128)(2,1)S(1)} %shard_map.116), channel_id=1, source_target_pairs={{0,1},{1,0},{2,3},{3,2},{4,5},{5,4},{6,7},{7,6},{8,9},{9,8},{10,11... | collective-permute-start | bytes 983048 | tf_op jit(solution)/shard_map/ppermute | solution.py:299
  48.7 0.6 collective-permute-done.17.refs_3_
  49.2 0.7 %collective-permute-done.19.refs_7_ = bf16[160,640]{1,0:T(8,128)(2,1)S(1)} collective-permute-done((bf16[160,640]{1,0:T(8,128)(2,1)S(1)}, bf16[160,640]{1,0:T(8,128)(2,1)S(1)}, u32[]{:S(2)}, u32[]{:S(2)}) %collective-permute-start.19) | collective-permute-done | bytes 204832 | tf_op jit(solution)/shard_map/ppermute | solution.py:296
  50.0 0.2 shard_map.121
  50.2 0.7 %collective-permute-start.20 = (bf16[160,640]{1,0:T(8,128)(2,1)S(1)}, bf16[160,640]{1,0:T(8,128)(2,1)S(1)}, u32[]{:S(2)}, u32[]{:S(2)}) collective-permute-start(bf16[160,640]{1,0:T(8,128)(2,1)S(1)} %get-tuple-element.71), channel_id=1, source_target_pairs={{0,16},{4,20},{8,24},{12,28},{16,0},{20,4},{24,8},{28,12},{1,17},{... | collective-permute-start | bytes 614408 | tf_op jit(solution)/shard_map/ppermute | solution.py:296
  50.9 0.7 %collective-permute-start.21 = (bf16[160,640]{1,0:T(8,128)(2,1)S(1)}, bf16[160,640]{1,0:T(8,128)(2,1)S(1)}, u32[]{:S(2)}, u32[]{:S(2)}) collective-permute-start(bf16[160,640]{1,0:T(8,128)(2,1)S(1)} %get-tuple-element.72), channel_id=1, source_target_pairs={{0,8},{4,12},{8,0},{12,4},{16,24},{20,28},{24,16},{28,20},{1,9},{5... | collective-permute-start | bytes 614408 | tf_op jit(solution)/shard_map/ppermute | solution.py:296
  51.7 2.5 %shard_map.120 = (bf16[256,640]{1,0:T(8,128)(2,1)}, bf16[256,640]{1,0:T(8,128)(2,1)}, bf16[256,640]{1,0:T(8,128)(2,1)}) custom-call(bf16[256,640]{1,0:T(8,128)(2,1)S(1)} %copy-done.1, bf16[256,640]{1,0:T(8,128)(2,1)S(1)} %copy-done.3, bf16[256,640]{1,0:T(8,128)(2,1)S(1)} %copy-done.5, f32[5,256,256]{2,1,0:T(8,128)S(1)} %get-tuple-element.53.probs_ref, ...), custom_call_target="tpu_custom_call" | custom-call | flops 419430400 | bytes 4259840 | tf_op jit(solution)/shard_map/pallas_call | solution.py:25
  54.2 2.1 %collective-permute-done.20.refs_2_ = bf16[160,640]{1,0:T(8,128)(2,1)S(1)} collective-permute-done((bf16[160,640]{1,0:T(8,128)(2,1)S(1)}, bf16[160,640]{1,0:T(8,128)(2,1)S(1)}, u32[]{:S(2)}, u32[]{:S(2)}) %collective-permute-start.20) | collective-permute-done | bytes 204832 | tf_op jit(solution)/shard_map/ppermute | solution.py:296
  56.3 0.7 %collective-permute-done.21.refs_3_ = bf16[160,640]{1,0:T(8,128)(2,1)S(1)} collective-permute-done((bf16[160,640]{1,0:T(8,128)(2,1)S(1)}, bf16[160,640]{1,0:T(8,128)(2,1)S(1)}, u32[]{:S(2)}, u32[]{:S(2)}) %collective-permute-start.21) | collective-permute-done | bytes 204832 | tf_op jit(solution)/shard_map/ppermute | solution.py:296
  57.0 1.0 %shard_map.122 = f32[320,640]{1,0:T(8,128)} custom-call(f32[160,640]{1,0:T(8,128)S(1)} %get-tuple-element.69.refs_0_, f32[160,640]{1,0:T(8,128)S(1)} %get-tuple-element.70.refs_1_, bf16[160,640]{1,0:T(8,128)(2,1)S(1)} %collective-permute-done.20.refs_2_, bf16[160,640]{1,0:T(8,128)(2,1)S(1)} %collective-permute-done.21.refs_3_), custom_call_target="tpu_custom_call" | custom-call | bytes 2048000 | tf_op jit(solution)/shard_map/pallas_call | solution.py:25
  58.0 0.5 shard_map.123
  58.4 0.1 collective-permute-start.22
  58.5 1.6 %collective-permute-done.22.other_ref = f32[320,256]{1,0:T(8,128)S(1)} collective-permute-done((f32[320,256]{1,0:T(8,128)S(1)}, f32[320,256]{1,0:T(8,128)S(1)}, u32[]{:S(2)}, u32[]{:S(2)}) %collective-permute-start.22) | collective-permute-done | bytes 327712 | tf_op jit(solution)/shard_map/ppermute | solution.py:296
  60.1 1.0 %shard_map.124 = bf16[256,640]{1,0:T(8,128)(2,1)} custom-call(bf16[256,640]{1,0:T(8,128)(2,1)S(1)} %copy-done.6, f32[320,256]{1,0:T(8,128)S(1)} %get-tuple-element.75.keep_ref, f32[320,256]{1,0:T(8,128)S(1)} %collective-permute-done.22.other_ref), custom_call_target="tpu_custom_call" | custom-call | bytes 1310720 | tf_op jit(solution)/shard_map/pallas_call | solution.py:25
  (21 shorter events, 0.1 us)
Async XLA Ops:
  0.6 4.6 %collective-permute-start = (bf16[256,640]{1,0:T(8,128)(2,1)}, bf16[256,640]{1,0:T(8,128)(2,1)S(1)}, u32[]{:S(2)}, u32[]{:S(2)}) collective-permute-start(bf16[256,640]{1,0:T(8,128)(2,1)} %own_ref.1), channel_id=1, source_target_pairs={{0,4},{4,0},{8,12},{12,8},{16,20},{20,16},{24,28},{28,24},{1,5},{5... | collective-permute-start | bytes 983048 | tf_op jit(solution)/shard_map/ppermute | solution.py:296
  1.1 12.8 %collective-permute-start.3 = (bf16[320,640]{1,0:T(8,128)(2,1)}, bf16[320,640]{1,0:T(8,128)(2,1)S(1)}, u32[]{:S(2)}, u32[]{:S(2)}) collective-permute-start(bf16[320,640]{1,0:T(8,128)(2,1)} %bitcast.9), channel_id=1, source_target_pairs={{0,8},{4,12},{8,0},{12,4},{16,24},{20,28},{24,16},{28,20},{1,9},{5... | collective-permute-start | bytes 1228808 | tf_op jit(solution)/shard_map/ppermute | solution.py:296
  3.7 11.7 %collective-permute-start.4 = (bf16[320,640]{1,0:T(8,128)(2,1)}, bf16[320,640]{1,0:T(8,128)(2,1)S(1)}, u32[]{:S(2)}, u32[]{:S(2)}) collective-permute-start(bf16[320,640]{1,0:T(8,128)(2,1)} %bitcast.10), channel_id=1, source_target_pairs={{0,16},{4,20},{8,24},{12,28},{16,0},{20,4},{24,8},{28,12},{1,17},{... | collective-permute-start | bytes 1228808 | tf_op jit(solution)/shard_map/ppermute | solution.py:296
  5.2 1.0 %copy-start.7 = (bf16[256,640]{1,0:T(8,128)(2,1)S(1)}, bf16[256,640]{1,0:T(8,128)(2,1)}, u32[]{:S(2)}) copy-start(bf16[256,640]{1,0:T(8,128)(2,1)} %own_ref.1) | copy-start | bytes 983044
  6.2 16.3 %copy-start.9 = (bf16[640,320]{0,1:T(8,128)(2,1)S(1)}, bf16[640,320]{0,1:T(8,128)(2,1)}, u32[]{:S(2)}) copy-start(bf16[640,320]{0,1:T(8,128)(2,1)} %param.12) | copy-start | bytes 1228804
  6.5 9.6 %collective-permute-start.1 = (bf16[320,512]{1,0:T(8,128)(2,1)S(1)}, bf16[320,512]{1,0:T(8,128)(2,1)S(1)}, u32[]{:S(2)}, u32[]{:S(2)}) collective-permute-start(bf16[320,512]{1,0:T(8,128)(2,1)S(1)} %shard_map.110.refs_0_), channel_id=1, source_target_pairs={{0,1},{1,0},{2,3},{3,2},{4,5},{5,4},{6,7},{7,6},{8,9},{9,8},{10,11... | collective-permute-start | bytes 983048 | tf_op jit(solution)/shard_map/ppermute | solution.py:299
  8.1 7.9 %collective-permute-start.2 = (bf16[320,512]{1,0:T(8,128)(2,1)S(1)}, bf16[320,512]{1,0:T(8,128)(2,1)S(1)}, u32[]{:S(2)}, u32[]{:S(2)}) collective-permute-start(bf16[320,512]{1,0:T(8,128)(2,1)S(1)} %shard_map.110.refs_0_), channel_id=1, source_target_pairs={{1,2},{2,1},{0,4},{3,7},{5,6},{6,5},{4,0},{7,3},{9,10},{10,9},{8,1... | collective-permute-start | bytes 983048 | tf_op jit(solution)/shard_map/ppermute | solution.py:306
  8.1 1.0 %copy-start = (bf16[256,640]{1,0:T(8,128)(2,1)S(1)}, bf16[256,640]{1,0:T(8,128)(2,1)}, u32[]{:S(2)}) copy-start(bf16[256,640]{1,0:T(8,128)(2,1)} %q_ref.3) | copy-start | bytes 983044
  9.1 1.0 %copy-start.2 = (bf16[256,640]{1,0:T(8,128)(2,1)S(1)}, bf16[256,640]{1,0:T(8,128)(2,1)}, u32[]{:S(2)}) copy-start(bf16[256,640]{1,0:T(8,128)(2,1)} %k_ref.3) | copy-start | bytes 983044
  10.1 1.0 %copy-start.4 = (bf16[256,640]{1,0:T(8,128)(2,1)S(1)}, bf16[256,640]{1,0:T(8,128)(2,1)}, u32[]{:S(2)}) copy-start(bf16[256,640]{1,0:T(8,128)(2,1)} %v_ref.3) | copy-start | bytes 983044
  11.0 0.7 %copy-start.8 = (s32[1,256]{1,0:T(1,128)S(1)}, s32[1,256]{1,0:T(1,128)}, u32[]{:S(2)}) copy-start(s32[1,256]{1,0:T(1,128)} %seg_ref.1) | copy-start | bytes 3076
  16.1 6.1 %collective-permute-start.5 = (bf16[160,640]{1,0:T(8,128)(2,1)S(1)}, bf16[160,640]{1,0:T(8,128)(2,1)S(1)}, u32[]{:S(2)}, u32[]{:S(2)}) collective-permute-start(bf16[160,640]{1,0:T(8,128)(2,1)S(1)} %slice.6), channel_id=1, source_target_pairs={{0,8},{4,12},{8,0},{12,4},{16,24},{20,28},{24,16},{28,20},{1,9},{5... | collective-permute-start | bytes 614408 | tf_op jit(solution)/shard_map/ppermute | solution.py:296
  16.7 5.8 %collective-permute-start.6 = (bf16[160,640]{1,0:T(8,128)(2,1)S(1)}, bf16[160,640]{1,0:T(8,128)(2,1)S(1)}, u32[]{:S(2)}, u32[]{:S(2)}) collective-permute-start(bf16[160,640]{1,0:T(8,128)(2,1)S(1)} %slice.7), channel_id=1, source_target_pairs={{0,16},{4,20},{8,24},{12,28},{16,0},{20,4},{24,8},{28,12},{1,17},{... | collective-permute-start | bytes 614408 | tf_op jit(solution)/shard_map/ppermute | solution.py:296
  18.2 9.3 %collective-permute-start.8 = (bf16[320,512]{1,0:T(8,128)(2,1)S(1)}, bf16[320,512]{1,0:T(8,128)(2,1)S(1)}, u32[]{:S(2)}, u32[]{:S(2)}) collective-permute-start(bf16[320,512]{1,0:T(8,128)(2,1)S(1)} %collective-permute-done.2.refs_0_), channel_id=1, source_target_pairs={{0,1},{1,0},{2,3},{3,2},{4,5},{5,4},{6,7},{7,6},{8,9},{9,8},{10,11... | collective-permute-start | bytes 983048 | tf_op jit(solution)/shard_map/ppermute | solution.py:299
  20.9 6.6 %collective-permute-start.9 = (bf16[320,512]{1,0:T(8,128)(2,1)S(1)}, bf16[320,512]{1,0:T(8,128)(2,1)S(1)}, u32[]{:S(2)}, u32[]{:S(2)}) collective-permute-start(bf16[320,512]{1,0:T(8,128)(2,1)S(1)} %collective-permute-done.1.refs_1_), channel_id=1, source_target_pairs={{1,2},{2,1},{0,4},{3,7},{5,6},{6,5},{4,0},{7,3},{9,10},{10,9},{8,1... | collective-permute-start | bytes 983048 | tf_op jit(solution)/shard_map/ppermute | solution.py:306
  20.9 6.6 %collective-permute-start.7 = (bf16[256,640]{1,0:T(8,128)(2,1)S(1)}, bf16[256,640]{1,0:T(8,128)(2,1)S(1)}, u32[]{:S(2)}, u32[]{:S(2)}) collective-permute-start(bf16[256,640]{1,0:T(8,128)(2,1)S(1)} %get-tuple-element.46.refs_1_.refs_4_.refs_2_), channel_id=1, source_target_pairs={{0,4},{4,0},{8,12},{12,8},{16,20},{20,16},{24,28},{28,24},{1,5},{5... | collective-permute-start | bytes 983048 | tf_op jit(solution)/shard_map/ppermute | solution.py:296
  28.0 7.8 %collective-permute-start.10 = (bf16[320,512]{1,0:T(8,128)(2,1)S(1)}, bf16[320,512]{1,0:T(8,128)(2,1)S(1)}, u32[]{:S(2)}, u32[]{:S(2)}) collective-permute-start(bf16[320,512]{1,0:T(8,128)(2,1)S(1)} %shard_map.112), channel_id=1, source_target_pairs={{0,1},{1,0},{2,3},{3,2},{4,5},{5,4},{6,7},{7,6},{8,9},{9,8},{10,11... | collective-permute-start | bytes 983048 | tf_op jit(solution)/shard_map/ppermute | solution.py:299
  36.3 7.1 %collective-permute-start.13 = (bf16[320,512]{1,0:T(8,128)(2,1)S(1)}, bf16[320,512]{1,0:T(8,128)(2,1)S(1)}, u32[]{:S(2)}, u32[]{:S(2)}) collective-permute-start(bf16[320,512]{1,0:T(8,128)(2,1)S(1)} %shard_map.115), channel_id=1, source_target_pairs={{0,1},{1,0},{2,3},{3,2},{4,5},{5,4},{6,7},{7,6},{8,9},{9,8},{10,11... | collective-permute-start | bytes 983048 | tf_op jit(solution)/shard_map/ppermute | solution.py:299
  37.4 7.0 %collective-permute-start.11 = (bf16[320,512]{1,0:T(8,128)(2,1)S(1)}, bf16[320,512]{1,0:T(8,128)(2,1)S(1)}, u32[]{:S(2)}, u32[]{:S(2)}) collective-permute-start(bf16[320,512]{1,0:T(8,128)(2,1)S(1)} %shard_map.115), channel_id=1, source_target_pairs={{1,2},{2,1},{0,4},{3,7},{5,6},{6,5},{4,0},{7,3},{9,10},{10,9},{8,1... | collective-permute-start | bytes 983048 | tf_op jit(solution)/shard_map/ppermute | solution.py:306
  37.4 8.0 %collective-permute-start.16 = (bf16[160,640]{1,0:T(8,128)(2,1)S(1)}, bf16[160,640]{1,0:T(8,128)(2,1)S(1)}, u32[]{:S(2)}, u32[]{:S(2)}) collective-permute-start(bf16[160,640]{1,0:T(8,128)(2,1)S(1)} %get-tuple-element.63), channel_id=1, source_target_pairs={{0,8},{4,12},{8,0},{12,4},{16,24},{20,28},{24,16},{28,20},{1,9},{5... | collective-permute-start | bytes 614408 | tf_op jit(solution)/shard_map/ppermute | solution.py:296
  38.4 7.9 %collective-permute-start.18 = (bf16[160,640]{1,0:T(8,128)(2,1)S(1)}, bf16[160,640]{1,0:T(8,128)(2,1)S(1)}, u32[]{:S(2)}, u32[]{:S(2)}) collective-permute-start(bf16[160,640]{1,0:T(8,128)(2,1)S(1)} %get-tuple-element.66), channel_id=1, source_target_pairs={{0,16},{4,20},{8,24},{12,28},{16,0},{20,4},{24,8},{28,12},{1,17},{... | collective-permute-start | bytes 614408 | tf_op jit(solution)/shard_map/ppermute | solution.py:296
  39.4 9.8 %collective-permute-start.17 = (bf16[160,640]{1,0:T(8,128)(2,1)S(1)}, bf16[160,640]{1,0:T(8,128)(2,1)S(1)}, u32[]{:S(2)}, u32[]{:S(2)}) collective-permute-start(bf16[160,640]{1,0:T(8,128)(2,1)S(1)} %get-tuple-element.57), channel_id=1, source_target_pairs={{0,8},{4,12},{8,0},{12,4},{16,24},{20,28},{24,16},{28,20},{1,9},{5... | collective-permute-start | bytes 614408 | tf_op jit(solution)/shard_map/ppermute | solution.py:296
  43.4 6.6 %collective-permute-start.19 = (bf16[160,640]{1,0:T(8,128)(2,1)S(1)}, bf16[160,640]{1,0:T(8,128)(2,1)S(1)}, u32[]{:S(2)}, u32[]{:S(2)}) collective-permute-start(bf16[160,640]{1,0:T(8,128)(2,1)S(1)} %get-tuple-element.68), channel_id=1, source_target_pairs={{0,16},{4,20},{8,24},{12,28},{16,0},{20,4},{24,8},{28,12},{1,17},{... | collective-permute-start | bytes 614408 | tf_op jit(solution)/shard_map/ppermute | solution.py:296
  44.3 7.3 %collective-permute-start.15 = (bf16[256,640]{1,0:T(8,128)(2,1)S(1)}, bf16[256,640]{1,0:T(8,128)(2,1)S(1)}, u32[]{:S(2)}, u32[]{:S(2)}) collective-permute-start(bf16[256,640]{1,0:T(8,128)(2,1)S(1)} %get-tuple-element.60), channel_id=1, source_target_pairs={{0,4},{4,0},{8,12},{12,8},{16,20},{20,16},{24,28},{28,24},{1,5},{5... | collective-permute-start | bytes 983048 | tf_op jit(solution)/shard_map/ppermute | solution.py:296
  45.3 6.3 %copy-start.1 = (bf16[256,640]{1,0:T(8,128)(2,1)S(1)}, bf16[256,640]{1,0:T(8,128)(2,1)}, u32[]{:S(2)}) copy-start(bf16[256,640]{1,0:T(8,128)(2,1)} %q_ref.3) | copy-start | bytes 983044
  45.4 6.3 %copy-start.3 = (bf16[256,640]{1,0:T(8,128)(2,1)S(1)}, bf16[256,640]{1,0:T(8,128)(2,1)}, u32[]{:S(2)}) copy-start(bf16[256,640]{1,0:T(8,128)(2,1)} %k_ref.3) | copy-start | bytes 983044
  45.4 6.3 %copy-start.5 = (bf16[256,640]{1,0:T(8,128)(2,1)S(1)}, bf16[256,640]{1,0:T(8,128)(2,1)}, u32[]{:S(2)}) copy-start(bf16[256,640]{1,0:T(8,128)(2,1)} %v_ref.3) | copy-start | bytes 983044
  45.4 12.6 %collective-permute-start.14 = (bf16[320,512]{1,0:T(8,128)(2,1)S(1)}, bf16[320,512]{1,0:T(8,128)(2,1)S(1)}, u32[]{:S(2)}, u32[]{:S(2)}) collective-permute-start(bf16[320,512]{1,0:T(8,128)(2,1)S(1)} %shard_map.117), channel_id=1, source_target_pairs={{1,2},{2,1},{0,4},{3,7},{5,6},{6,5},{4,0},{7,3},{9,10},{10,9},{8,1... | collective-permute-start | bytes 983048 | tf_op jit(solution)/shard_map/ppermute | solution.py:306
  46.3 11.7 %collective-permute-start.12 = (bf16[320,512]{1,0:T(8,128)(2,1)S(1)}, bf16[320,512]{1,0:T(8,128)(2,1)S(1)}, u32[]{:S(2)}, u32[]{:S(2)}) collective-permute-start(bf16[320,512]{1,0:T(8,128)(2,1)S(1)} %shard_map.116), channel_id=1, source_target_pairs={{0,1},{1,0},{2,3},{3,2},{4,5},{5,4},{6,7},{7,6},{8,9},{9,8},{10,11... | collective-permute-start | bytes 983048 | tf_op jit(solution)/shard_map/ppermute | solution.py:299
  50.2 6.0 %collective-permute-start.20 = (bf16[160,640]{1,0:T(8,128)(2,1)S(1)}, bf16[160,640]{1,0:T(8,128)(2,1)S(1)}, u32[]{:S(2)}, u32[]{:S(2)}) collective-permute-start(bf16[160,640]{1,0:T(8,128)(2,1)S(1)} %get-tuple-element.71), channel_id=1, source_target_pairs={{0,16},{4,20},{8,24},{12,28},{16,0},{20,4},{24,8},{28,12},{1,17},{... | collective-permute-start | bytes 614408 | tf_op jit(solution)/shard_map/ppermute | solution.py:296
  50.9 6.0 %collective-permute-start.21 = (bf16[160,640]{1,0:T(8,128)(2,1)S(1)}, bf16[160,640]{1,0:T(8,128)(2,1)S(1)}, u32[]{:S(2)}, u32[]{:S(2)}) collective-permute-start(bf16[160,640]{1,0:T(8,128)(2,1)S(1)} %get-tuple-element.72), channel_id=1, source_target_pairs={{0,8},{4,12},{8,0},{12,4},{16,24},{20,28},{24,16},{28,20},{1,9},{5... | collective-permute-start | bytes 614408 | tf_op jit(solution)/shard_map/ppermute | solution.py:296
  57.9 2.2 %copy-start.6 = (bf16[256,640]{1,0:T(8,128)(2,1)S(1)}, bf16[256,640]{1,0:T(8,128)(2,1)}, u32[]{:S(2)}) copy-start(bf16[256,640]{1,0:T(8,128)(2,1)} %residual_ref.1) | copy-start | bytes 983044
  58.4 1.7 %collective-permute-start.22 = (f32[320,256]{1,0:T(8,128)S(1)}, f32[320,256]{1,0:T(8,128)S(1)}, u32[]{:S(2)}, u32[]{:S(2)}) collective-permute-start(f32[320,256]{1,0:T(8,128)S(1)} %get-tuple-element.76), channel_id=1, source_target_pairs={{0,4},{4,0},{8,12},{12,8},{16,20},{20,16},{24,28},{28,24},{1,5},{5... | collective-permute-start | bytes 983048 | tf_op jit(solution)/shard_map/ppermute | solution.py:296

commit v3 on v2

--- a/solution.py
+++ b/solution.py
@@ -106,22 +106,65 @@
     return (z == 1) | (z == 2)
 
 
+def own_bits():
+    core = lax.rem(lax.axis_index("blk"), 2)
+    return 1 + core, 2 - core
+
+
+def late_slot(group):
+    return plane_slot(lax.axis_index("shard") ^ 3, group)
+
+
 def project_part(w_ref, ctx_ref, plane, group):
     return dot(w_ref[plane_slot(plane, group)], ctx_ref[...], NT)
 
 
-def first_message_kernel(group, w_ref, own_ref, other_ref, passing_ref, out_ref):
+def choose(condition, then, other):
+    pl.when(condition)(then)
+    pl.when(~condition)(other)
+
+
+def first_message_kernel(group, own_w, near_w, soon_w, own_ref, other_ref, passing_ref, out_ref):
     count = own_ref.shape[0]
-    z = lax.axis_index("shard")
+    z, slot, first = lax.axis_index("shard"), late_slot(group), own_bits()[0]
+
+    def share(w_ref):
+        for i, ctx_ref in enumerate((own_ref, other_ref)):
+            out_ref[:, pl.ds(i * count, count)] = dot(w_ref[...], ctx_ref[...], NT).astype(BF16)
 
     @pl.when(is_inner(z))
     def _():
         out_ref[...] = passing_ref[...]
 
+    for place, w_ref in (
+        (slot == 0, own_w),
+        (slot == first, near_w),
+        ((slot != 0) & (slot != first), soon_w),
+    ):
+        pl.when(~is_inner(z) & place)(lambda w_ref=w_ref: share(w_ref))
+
+
+def all_columns_kernel(group, own_w, near_w, soon_w, last_w, out_ref):
+    first, second = own_bits()
+    out_ref[0] = own_w[...]
+    out_ref[first] = near_w[...]
+    far_soon = (late_slot(group) & first) == first
+    out_ref[jnp.where(far_soon, 3, second)] = soon_w[...]
+    out_ref[jnp.where(far_soon, second, 3)] = last_w[...]
+
+
+def second_message_kernel(group, w_ref, own_ref, other_ref, passing_ref, out_ref):
+    count = own_ref.shape[0]
+    z = lax.axis_index("shard")
+
+    @pl.when(is_inner(z))
+    def _():
+        out_ref[...] = passing_ref[...]
+
     @pl.when(~is_inner(z))
     def _():
         for i, ctx_ref in enumerate((own_ref, other_ref)):
-            part = project_part(w_ref, ctx_ref, z ^ 3, group)
+            part = project_part(w_ref, ctx_ref, z ^ 2, group)
             out_ref[:, pl.ds(i * count, count)] = part.astype(BF16)
 
 
@@ -209,80 +252,54 @@
     return part + dot(unit_ref[:, count:], other_ref[...], NN)
 
 
-def late_slot(group):
-    return plane_slot(lax.axis_index("shard") ^ 3, group)
-
-
-def choose(condition, then, other):
-    pl.when(condition)(then)
-    pl.when(~condition)(other)
-
-
 def weight_early_kernel(group, *refs):
-    *unit_refs, own_ref, other_ref, send_a, send_b, keep_a, keep_b, rest_a, rest_b = refs
-    rows = rest_a.shape[0]
-    late = late_slot(group)
+    *unit_refs, own_ref, other_ref, send, keep, rest = refs
+    late, first = late_slot(group), own_bits()[0]
 
     def body(plane, unit_ref):
         slot = plane_slot(plane, group)
         part = weight_part(unit_ref, own_ref, other_ref)
 
-        def place(block, bit, send, keep, rest):
-            def into_rest():
-                rest[...] = block
-
-            def into_send():
-                send[...] = block.astype(BF16)
-
-            def into_keep():
-                keep[...] = block
-
-            def early():
-                choose((slot & bit) == bit, into_send, into_keep)
-
-            choose(slot == (late ^ bit), into_rest, early)
-
-        place(part[:rows], 1, send_a, keep_a, rest_a)
-        place(part[rows:], 2, send_b, keep_b, rest_b)
+        def into_rest():
+            rest[...] = part
+
+        def into_send():
+            send[...] = part.astype(BF16)
+
+        def into_keep():
+            keep[...] = part
+
+        def early():
+            choose((slot & first) == first, into_send, into_keep)
+
+        choose(slot == (late ^ first), into_rest, early)
 
     early_planes(*unit_refs, body)
 
 
-def weight_late_kernel(group, *refs):
-    inner_ref, outer_ref, own_ref, other_ref, rest_a, rest_b, send_a, send_b, keep_a, keep_b = refs
-    rows = rest_a.shape[0]
-    late = late_slot(group)
+def weight_late_kernel(group, inner_ref, outer_ref, own_ref, other_ref, rest, send, keep):
+    late, first = late_slot(group), own_bits()[0]
+    sends = (late & first) == first
 
     def body(plane, unit_ref):
         part = weight_part(unit_ref, own_ref, other_ref)
-
-        def place(block, bit, send, keep, rest):
-            sends = (late & bit) == bit
-            send[...] = jnp.where(sends, block, rest[...]).astype(BF16)
-            keep[...] = jnp.where(sends, rest[...], block)
-
-        place(part[:rows], 1, send_a, keep_a, rest_a)
-        place(part[rows:], 2, send_b, keep_b, rest_b)
+        send[...] = jnp.where(sends, part, rest[...]).astype(BF16)
+        keep[...] = jnp.where(sends, rest[...], part)
 
     late_plane(inner_ref, outer_ref, body)
 
 
-def half_sum_kernel(group, *refs):
-    late = late_slot(group)
-    send_a, send_b, left_a, left_b = refs[8:]
-    for stream, send, left, keeps in ((0, send_a, left_a, 2), (1, send_b, left_b, 1)):
-        early_keep, early_from, late_keep, late_from = refs[4 * stream : 4 * stream + 4]
-        early_sum = early_keep[...] + early_from[...].astype(F32)
-        late_sum = late_keep[...] + late_from[...].astype(F32)
-        goes = (late & keeps) == keeps
-        send[...] = jnp.where(goes, late_sum, early_sum).astype(BF16)
-        left[...] = jnp.where(goes, early_sum, late_sum)
-
-
-def grad_sum_kernel(scale, left_a, left_b, from_a, from_b, out_ref):
-    rows = left_a.shape[0]
-    out_ref[:rows] = (left_a[...] + from_a[...].astype(F32)) * scale
-    out_ref[rows:] = (left_b[...] + from_b[...].astype(F32)) * scale
+def half_sum_kernel(group, early_keep, early_from, late_keep, late_from, send, left):
+    second = own_bits()[1]
+    goes = (late_slot(group) & second) == second
+    early_sum = early_keep[...] + early_from[...].astype(F32)
+    late_sum = late_keep[...] + late_from[...].astype(F32)
+    send[...] = jnp.where(goes, late_sum, early_sum).astype(BF16)
+    left[...] = jnp.where(goes, early_sum, late_sum)
+
+
+def grad_sum_kernel(scale, left_ref, from_ref, out_ref):
+    out_ref[...] = (left_ref[...] + from_ref[...].astype(F32)) * scale
 
 
 def solution(mesh):
@@ -295,6 +312,10 @@
     def swap(value, bit):
         return lax.ppermute(value, "blk", [(i, i ^ bit) for i in range(blk)])
 
+    def core_swap(value, first):
+        bits = (1, 2) if first else (2, 1)
+        return lax.ppermute(value, "blk", [(i, i ^ (group * bits[i % 2])) for i in range(blk)])
+
     def pair_swap(value):
         return lax.ppermute(value, "shard", [(0, 1), (1, 0), (2, 3), (3, 2)])
 
@@ -305,13 +326,15 @@
             pairs += [(b * planes + z, (b ^ 1) * planes + z) for z in (0, 3)]
         return lax.ppermute(value, ("blk", "shard"), pairs)
 
+    def together(*values):
+        return lax.optimization_barrier(values)
+
     def bound(kernel, *static):
         return lambda *refs: kernel(*static, *refs)
 
     def per_device(queries, key_rows, values, segment_ids, residual, out_weight, cotangent):
         count, width = queries.shape
         half = width // 2
-        cut = half // 2
         position = lax.axis_index("blk") // 2
         unit_flops = 4 * half * count * width
         message = shape(half, 2 * count)
@@ -327,82 +350,118 @@
                 [jnp.where(upper, there, w_own), jnp.where(upper, w_own, there)], axis=0
             )
             bit *= 2
-        w_one, w_two = swap(w_own, group), swap(w_own, 2 * group)
+
+        w_near = core_swap(w_own, True)
         unit = make_unit(cotangent, cot_other, strips)
         near, inner_far = pair_swap(unit), mid_swap(unit)
+
+        first = own_bits()[0]
+        far_soon = (late_slot(group) & first) == first
+        w_soon = core_swap(jnp.where(far_soon, w_near, w_own), False)
+        w_last = core_swap(jnp.where(far_soon, w_own, w_near), False)
+        asked, w_near = together(queries, w_near)
         ctx, probs = call(
             forward_kernel,
             (shape(count, width), shape(width // HEAD, count, count, dtype=F32)),
-            queries,
+            asked,
             key_rows,
             values,
             segment_ids,
             flops=4 * count * count * width,
         )
+        near, inner_far, ctx = together(near, inner_far, ctx)
         ctx_other = swap(ctx, 1)
-        near, inner_far, w_one, w_two, ctx = lax.optimization_barrier(
-            (near, inner_far, w_one, w_two, ctx)
-        )
-        w_far = [swap(w_two[:cut], group), swap(w_one[cut:], 2 * group)]
-        w_all = jnp.stack([w_own, w_one, w_two, jnp.concatenate(w_far, axis=0)])
-
-        outer_next, inner_next = pair_swap(inner_far), mid_swap(near)
-        outer_next, inner_next = lax.optimization_barrier((outer_next, inner_next))
-        early = call(
-            bound(d_context_early_kernel, group),
-            (shape(2 * count, width, dtype=F32),),
-            unit,
-            near,
-            outer_next,
-            inner_next,
-            w_all,
-            flops=3 * unit_flops,
-        )[0]
-
+
+        inner_next = mid_swap(near)
+        out = call(
+            bound(first_message_kernel, group),
+            (message,),
+            w_own,
+            w_near,
+            w_soon,
+            ctx,
+            ctx_other,
+            inner_far,
+            flops=unit_flops,
+        )[0]
+        pair_two = pair_swap(out)
+        w_all = call(
+            bound(all_columns_kernel, group),
+            (shape(planes, half, width),),
+            w_own,
+            w_near,
+            w_soon,
+            w_last,
+        )[0]
         sources = (w_all, ctx, ctx_other)
+
         out = call(
-            bound(first_message_kernel, group), (message,), *sources, inner_next, flops=unit_flops
-        )[0]
-        block, rest = shape(cut, width), shape(cut, width, dtype=F32)
-        early_send_a, early_send_b, early_keep_a, early_keep_b, rest_a, rest_b = call(
+            bound(second_message_kernel, group), (message,), *sources, inner_next, flops=unit_flops
+        )[0]
+        pair_three = pair_swap(out)
+        out, pair_two = together(out, pair_two)
+        out = call(
+            bound(message_kernel, 2, group), (message,), *sources, pair_two, flops=unit_flops
+        )[0]
+        mid_three = mid_swap(out)
+        block, rest = shape(half, width), shape(half, width, dtype=F32)
+        ready = (unit, near, pair_two, inner_next)
+        early_send, early_keep, early_rest = call(
             bound(weight_early_kernel, group),
-            (block, block, rest, rest, rest, rest),
-            unit,
-            near,
-            outer_next,
-            inner_next,
+            (block, rest, rest),
+            *ready,
             ctx,
             ctx_other,
             flops=3 * unit_flops,
         )
-        early_from_a, early_from_b = swap(early_send_a, group), swap(early_send_b, 2 * group)
-        passed, early, rest_a = lax.optimization_barrier((pair_swap(out), early, rest_a))
-        late_send_a, late_send_b, late_keep_a, late_keep_b = call(
+        early_from = core_swap(early_send, True)
+        d_ctx_early = call(
+            bound(d_context_early_kernel, group),
+            (shape(2 * count, width, dtype=F32),),
+            *ready,
+            w_all,
+            flops=3 * unit_flops,
+        )[0]
+        pair_three, d_ctx_early, early_rest = together(pair_three, d_ctx_early, early_rest)
+
+        late_send, late_keep = call(
             bound(weight_late_kernel, group),
-            (block, block, rest, rest),
+            (block, rest),
             inner_far,
-            passed,
+            pair_three,
             ctx,
             ctx_other,
-            rest_a,
-            rest_b,
+            early_rest,
             flops=unit_flops,
         )
-        late_from_a, late_from_b = swap(late_send_a, group), swap(late_send_b, 2 * group)
-        out = call(
-            bound(message_kernel, 2, group), (message,), *sources, passed, flops=unit_flops
-        )[0]
-        from_pair, from_mid = pair_swap(out), mid_swap(out)
-        early, late_send_a = lax.optimization_barrier((early, late_send_a))
+        late_from = core_swap(late_send, True)
+        d_ctx_early, late_send = together(d_ctx_early, late_send)
         mine, send = call(
             bound(d_context_late_kernel, group),
             (shape(count, width, dtype=F32), shape(count, width)),
             inner_far,
-            passed,
+            pair_three,
             w_all,
-            early,
+            d_ctx_early,
             flops=unit_flops,
         )
+        d_ctx_other = swap(send, 1)
+        mine, pair_three, early_from = together(mine, pair_three, early_from)
+        out = call(
+            bound(message_kernel, 3, group), (message,), *sources, pair_three, flops=unit_flops
+        )[0]
+        mid_four = mid_swap(out)
+        out = call(
+            bound(message_kernel, 1, group), (message,), *sources, mid_three, flops=unit_flops
+        )[0]
+        pair_four = pair_swap(out)
+        late_from, out = together(late_from, out)
+        send, left = call(
+            bound(half_sum_kernel, group), (block, rest), early_keep, early_from, late_keep, late_from
+        )
+        second_from = core_swap(send, False)
+
+        mine, send = together(mine, send)
         d_queries, d_keys, d_values = call(
             backward_kernel,
             (shape(count, width),) * 3,
@@ -411,36 +470,27 @@
             values,
             probs,
             mine,
-            swap(send, 1),
+            d_ctx_other,
             flops=10 * count * count * width,
         )
-        to_pair = call(
-            bound(message_kernel, 1, group), (message,), *sources, from_mid, flops=unit_flops
-        )[0]
-        to_mid = call(
-            bound(message_kernel, 3, group), (message,), *sources, from_pair, flops=unit_flops
-        )[0]
-        send_a, send_b, left_a, left_b = call(
-            bound(half_sum_kernel, group),
-            (block, block, rest, rest),
-            early_keep_a,
-            early_from_a,
-            late_keep_a,
-            late_from_a,
-            early_keep_b,
-            early_from_b,
-            late_keep_b,
-            late_from_b,
-        )
-        from_a, from_b = swap(send_a, 2 * group), swap(send_b, group)
+        pair_four, mid_four, d_queries = together(pair_four, mid_four, d_queries)
+        keep, send = call(
+            bound(last_project_kernel, group),
+            (shape(half, count, dtype=F32),) * 2,
+            *sources,
+            pair_four,
+            mid_four,
+            flops=unit_flops,
+        )
+        last_other = swap(send, 1)
+        left, keep = together(left, keep)
         total = call(
             bound(grad_sum_kernel, 1.0 / math.sqrt(count * blk)),
             (shape(half, width, dtype=F32),),
-            left_a,
-            left_b,
-            from_a,
-            from_b,
-        )[0]
+            left,
+            second_from,
+        )[0]
+        layer_out = make_layer_out(residual, keep, last_other, strips)
         bit = strips // 2
         while bit >= 1:
             lower, upper = jnp.split(total, 2, axis=0)
@@ -448,19 +498,6 @@
             sent = jnp.where(right, lower, upper)
             total = jnp.where(right, upper, lower) + swap(sent, 2 * bit)
             bit //= 2
-
-        from_pair, from_mid, d_queries, total = lax.optimization_barrier(
-            (pair_swap(to_pair), mid_swap(to_mid), d_queries, total)
-        )
-        keep, send = call(
-            bound(last_project_kernel, group),
-            (shape(half, count, dtype=F32),) * 2,
-            *sources,
-            from_pair,
-            from_mid,
-            flops=unit_flops,
-        )
-        layer_out = make_layer_out(residual, keep, swap(send, 1), strips)
 
         return layer_out, total, d_queries, d_keys, d_values
 

time: 61.4 us -> 55.7 us (0.907)
  waiting for transfers between devices: 21.4 us -> 14.6 us
  starting transfers between devices: 21.2 us -> 25.7 us
  local copies, waits for them, and re-layouts: 4.63 us -> 1 us
    ppermute x14 -> x4, starting transfers between devices: 11.4 us -> 0.15 us  [swap(): return lax.ppermute(value, 'blk', [(i, i ^ bit) for i in range(blk)])]
    ppermute x0 -> x6, starting transfers between devices: none -> 11.2 us  [core_swap(): lax.ppermute(value, 'blk', [(i, i ^ group * bits[i % 2]) for i in range(b...]
    ppermute x14 -> x4, waiting for transfers between devices: 9.62 us -> 1.93 us  [swap(): return lax.ppermute(value, 'blk', [(i, i ^ bit) for i in range(blk)])]
    ppermute x0 -> x6, waiting for transfers between devices: none -> 6.8 us  [core_swap(): lax.ppermute(value, 'blk', [(i, i ^ group * bits[i % 2]) for i in range(b...]
    ppermute x5 -> x4, waiting for transfers between devices: 11.7 us -> 5.84 us  [pair_swap(): return lax.ppermute(value, 'shard', [(0, 1), (1, 0), (2, 3), (3, 2)])]
    ppermute x5 -> x4, starting transfers between devices: 9.21 us -> 14.2 us  [pair_swap(): return lax.ppermute(value, 'shard', [(0, 1), (1, 0), (2, 3), (3, 2)])]
    unnamed x20 -> x14, local copies, waits for them, and re-layouts: 4.59 us -> 1 us
    pallas_call x15 -> x17, Pallas kernels: 12.8 us -> 13.4 us  [call(): pl.pallas_call(kernel, out_shape=tuple(outs), in_specs=[pl.BlockSpec(memo...]
  transfers between devices with their start and end apart: 23 -> 18, of which waited for: 14 -> 9; matrix products, arithmetic and copies ran while one was open for 0% -> 0% of each run, Pallas kernels for 17% -> 22%
where the time goes in v3:
time: 55.7 us; the launch traced here: 55.5 us
  starting transfers between devices  25.7 us (46%)
  waiting for transfers between devices  14.6 us (26%)
  Pallas kernels  13.4 us (24%)
  local copies, waits for them, and re-layouts  1 us (2%)
  between operations  0.83 us (1%)
    ppermute x4, starting transfers between devices, pair_swap(): return lax.ppermute(value, 'shard', [(0, 1), (1, 0), (2, 3), (3, 2)])  14.2 us
    pallas_call x17, Pallas kernels, call(): pl.pallas_call(kernel, out_shape=tuple(outs), in_specs=[pl.BlockSpec(memo...  13.4 us
    ppermute x6, starting transfers between devices, core_swap(): lax.ppermute(value, 'blk', [(i, i ^ group * bits[i % 2]) for i in range(b...  11.2 us
    ppermute x6, waiting for transfers between devices, core_swap(): lax.ppermute(value, 'blk', [(i, i ^ group * bits[i % 2]) for i in range(b...  6.8 us
    ppermute x4, waiting for transfers between devices, pair_swap(): return lax.ppermute(value, 'shard', [(0, 1), (1, 0), (2, 3), (3, 2)])  5.84 us
    ppermute x4, waiting for transfers between devices, swap(): return lax.ppermute(value, 'blk', [(i, i ^ bit) for i in range(blk)])  1.93 us
  transfers between devices with their start and end apart: 18, of which 9 were waited for; matrix products, arithmetic and copies ran while one was open for 0% of the time, Pallas kernels for 22%

profile of v3, /device:TPU:0, one launch (start us, length us, event | category | flops | bytes accessed | tf_op | source)
XLA Modules:
  0.0 55.5 jit_solution(978456612959168706)
XLA Ops:
  0.6 0.0 copy-start
  0.6 3.0 %collective-permute-start.3 = (bf16[320,640]{1,0:T(8,128)(2,1)}, bf16[320,640]{1,0:T(8,128)(2,1)S(1)}, u32[]{:S(2)}, u32[]{:S(2)}) collective-permute-start(bf16[320,640]{1,0:T(8,128)(2,1)} %bitcast.3), channel_id=1, source_target_pairs={{0,8},{4,20},{8,0},{12,28},{16,24},{20,4},{24,16},{28,12},{1,9},{5... | collective-permute-start | bytes 1228808 | tf_op jit(solution)/shard_map/ppermute | solution.py:317
  3.6 0.0 collective-permute-start
  3.6 0.0 copy-start.1
  3.7 1.8 %collective-permute-done.other_ref = bf16[256,640]{1,0:T(8,128)(2,1)S(1)} collective-permute-done((bf16[256,640]{1,0:T(8,128)(2,1)}, bf16[256,640]{1,0:T(8,128)(2,1)S(1)}, u32[]{:S(2)}, u32[]{:S(2)}) %collective-permute-start) | collective-permute-done | bytes 327712 | tf_op jit(solution)/shard_map/ppermute | solution.py:313
  5.5 1.0 %copy-done.5 = bf16[256,640]{1,0:T(8,128)(2,1)S(1)} copy-done((bf16[256,640]{1,0:T(8,128)(2,1)S(1)}, bf16[256,640]{1,0:T(8,128)(2,1)}, u32[]{:S(2)}) %copy-start.5) | copy-done | bytes 327704
  6.5 0.2 shard_map.110.refs_0_
  6.7 1.6 %collective-permute-start.1 = (bf16[320,512]{1,0:T(8,128)(2,1)S(1)}, bf16[320,512]{1,0:T(8,128)(2,1)S(1)}, u32[]{:S(2)}, u32[]{:S(2)}) collective-permute-start(bf16[320,512]{1,0:T(8,128)(2,1)S(1)} %shard_map.110.refs_0_), channel_id=1, source_target_pairs={{0,1},{1,0},{2,3},{3,2},{4,5},{5,4},{6,7},{7,6},{8,9},{9,8},{10,11... | collective-permute-start | bytes 983048 | tf_op jit(solution)/shard_map/ppermute | solution.py:320
  8.4 0.0 collective-permute-start.2
  8.4 1.4 %collective-permute-done.3.refs_1_ = bf16[320,640]{1,0:T(8,128)(2,1)S(1)} collective-permute-done((bf16[320,640]{1,0:T(8,128)(2,1)}, bf16[320,640]{1,0:T(8,128)(2,1)S(1)}, u32[]{:S(2)}, u32[]{:S(2)}) %collective-permute-start.3) | collective-permute-done | bytes 409632 | tf_op jit(solution)/shard_map/ppermute | solution.py:317
  9.8 0.0 copy-done
  9.8 0.1 broadcast_select_fusion
  9.9 2.1 %collective-permute-start.4 = (bf16[320,640]{1,0:T(8,128)(2,1)S(1)}, bf16[320,640]{1,0:T(8,128)(2,1)S(1)}, u32[]{:S(2)}, u32[]{:S(2)}) collective-permute-start(bf16[320,640]{1,0:T(8,128)(2,1)S(1)} %get-tuple-element.78), channel_id=1, source_target_pairs={{0,16},{4,12},{8,24},{12,4},{16,0},{20,28},{24,8},{28,20},{1,17},{... | collective-permute-start | bytes 1228808 | tf_op jit(solution)/shard_map/ppermute | solution.py:317
  12.0 0.0 copy-done.1
  12.0 0.0 copy-done.2
  12.0 0.0 copy-done.3
  12.0 0.0 copy-done.6
  12.0 1.3 %shard_map.111 = (bf16[256,640]{1,0:T(8,128)(2,1)S(1)}, f32[5,256,256]{2,1,0:T(8,128)S(1)}) custom-call(bf16[256,640]{1,0:T(8,128)(2,1)S(1)} %copy-done.1, bf16[256,640]{1,0:T(8,128)(2,1)S(1)} %copy-done.2, bf16[256,640]{1,0:T(8,128)(2,1)S(1)} %copy-done.3, s32[1,256]{1,0:T(1,128)S(1)} %copy-done.6), custom_call_target="tpu_custom_call" | custom-call | flops 167772160 | bytes 2622464 | tf_op jit(solution)/shard_map/pallas_call | solution.py:25
  13.3 3.3 %collective-permute-done.1.refs_1_ = bf16[320,512]{1,0:T(8,128)(2,1)S(1)} collective-permute-done((bf16[320,512]{1,0:T(8,128)(2,1)S(1)}, bf16[320,512]{1,0:T(8,128)(2,1)S(1)}, u32[]{:S(2)}, u32[]{:S(2)}) %collective-permute-start.1) | collective-permute-done | bytes 327712 | tf_op jit(solution)/shard_map/ppermute | solution.py:320
  16.5 0.0 collective-permute-done.2.refs_5_.refs_0_
  16.5 0.0 collective-permute-start.6
  16.5 1.5 %collective-permute-start.5 = (bf16[320,640]{1,0:T(8,128)(2,1)S(1)}, bf16[320,640]{1,0:T(8,128)(2,1)S(1)}, u32[]{:S(2)}, u32[]{:S(2)}) collective-permute-start(bf16[320,640]{1,0:T(8,128)(2,1)S(1)} %get-tuple-element.77), channel_id=1, source_target_pairs={{0,16},{4,12},{8,24},{12,4},{16,0},{20,28},{24,8},{28,20},{1,17},{... | collective-permute-start | bytes 1228808 | tf_op jit(solution)/shard_map/ppermute | solution.py:317
  18.1 0.0 collective-permute-start.7
  18.1 0.0 collective-permute-done.4.refs_2_
  18.1 0.1 collective-permute-done.6.refs_2_.refs_4_.refs_5_.refs_3_
  18.2 0.4 shard_map.114
  18.6 4.0 %collective-permute-start.8 = (bf16[320,512]{1,0:T(8,128)(2,1)S(1)}, bf16[320,512]{1,0:T(8,128)(2,1)S(1)}, u32[]{:S(2)}, u32[]{:S(2)}) collective-permute-start(bf16[320,512]{1,0:T(8,128)(2,1)S(1)} %shard_map.114), channel_id=1, source_target_pairs={{0,1},{1,0},{2,3},{3,2},{4,5},{5,4},{6,7},{7,6},{8,9},{9,8},{10,11... | collective-permute-start | bytes 983048 | tf_op jit(solution)/shard_map/ppermute | solution.py:320
  22.6 1.9 %collective-permute-done.5.refs_3_ = bf16[320,640]{1,0:T(8,128)(2,1)S(1)} collective-permute-done((bf16[320,640]{1,0:T(8,128)(2,1)S(1)}, bf16[320,640]{1,0:T(8,128)(2,1)S(1)}, u32[]{:S(2)}, u32[]{:S(2)}) %collective-permute-start.5) | collective-permute-done | bytes 409632 | tf_op jit(solution)/shard_map/ppermute | solution.py:317
  24.5 0.1 shard_map.112.refs_0_.refs_4_.refs_2_
  24.6 0.0 collective-permute-done.7.refs_3_
  24.6 0.5 shard_map.113
  25.1 5.0 %collective-permute-start.9 = (bf16[320,512]{1,0:T(8,128)(2,1)S(1)}, bf16[320,512]{1,0:T(8,128)(2,1)S(1)}, u32[]{:S(2)}, u32[]{:S(2)}) collective-permute-start(bf16[320,512]{1,0:T(8,128)(2,1)S(1)} %shard_map.113), channel_id=1, source_target_pairs={{0,1},{1,0},{2,3},{3,2},{4,5},{5,4},{6,7},{7,6},{8,9},{9,8},{10,11... | collective-permute-start | bytes 983048 | tf_op jit(solution)/shard_map/ppermute | solution.py:320
  30.1 0.0 collective-permute-done.8.refs_2_.refs_3_
  30.1 1.6 %shard_map.115 = (bf16[320,640]{1,0:T(8,128)(2,1)S(1)}, f32[320,640]{1,0:T(8,128)S(1)}, f32[320,640]{1,0:T(8,128)S(1)}) custom-call(bf16[320,512]{1,0:T(8,128)(2,1)S(1)} %shard_map.110.refs_0_, bf16[320,512]{1,0:T(8,128)(2,1)S(1)} %collective-permute-done.1.refs_1_, bf16[320,512]{1,0:T(8,128)(2,1)S(1)} %collective-permute-done.8.refs_2_.refs_3_, ...), custom_call_target="tpu_custom_call" | custom-call | flops 629145600 | bytes 4014080 | tf_op jit(solution)/shard_map/pallas_call | solution.py:25
  31.7 1.1 %collective-permute-start.10 = (bf16[320,640]{1,0:T(8,128)(2,1)S(1)}, bf16[320,640]{1,0:T(8,128)(2,1)S(1)}, u32[]{:S(2)}, u32[]{:S(2)}) collective-permute-start(bf16[320,640]{1,0:T(8,128)(2,1)S(1)} %get-tuple-element.56), channel_id=1, source_target_pairs={{0,8},{4,20},{8,0},{12,28},{16,24},{20,4},{24,16},{28,12},{1,9},{5... | collective-permute-start | bytes 1228808 | tf_op jit(solution)/shard_map/ppermute | solution.py:317
  32.8 0.4 shard_map.119
  33.3 0.1 collective-permute-start.12
  33.4 1.5 %shard_map.116.refs_3_ = f32[512,640]{1,0:T(8,128)S(1)} custom-call(bf16[320,512]{1,0:T(8,128)(2,1)S(1)} %shard_map.110.refs_0_, bf16[320,512]{1,0:T(8,128)(2,1)S(1)} %collective-permute-done.1.refs_1_, bf16[320,512]{1,0:T(8,128)(2,1)S(1)} %collective-permute-done.8.refs_2_.refs_3_, bf16[320,512]{1,0:T(8,128)(2,1)S(1)} %collective-permute-done.7.refs_3_, ...), custom_call_target="tpu_custom_call" | custom-call | flops 629145600 | bytes 4259840 | tf_op jit(solution)/shard_map/pallas_call | solution.py:25
  34.9 2.0 %collective-permute-done.9.refs_1_.refs_3_ = bf16[320,512]{1,0:T(8,128)(2,1)S(1)} collective-permute-done((bf16[320,512]{1,0:T(8,128)(2,1)S(1)}, bf16[320,512]{1,0:T(8,128)(2,1)S(1)}, u32[]{:S(2)}, u32[]{:S(2)}) %collective-permute-start.9) | collective-permute-done | bytes 327712 | tf_op jit(solution)/shard_map/ppermute | solution.py:320
  36.9 0.4 shard_map.117
  37.3 1.6 %collective-permute-start.11 = (bf16[320,640]{1,0:T(8,128)(2,1)S(1)}, bf16[320,640]{1,0:T(8,128)(2,1)S(1)}, u32[]{:S(2)}, u32[]{:S(2)}) collective-permute-start(bf16[320,640]{1,0:T(8,128)(2,1)S(1)} %get-tuple-element.53), channel_id=1, source_target_pairs={{0,8},{4,20},{8,0},{12,28},{16,24},{20,4},{24,16},{28,12},{1,9},{5... | collective-permute-start | bytes 1228808 | tf_op jit(solution)/shard_map/ppermute | solution.py:317
  38.9 0.8 %shard_map.118 = (f32[256,640]{1,0:T(8,128)S(1)}, bf16[256,640]{1,0:T(8,128)(2,1)S(1)}) custom-call(bf16[320,512]{1,0:T(8,128)(2,1)S(1)} %collective-permute-done.2.refs_5_.refs_0_, bf16[320,512]{1,0:T(8,128)(2,1)S(1)} %collective-permute-done.9.refs_1_.refs_3_, bf16[4,320,640]{2,1,0:T(8,128)(2,1)S(1)} %shard_map.112.refs_0_.refs_4_.refs_2_, ...), custom_call_target="tpu_custom_call" | custom-call | flops 209715200 | bytes 4587520 | tf_op jit(solution)/shard_map/pallas_call | solution.py:25
  39.7 0.1 collective-permute-start.15
  39.8 0.0 collective-permute-done.12.refs_3_
  39.8 0.5 shard_map.120
  40.3 3.6 %collective-permute-start.13 = (bf16[320,512]{1,0:T(8,128)(2,1)S(1)}, bf16[320,512]{1,0:T(8,128)(2,1)S(1)}, u32[]{:S(2)}, u32[]{:S(2)}) collective-permute-start(bf16[320,512]{1,0:T(8,128)(2,1)S(1)} %shard_map.120), channel_id=1, source_target_pairs={{0,1},{1,0},{2,3},{3,2},{4,5},{5,4},{6,7},{7,6},{8,9},{9,8},{10,11... | collective-permute-start | bytes 983048 | tf_op jit(solution)/shard_map/ppermute | solution.py:320
  43.9 0.0 collective-permute-done.10.refs_1_
  43.9 0.4 shard_map.122
  44.3 0.1 collective-permute-start.14
  44.4 0.9 %collective-permute-done.11.refs_3_ = bf16[320,640]{1,0:T(8,128)(2,1)S(1)} collective-permute-done((bf16[320,640]{1,0:T(8,128)(2,1)S(1)}, bf16[320,640]{1,0:T(8,128)(2,1)S(1)}, u32[]{:S(2)}, u32[]{:S(2)}) %collective-permute-start.11) | collective-permute-done | bytes 409632 | tf_op jit(solution)/shard_map/ppermute | solution.py:317
  45.3 0.2 shard_map.121
  45.6 1.7 %collective-permute-start.17 = (bf16[320,640]{1,0:T(8,128)(2,1)S(1)}, bf16[320,640]{1,0:T(8,128)(2,1)S(1)}, u32[]{:S(2)}, u32[]{:S(2)}) collective-permute-start(bf16[320,640]{1,0:T(8,128)(2,1)S(1)} %get-tuple-element.64), channel_id=1, source_target_pairs={{0,16},{4,12},{8,24},{12,4},{16,0},{20,28},{24,8},{28,20},{1,17},{... | collective-permute-start | bytes 1228808 | tf_op jit(solution)/shard_map/ppermute | solution.py:317
  47.3 0.0 collective-permute-done.15.other_ref
  47.3 2.5 %shard_map.123 = (bf16[256,640]{1,0:T(8,128)(2,1)}, bf16[256,640]{1,0:T(8,128)(2,1)}, bf16[256,640]{1,0:T(8,128)(2,1)}) custom-call(bf16[256,640]{1,0:T(8,128)(2,1)S(1)} %copy-done.1, bf16[256,640]{1,0:T(8,128)(2,1)S(1)} %copy-done.2, bf16[256,640]{1,0:T(8,128)(2,1)S(1)} %copy-done.3, f32[5,256,256]{2,1,0:T(8,128)S(1)} %get-tuple-element.62.probs_ref, ...), custom_call_target="tpu_custom_call" | custom-call | flops 419430400 | bytes 4259840 | tf_op jit(solution)/shard_map/pallas_call | solution.py:25
  49.8 0.6 %collective-permute-done.13.refs_3_ = bf16[320,512]{1,0:T(8,128)(2,1)S(1)} collective-permute-done((bf16[320,512]{1,0:T(8,128)(2,1)S(1)}, bf16[320,512]{1,0:T(8,128)(2,1)S(1)}, u32[]{:S(2)}, u32[]{:S(2)}) %collective-permute-start.13) | collective-permute-done | bytes 327712 | tf_op jit(solution)/shard_map/ppermute | solution.py:320
  50.4 0.0 collective-permute-done.14.refs_4_
  50.5 0.5 shard_map.124
  50.9 0.0 copy-start.4
  50.9 0.1 collective-permute-start.16
  51.0 2.6 %collective-permute-done.17.refs_1_ = bf16[320,640]{1,0:T(8,128)(2,1)S(1)} collective-permute-done((bf16[320,640]{1,0:T(8,128)(2,1)S(1)}, bf16[320,640]{1,0:T(8,128)(2,1)S(1)}, u32[]{:S(2)}, u32[]{:S(2)}) %collective-permute-start.17) | collective-permute-done | bytes 409632 | tf_op jit(solution)/shard_map/ppermute | solution.py:317
  53.6 1.0 %shard_map.126 = f32[320,640]{1,0:T(8,128)} custom-call(f32[320,640]{1,0:T(8,128)S(1)} %get-tuple-element.73.refs_0_, bf16[320,640]{1,0:T(8,128)(2,1)S(1)} %collective-permute-done.17.refs_1_), custom_call_target="tpu_custom_call" | custom-call | bytes 2048000 | tf_op jit(solution)/shard_map/pallas_call | solution.py:25
  54.6 0.0 collective-permute-done.16.other_ref
  54.6 0.0 copy-done.4
  54.6 1.0 %shard_map.125 = bf16[256,640]{1,0:T(8,128)(2,1)} custom-call(bf16[256,640]{1,0:T(8,128)(2,1)S(1)} %copy-done.4, f32[320,256]{1,0:T(8,128)S(1)} %get-tuple-element.71.keep_ref, f32[320,256]{1,0:T(8,128)S(1)} %collective-permute-done.16.other_ref), custom_call_target="tpu_custom_call" | custom-call | bytes 1310720 | tf_op jit(solution)/shard_map/pallas_call | solution.py:25
  (4 shorter events, 0.0 us)
Async XLA Ops:
  0.6 9.2 %copy-start = (bf16[640,320]{0,1:T(8,128)(2,1)S(1)}, bf16[640,320]{0,1:T(8,128)(2,1)}, u32[]{:S(2)}) copy-start(bf16[640,320]{0,1:T(8,128)(2,1)} %param.12) | copy-start | bytes 1228804
  0.6 9.1 %collective-permute-start.3 = (bf16[320,640]{1,0:T(8,128)(2,1)}, bf16[320,640]{1,0:T(8,128)(2,1)S(1)}, u32[]{:S(2)}, u32[]{:S(2)}) collective-permute-start(bf16[320,640]{1,0:T(8,128)(2,1)} %bitcast.3), channel_id=1, source_target_pairs={{0,8},{4,20},{8,0},{12,28},{16,24},{20,4},{24,16},{28,12},{1,9},{5... | collective-permute-start | bytes 1228808 | tf_op jit(solution)/shard_map/ppermute | solution.py:317
  3.6 1.8 %collective-permute-start = (bf16[256,640]{1,0:T(8,128)(2,1)}, bf16[256,640]{1,0:T(8,128)(2,1)S(1)}, u32[]{:S(2)}, u32[]{:S(2)}) collective-permute-start(bf16[256,640]{1,0:T(8,128)(2,1)} %own_ref.1), channel_id=1, source_target_pairs={{0,4},{4,0},{8,12},{12,8},{16,20},{20,16},{24,28},{28,24},{1,5},{5... | collective-permute-start | bytes 983048 | tf_op jit(solution)/shard_map/ppermute | solution.py:313
  3.6 8.3 %copy-start.1 = (bf16[256,640]{1,0:T(8,128)(2,1)S(1)}, bf16[256,640]{1,0:T(8,128)(2,1)}, u32[]{:S(2)}) copy-start(bf16[256,640]{1,0:T(8,128)(2,1)} %q_ref.2) | copy-start | bytes 983044
  3.7 8.3 %copy-start.2 = (bf16[256,640]{1,0:T(8,128)(2,1)S(1)}, bf16[256,640]{1,0:T(8,128)(2,1)}, u32[]{:S(2)}) copy-start(bf16[256,640]{1,0:T(8,128)(2,1)} %k_ref.3) | copy-start | bytes 983044
  3.7 8.3 %copy-start.3 = (bf16[256,640]{1,0:T(8,128)(2,1)S(1)}, bf16[256,640]{1,0:T(8,128)(2,1)}, u32[]{:S(2)}) copy-start(bf16[256,640]{1,0:T(8,128)(2,1)} %v_ref.3) | copy-start | bytes 983044
  5.5 1.0 %copy-start.5 = (bf16[256,640]{1,0:T(8,128)(2,1)S(1)}, bf16[256,640]{1,0:T(8,128)(2,1)}, u32[]{:S(2)}) copy-start(bf16[256,640]{1,0:T(8,128)(2,1)} %own_ref.1) | copy-start | bytes 983044
  6.5 5.5 %copy-start.6 = (s32[1,256]{1,0:T(1,128)S(1)}, s32[1,256]{1,0:T(1,128)}, u32[]{:S(2)}) copy-start(s32[1,256]{1,0:T(1,128)} %seg_ref.1) | copy-start | bytes 3076
  6.7 9.8 %collective-permute-start.1 = (bf16[320,512]{1,0:T(8,128)(2,1)S(1)}, bf16[320,512]{1,0:T(8,128)(2,1)S(1)}, u32[]{:S(2)}, u32[]{:S(2)}) collective-permute-start(bf16[320,512]{1,0:T(8,128)(2,1)S(1)} %shard_map.110.refs_0_), channel_id=1, source_target_pairs={{0,1},{1,0},{2,3},{3,2},{4,5},{5,4},{6,7},{7,6},{8,9},{9,8},{10,11... | collective-permute-start | bytes 983048 | tf_op jit(solution)/shard_map/ppermute | solution.py:320
  8.4 8.2 %collective-permute-start.2 = (bf16[320,512]{1,0:T(8,128)(2,1)S(1)}, bf16[320,512]{1,0:T(8,128)(2,1)S(1)}, u32[]{:S(2)}, u32[]{:S(2)}) collective-permute-start(bf16[320,512]{1,0:T(8,128)(2,1)S(1)} %shard_map.110.refs_0_), channel_id=1, source_target_pairs={{1,2},{2,1},{0,4},{3,7},{5,6},{6,5},{4,0},{7,3},{9,10},{10,9},{8,1... | collective-permute-start | bytes 983048 | tf_op jit(solution)/shard_map/ppermute | solution.py:327
  9.9 8.2 %collective-permute-start.4 = (bf16[320,640]{1,0:T(8,128)(2,1)S(1)}, bf16[320,640]{1,0:T(8,128)(2,1)S(1)}, u32[]{:S(2)}, u32[]{:S(2)}) collective-permute-start(bf16[320,640]{1,0:T(8,128)(2,1)S(1)} %get-tuple-element.78), channel_id=1, source_target_pairs={{0,16},{4,12},{8,24},{12,4},{16,0},{20,28},{24,8},{28,20},{1,17},{... | collective-permute-start | bytes 1228808 | tf_op jit(solution)/shard_map/ppermute | solution.py:317
  16.5 1.6 %collective-permute-start.6 = (bf16[256,640]{1,0:T(8,128)(2,1)S(1)}, bf16[256,640]{1,0:T(8,128)(2,1)S(1)}, u32[]{:S(2)}, u32[]{:S(2)}) collective-permute-start(bf16[256,640]{1,0:T(8,128)(2,1)S(1)} %get-tuple-element.45.refs_1_.refs_3_.refs_4_.refs_2_), channel_id=1, source_target_pairs={{0,4},{4,0},{8,12},{12,8},{16,20},{20,16},{24,28},{28,24},{1,5},{5... | collective-permute-start | bytes 983048 | tf_op jit(solution)/shard_map/ppermute | solution.py:313
  16.5 8.0 %collective-permute-start.5 = (bf16[320,640]{1,0:T(8,128)(2,1)S(1)}, bf16[320,640]{1,0:T(8,128)(2,1)S(1)}, u32[]{:S(2)}, u32[]{:S(2)}) collective-permute-start(bf16[320,640]{1,0:T(8,128)(2,1)S(1)} %get-tuple-element.77), channel_id=1, source_target_pairs={{0,16},{4,12},{8,24},{12,4},{16,0},{20,28},{24,8},{28,20},{1,17},{... | collective-permute-start | bytes 1228808 | tf_op jit(solution)/shard_map/ppermute | solution.py:317
  18.1 6.6 %collective-permute-start.7 = (bf16[320,512]{1,0:T(8,128)(2,1)S(1)}, bf16[320,512]{1,0:T(8,128)(2,1)S(1)}, u32[]{:S(2)}, u32[]{:S(2)}) collective-permute-start(bf16[320,512]{1,0:T(8,128)(2,1)S(1)} %collective-permute-done.1.refs_1_), channel_id=1, source_target_pairs={{1,2},{2,1},{0,4},{3,7},{5,6},{6,5},{4,0},{7,3},{9,10},{10,9},{8,1... | collective-permute-start | bytes 983048 | tf_op jit(solution)/shard_map/ppermute | solution.py:327
  18.6 11.5 %collective-permute-start.8 = (bf16[320,512]{1,0:T(8,128)(2,1)S(1)}, bf16[320,512]{1,0:T(8,128)(2,1)S(1)}, u32[]{:S(2)}, u32[]{:S(2)}) collective-permute-start(bf16[320,512]{1,0:T(8,128)(2,1)S(1)} %shard_map.114), channel_id=1, source_target_pairs={{0,1},{1,0},{2,3},{3,2},{4,5},{5,4},{6,7},{7,6},{8,9},{9,8},{10,11... | collective-permute-start | bytes 983048 | tf_op jit(solution)/shard_map/ppermute | solution.py:320
  25.1 11.8 %collective-permute-start.9 = (bf16[320,512]{1,0:T(8,128)(2,1)S(1)}, bf16[320,512]{1,0:T(8,128)(2,1)S(1)}, u32[]{:S(2)}, u32[]{:S(2)}) collective-permute-start(bf16[320,512]{1,0:T(8,128)(2,1)S(1)} %shard_map.113), channel_id=1, source_target_pairs={{0,1},{1,0},{2,3},{3,2},{4,5},{5,4},{6,7},{7,6},{8,9},{9,8},{10,11... | collective-permute-start | bytes 983048 | tf_op jit(solution)/shard_map/ppermute | solution.py:320
  31.7 12.2 %collective-permute-start.10 = (bf16[320,640]{1,0:T(8,128)(2,1)S(1)}, bf16[320,640]{1,0:T(8,128)(2,1)S(1)}, u32[]{:S(2)}, u32[]{:S(2)}) collective-permute-start(bf16[320,640]{1,0:T(8,128)(2,1)S(1)} %get-tuple-element.56), channel_id=1, source_target_pairs={{0,8},{4,20},{8,0},{12,28},{16,24},{20,4},{24,16},{28,12},{1,9},{5... | collective-permute-start | bytes 1228808 | tf_op jit(solution)/shard_map/ppermute | solution.py:317
  33.3 6.5 %collective-permute-start.12 = (bf16[320,512]{1,0:T(8,128)(2,1)S(1)}, bf16[320,512]{1,0:T(8,128)(2,1)S(1)}, u32[]{:S(2)}, u32[]{:S(2)}) collective-permute-start(bf16[320,512]{1,0:T(8,128)(2,1)S(1)} %shard_map.119), channel_id=1, source_target_pairs={{1,2},{2,1},{0,4},{3,7},{5,6},{6,5},{4,0},{7,3},{9,10},{10,9},{8,1... | collective-permute-start | bytes 983048 | tf_op jit(solution)/shard_map/ppermute | solution.py:327
  37.3 8.0 %collective-permute-start.11 = (bf16[320,640]{1,0:T(8,128)(2,1)S(1)}, bf16[320,640]{1,0:T(8,128)(2,1)S(1)}, u32[]{:S(2)}, u32[]{:S(2)}) collective-permute-start(bf16[320,640]{1,0:T(8,128)(2,1)S(1)} %get-tuple-element.53), channel_id=1, source_target_pairs={{0,8},{4,20},{8,0},{12,28},{16,24},{20,4},{24,16},{28,12},{1,9},{5... | collective-permute-start | bytes 1228808 | tf_op jit(solution)/shard_map/ppermute | solution.py:317
  39.7 7.6 %collective-permute-start.15 = (bf16[256,640]{1,0:T(8,128)(2,1)S(1)}, bf16[256,640]{1,0:T(8,128)(2,1)S(1)}, u32[]{:S(2)}, u32[]{:S(2)}) collective-permute-start(bf16[256,640]{1,0:T(8,128)(2,1)S(1)} %get-tuple-element.66), channel_id=1, source_target_pairs={{0,4},{4,0},{8,12},{12,8},{16,20},{20,16},{24,28},{28,24},{1,5},{5... | collective-permute-start | bytes 983048 | tf_op jit(solution)/shard_map/ppermute | solution.py:313
  40.3 10.2 %collective-permute-start.13 = (bf16[320,512]{1,0:T(8,128)(2,1)S(1)}, bf16[320,512]{1,0:T(8,128)(2,1)S(1)}, u32[]{:S(2)}, u32[]{:S(2)}) collective-permute-start(bf16[320,512]{1,0:T(8,128)(2,1)S(1)} %shard_map.120), channel_id=1, source_target_pairs={{0,1},{1,0},{2,3},{3,2},{4,5},{5,4},{6,7},{7,6},{8,9},{9,8},{10,11... | collective-permute-start | bytes 983048 | tf_op jit(solution)/shard_map/ppermute | solution.py:320
  44.3 6.1 %collective-permute-start.14 = (bf16[320,512]{1,0:T(8,128)(2,1)S(1)}, bf16[320,512]{1,0:T(8,128)(2,1)S(1)}, u32[]{:S(2)}, u32[]{:S(2)}) collective-permute-start(bf16[320,512]{1,0:T(8,128)(2,1)S(1)} %shard_map.122), channel_id=1, source_target_pairs={{1,2},{2,1},{0,4},{3,7},{5,6},{6,5},{4,0},{7,3},{9,10},{10,9},{8,1... | collective-permute-start | bytes 983048 | tf_op jit(solution)/shard_map/ppermute | solution.py:327
  45.6 8.0 %collective-permute-start.17 = (bf16[320,640]{1,0:T(8,128)(2,1)S(1)}, bf16[320,640]{1,0:T(8,128)(2,1)S(1)}, u32[]{:S(2)}, u32[]{:S(2)}) collective-permute-start(bf16[320,640]{1,0:T(8,128)(2,1)S(1)} %get-tuple-element.64), channel_id=1, source_target_pairs={{0,16},{4,12},{8,24},{12,4},{16,0},{20,28},{24,8},{28,20},{1,17},{... | collective-permute-start | bytes 1228808 | tf_op jit(solution)/shard_map/ppermute | solution.py:317
  50.9 3.6 %copy-start.4 = (bf16[256,640]{1,0:T(8,128)(2,1)S(1)}, bf16[256,640]{1,0:T(8,128)(2,1)}, u32[]{:S(2)}) copy-start(bf16[256,640]{1,0:T(8,128)(2,1)} %residual_ref.1) | copy-start | bytes 983044
  50.9 3.6 %collective-permute-start.16 = (f32[320,256]{1,0:T(8,128)S(1)}, f32[320,256]{1,0:T(8,128)S(1)}, u32[]{:S(2)}, u32[]{:S(2)}) collective-permute-start(f32[320,256]{1,0:T(8,128)S(1)} %get-tuple-element.72), channel_id=1, source_target_pairs={{0,4},{4,0},{8,12},{12,8},{16,20},{20,16},{24,28},{28,24},{1,5},{5... | collective-permute-start | bytes 983048 | tf_op jit(solution)/shard_map/ppermute | solution.py:313

commit v4 on v3

--- a/solution.py
+++ b/solution.py
@@ -253,7 +253,8 @@
 
 
 def weight_early_kernel(group, *refs):
-    *unit_refs, own_ref, other_ref, send, keep, rest = refs
+    *unit_refs, own_ref, other_ref, send_a, send_b, keep, rest = refs
+    rows = send_a.shape[0]
     late, first = late_slot(group), own_bits()[0]
 
     def body(plane, unit_ref):
@@ -264,7 +265,8 @@
             rest[...] = part
 
         def into_send():
-            send[...] = part.astype(BF16)
+            send_a[...] = part[:rows].astype(BF16)
+            send_b[...] = part[rows:].astype(BF16)
 
         def into_keep():
             keep[...] = part
@@ -289,13 +291,15 @@
     late_plane(inner_ref, outer_ref, body)
 
 
-def half_sum_kernel(group, early_keep, early_from, late_keep, late_from, send, left):
+def half_sum_kernel(group, early_keep, early_from_a, early_from_b, late_keep, late_from, send, left):
+    rows = early_from_a.shape[0]
     second = own_bits()[1]
     goes = (late_slot(group) & second) == second
-    early_sum = early_keep[...] + early_from[...].astype(F32)
-    late_sum = late_keep[...] + late_from[...].astype(F32)
-    send[...] = jnp.where(goes, late_sum, early_sum).astype(BF16)
-    left[...] = jnp.where(goes, early_sum, late_sum)
+    for at, early_from in ((pl.ds(0, rows), early_from_a), (pl.ds(rows, rows), early_from_b)):
+        early_sum = early_keep[at] + early_from[...].astype(F32)
+        late_sum = late_keep[at] + late_from[at].astype(F32)
+        send[at] = jnp.where(goes, late_sum, early_sum).astype(BF16)
+        left[at] = jnp.where(goes, early_sum, late_sum)
 
 
 def grad_sum_kernel(scale, left_ref, from_ref, out_ref):
@@ -406,15 +410,16 @@
         mid_three = mid_swap(out)
         block, rest = shape(half, width), shape(half, width, dtype=F32)
         ready = (unit, near, pair_two, inner_next)
-        early_send, early_keep, early_rest = call(
+        piece = shape(half // 2, width)
+        early_send_a, early_send_b, early_keep, early_rest = call(
             bound(weight_early_kernel, group),
-            (block, rest, rest),
+            (piece, piece, rest, rest),
             *ready,
             ctx,
             ctx_other,
             flops=3 * unit_flops,
         )
-        early_from = core_swap(early_send, True)
+        early_from_a, early_from_b = core_swap(early_send_a, True), core_swap(early_send_b, True)
         d_ctx_early = call(
             bound(d_context_early_kernel, group),
             (shape(2 * count, width, dtype=F32),),
@@ -435,7 +440,17 @@
             flops=unit_flops,
         )
         late_from = core_swap(late_send, True)
-        d_ctx_early, late_send = together(d_ctx_early, late_send)
+        mid_three, late_send = together(mid_three, late_send)
+        out = call(
+            bound(message_kernel, 1, group), (message,), *sources, mid_three, flops=unit_flops
+        )[0]
+        pair_four = pair_swap(out)
+        pair_three, early_from_a, early_from_b, out = together(pair_three, early_from_a, early_from_b, out)
+        out = call(
+            bound(message_kernel, 3, group), (message,), *sources, pair_three, flops=unit_flops
+        )[0]
+        mid_four = mid_swap(out)
+        d_ctx_early, out = together(d_ctx_early, out)
         mine, send = call(
             bound(d_context_late_kernel, group),
             (shape(count, width, dtype=F32), shape(count, width)),
@@ -446,22 +461,23 @@
             flops=unit_flops,
         )
         d_ctx_other = swap(send, 1)
-        mine, pair_three, early_from = together(mine, pair_three, early_from)
-        out = call(
-            bound(message_kernel, 3, group), (message,), *sources, pair_three, flops=unit_flops
-        )[0]
-        mid_four = mid_swap(out)
-        out = call(
-            bound(message_kernel, 1, group), (message,), *sources, mid_three, flops=unit_flops
-        )[0]
-        pair_four = pair_swap(out)
         late_from, out = together(late_from, out)
         send, left = call(
-            bound(half_sum_kernel, group), (block, rest), early_keep, early_from, late_keep, late_from
+            bound(half_sum_kernel, group), (block, rest), early_keep, early_from_a, early_from_b, late_keep, late_from
         )
         second_from = core_swap(send, False)
 
-        mine, send = together(mine, send)
+        pair_four, mid_four = together(pair_four, mid_four)
+        keep, send = call(
+            bound(last_project_kernel, group),
+            (shape(half, count, dtype=F32),) * 2,
+            *sources,
+            pair_four,
+            mid_four,
+            flops=unit_flops,
+        )
+        last_other = swap(send, 1)
+        mine, keep = together(mine, keep)
         d_queries, d_keys, d_values = call(
             backward_kernel,
             (shape(count, width),) * 3,
@@ -473,24 +489,14 @@
             d_ctx_other,
             flops=10 * count * count * width,
         )
-        pair_four, mid_four, d_queries = together(pair_four, mid_four, d_queries)
-        keep, send = call(
-            bound(last_project_kernel, group),
-            (shape(half, count, dtype=F32),) * 2,
-            *sources,
-            pair_four,
-            mid_four,
-            flops=unit_flops,
-        )
-        last_other = swap(send, 1)
-        left, keep = together(left, keep)
+        layer_out = make_layer_out(residual, keep, last_other, strips)
+        left, layer_out = together(left, layer_out)
         total = call(
             bound(grad_sum_kernel, 1.0 / math.sqrt(count * blk)),
             (shape(half, width, dtype=F32),),
             left,
             second_from,
         )[0]
-        layer_out = make_layer_out(residual, keep, last_other, strips)
         bit = strips // 2
         while bit >= 1:
             lower, upper = jnp.split(total, 2, axis=0)

time: 55.7 us -> 54.7 us (0.982)
    ppermute x4, starting transfers between devices: 14.2 us -> 12.5 us  [pair_swap(): return lax.ppermute(value, 'shard', [(0, 1), (1, 0), (2, 3), (3, 2)])]
    ppermute x4, waiting for transfers between devices: 5.84 us -> 4.28 us  [pair_swap(): return lax.ppermute(value, 'shard', [(0, 1), (1, 0), (2, 3), (3, 2)])]
    ppermute x6 -> x7, starting transfers between devices: 11.2 us -> 12.1 us  [core_swap(): lax.ppermute(value, 'blk', [(i, i ^ group * bits[i % 2]) for i in range(b...]
    ppermute x4, waiting for transfers between devices: 1.93 us -> 2.51 us  [swap(): return lax.ppermute(value, 'blk', [(i, i ^ bit) for i in range(blk)])]
    ppermute x6 -> x7, waiting for transfers between devices: 6.8 us -> 7.36 us  [core_swap(): lax.ppermute(value, 'blk', [(i, i ^ group * bits[i % 2]) for i in range(b...]
  transfers between devices with their start and end apart: 18 -> 19, of which waited for: 9 -> 9; matrix products, arithmetic and copies ran while one was open for 0% -> 0% of each run, Pallas kernels for 22% -> 22%
where the time goes in v4:
time: 54.7 us; the launch traced here: 54.5 us
  starting transfers between devices  25.3 us (46%)
  waiting for transfers between devices  14.2 us (26%)
  Pallas kernels  13.2 us (24%)
  local copies, waits for them, and re-layouts  1 us (2%)
  between operations  0.82 us (1%)
    pallas_call x17, Pallas kernels, call(): pl.pallas_call(kernel, out_shape=tuple(outs), in_specs=[pl.BlockSpec(memo...  13.2 us
    ppermute x4, starting transfers between devices, pair_swap(): return lax.ppermute(value, 'shard', [(0, 1), (1, 0), (2, 3), (3, 2)])  12.5 us
    ppermute x7, starting transfers between devices, core_swap(): lax.ppermute(value, 'blk', [(i, i ^ group * bits[i % 2]) for i in range(b...  12.1 us
    ppermute x7, waiting for transfers between devices, core_swap(): lax.ppermute(value, 'blk', [(i, i ^ group * bits[i % 2]) for i in range(b...  7.36 us
    ppermute x4, waiting for transfers between devices, pair_swap(): return lax.ppermute(value, 'shard', [(0, 1), (1, 0), (2, 3), (3, 2)])  4.28 us
    ppermute x4, waiting for transfers between devices, swap(): return lax.ppermute(value, 'blk', [(i, i ^ bit) for i in range(blk)])  2.51 us
  transfers between devices with their start and end apart: 19, of which 9 were waited for; matrix products, arithmetic and copies ran while one was open for 0% of the time, Pallas kernels for 22%

profile of v4, /device:TPU:0, one launch (start us, length us, event | category | flops | bytes accessed | tf_op | source)
XLA Modules:
  0.0 54.5 jit_solution(13068819529066452885)
XLA Ops:
  0.6 0.0 copy-start
  0.6 3.0 %collective-permute-start.3 = (bf16[320,640]{1,0:T(8,128)(2,1)}, bf16[320,640]{1,0:T(8,128)(2,1)S(1)}, u32[]{:S(2)}, u32[]{:S(2)}) collective-permute-start(bf16[320,640]{1,0:T(8,128)(2,1)} %bitcast.3), channel_id=1, source_target_pairs={{0,8},{4,20},{8,0},{12,28},{16,24},{20,4},{24,16},{28,12},{1,9},{5... | collective-permute-start | bytes 1228808 | tf_op jit(solution)/shard_map/ppermute | solution.py:321
  3.6 0.0 collective-permute-start
  3.7 1.8 %collective-permute-done.other_ref = bf16[256,640]{1,0:T(8,128)(2,1)S(1)} collective-permute-done((bf16[256,640]{1,0:T(8,128)(2,1)}, bf16[256,640]{1,0:T(8,128)(2,1)S(1)}, u32[]{:S(2)}, u32[]{:S(2)}) %collective-permute-start) | collective-permute-done | bytes 327712 | tf_op jit(solution)/shard_map/ppermute | solution.py:317
  5.5 1.0 %copy-done.5 = bf16[256,640]{1,0:T(8,128)(2,1)S(1)} copy-done((bf16[256,640]{1,0:T(8,128)(2,1)S(1)}, bf16[256,640]{1,0:T(8,128)(2,1)}, u32[]{:S(2)}) %copy-start.5) | copy-done | bytes 327704
  6.5 0.2 shard_map.110.refs_0_
  6.7 1.6 %collective-permute-start.1 = (bf16[320,512]{1,0:T(8,128)(2,1)S(1)}, bf16[320,512]{1,0:T(8,128)(2,1)S(1)}, u32[]{:S(2)}, u32[]{:S(2)}) collective-permute-start(bf16[320,512]{1,0:T(8,128)(2,1)S(1)} %shard_map.110.refs_0_), channel_id=1, source_target_pairs={{0,1},{1,0},{2,3},{3,2},{4,5},{5,4},{6,7},{7,6},{8,9},{9,8},{10,11... | collective-permute-start | bytes 983048 | tf_op jit(solution)/shard_map/ppermute | solution.py:324
  8.4 0.0 collective-permute-start.2
  8.4 1.4 %collective-permute-done.3.refs_1_ = bf16[320,640]{1,0:T(8,128)(2,1)S(1)} collective-permute-done((bf16[320,640]{1,0:T(8,128)(2,1)}, bf16[320,640]{1,0:T(8,128)(2,1)S(1)}, u32[]{:S(2)}, u32[]{:S(2)}) %collective-permute-start.3) | collective-permute-done | bytes 409632 | tf_op jit(solution)/shard_map/ppermute | solution.py:321
  9.8 0.0 copy-done
  9.8 0.1 broadcast_select_fusion
  9.9 2.1 %collective-permute-start.4 = (bf16[320,640]{1,0:T(8,128)(2,1)S(1)}, bf16[320,640]{1,0:T(8,128)(2,1)S(1)}, u32[]{:S(2)}, u32[]{:S(2)}) collective-permute-start(bf16[320,640]{1,0:T(8,128)(2,1)S(1)} %get-tuple-element.80), channel_id=1, source_target_pairs={{0,16},{4,12},{8,24},{12,4},{16,0},{20,28},{24,8},{28,20},{1,17},{... | collective-permute-start | bytes 1228808 | tf_op jit(solution)/shard_map/ppermute | solution.py:321
  12.0 0.0 copy-done.1
  12.0 0.0 copy-done.2
  12.0 0.0 copy-done.3
  12.0 0.0 copy-done.6
  12.0 1.3 %shard_map.111 = (bf16[256,640]{1,0:T(8,128)(2,1)S(1)}, f32[5,256,256]{2,1,0:T(8,128)S(1)}) custom-call(bf16[256,640]{1,0:T(8,128)(2,1)S(1)} %copy-done.1, bf16[256,640]{1,0:T(8,128)(2,1)S(1)} %copy-done.2, bf16[256,640]{1,0:T(8,128)(2,1)S(1)} %copy-done.3, s32[1,256]{1,0:T(1,128)S(1)} %copy-done.6), custom_call_target="tpu_custom_call" | custom-call | flops 167772160 | bytes 2622464 | tf_op jit(solution)/shard_map/pallas_call | solution.py:25
  13.3 3.3 %collective-permute-done.1.refs_1_ = bf16[320,512]{1,0:T(8,128)(2,1)S(1)} collective-permute-done((bf16[320,512]{1,0:T(8,128)(2,1)S(1)}, bf16[320,512]{1,0:T(8,128)(2,1)S(1)}, u32[]{:S(2)}, u32[]{:S(2)}) %collective-permute-start.1) | collective-permute-done | bytes 327712 | tf_op jit(solution)/shard_map/ppermute | solution.py:324
  16.5 0.0 collective-permute-done.2.refs_5_.refs_0_
  16.5 0.0 collective-permute-start.6
  16.5 1.5 %collective-permute-start.5 = (bf16[320,640]{1,0:T(8,128)(2,1)S(1)}, bf16[320,640]{1,0:T(8,128)(2,1)S(1)}, u32[]{:S(2)}, u32[]{:S(2)}) collective-permute-start(bf16[320,640]{1,0:T(8,128)(2,1)S(1)} %get-tuple-element.79), channel_id=1, source_target_pairs={{0,16},{4,12},{8,24},{12,4},{16,0},{20,28},{24,8},{28,20},{1,17},{... | collective-permute-start | bytes 1228808 | tf_op jit(solution)/shard_map/ppermute | solution.py:321
  18.1 0.0 collective-permute-start.7
  18.1 0.0 collective-permute-done.4.refs_2_
  18.1 0.1 collective-permute-done.6.refs_2_.refs_4_.refs_5_.refs_3_
  18.2 0.4 shard_map.114
  18.6 4.0 %collective-permute-start.8 = (bf16[320,512]{1,0:T(8,128)(2,1)S(1)}, bf16[320,512]{1,0:T(8,128)(2,1)S(1)}, u32[]{:S(2)}, u32[]{:S(2)}) collective-permute-start(bf16[320,512]{1,0:T(8,128)(2,1)S(1)} %shard_map.114), channel_id=1, source_target_pairs={{0,1},{1,0},{2,3},{3,2},{4,5},{5,4},{6,7},{7,6},{8,9},{9,8},{10,11... | collective-permute-start | bytes 983048 | tf_op jit(solution)/shard_map/ppermute | solution.py:324
  22.6 1.9 %collective-permute-done.5.refs_3_ = bf16[320,640]{1,0:T(8,128)(2,1)S(1)} collective-permute-done((bf16[320,640]{1,0:T(8,128)(2,1)S(1)}, bf16[320,640]{1,0:T(8,128)(2,1)S(1)}, u32[]{:S(2)}, u32[]{:S(2)}) %collective-permute-start.5) | collective-permute-done | bytes 409632 | tf_op jit(solution)/shard_map/ppermute | solution.py:321
  24.5 0.1 shard_map.112.refs_0_.refs_4_.refs_2_
  24.6 0.0 collective-permute-done.7.refs_3_
  24.6 0.5 shard_map.113
  25.1 5.0 %collective-permute-start.9 = (bf16[320,512]{1,0:T(8,128)(2,1)S(1)}, bf16[320,512]{1,0:T(8,128)(2,1)S(1)}, u32[]{:S(2)}, u32[]{:S(2)}) collective-permute-start(bf16[320,512]{1,0:T(8,128)(2,1)S(1)} %shard_map.113), channel_id=1, source_target_pairs={{0,1},{1,0},{2,3},{3,2},{4,5},{5,4},{6,7},{7,6},{8,9},{9,8},{10,11... | collective-permute-start | bytes 983048 | tf_op jit(solution)/shard_map/ppermute | solution.py:324
  30.1 0.0 collective-permute-done.8.refs_2_.refs_3_
  30.1 0.4 shard_map.117
  30.6 0.1 collective-permute-start.12
  30.7 1.6 %shard_map.115 = (bf16[160,640]{1,0:T(8,128)(2,1)S(1)}, bf16[160,640]{1,0:T(8,128)(2,1)S(1)}, f32[320,640]{1,0:T(8,128)S(1)}, f32[320,640]{1,0:T(8,128)S(1)}) custom-call(bf16[320,512]{1,0:T(8,128)(2,1)S(1)} %shard_map.110.refs_0_, bf16[320,512]{1,0:T(8,128)(2,1)S(1)} %collective-permute-done.1.refs_1_, ...), custom_call_target="tpu_custom_call" | custom-call | flops 629145600 | bytes 4014080 | tf_op jit(solution)/shard_map/pallas_call | solution.py:25
  32.2 1.1 %collective-permute-start.10 = (bf16[160,640]{1,0:T(8,128)(2,1)S(1)}, bf16[160,640]{1,0:T(8,128)(2,1)S(1)}, u32[]{:S(2)}, u32[]{:S(2)}) collective-permute-start(bf16[160,640]{1,0:T(8,128)(2,1)S(1)} %get-tuple-element.52), channel_id=1, source_target_pairs={{0,8},{4,20},{8,0},{12,28},{16,24},{20,4},{24,16},{28,12},{1,9},{5... | collective-permute-start | bytes 614408 | tf_op jit(solution)/shard_map/ppermute | solution.py:321
  33.4 0.9 %collective-permute-start.11 = (bf16[160,640]{1,0:T(8,128)(2,1)S(1)}, bf16[160,640]{1,0:T(8,128)(2,1)S(1)}, u32[]{:S(2)}, u32[]{:S(2)}) collective-permute-start(bf16[160,640]{1,0:T(8,128)(2,1)S(1)} %get-tuple-element.53), channel_id=1, source_target_pairs={{0,8},{4,20},{8,0},{12,28},{16,24},{20,4},{24,16},{28,12},{1,9},{5... | collective-permute-start | bytes 614408 | tf_op jit(solution)/shard_map/ppermute | solution.py:321
  34.3 1.5 %shard_map.116.refs_3_ = f32[512,640]{1,0:T(8,128)S(1)} custom-call(bf16[320,512]{1,0:T(8,128)(2,1)S(1)} %shard_map.110.refs_0_, bf16[320,512]{1,0:T(8,128)(2,1)S(1)} %collective-permute-done.1.refs_1_, bf16[320,512]{1,0:T(8,128)(2,1)S(1)} %collective-permute-done.8.refs_2_.refs_3_, bf16[320,512]{1,0:T(8,128)(2,1)S(1)} %collective-permute-done.7.refs_3_, ...), custom_call_target="tpu_custom_call" | custom-call | flops 629145600 | bytes 4259840 | tf_op jit(solution)/shard_map/pallas_call | solution.py:25
  35.9 1.0 %collective-permute-done.9.refs_1_.refs_3_ = bf16[320,512]{1,0:T(8,128)(2,1)S(1)} collective-permute-done((bf16[320,512]{1,0:T(8,128)(2,1)S(1)}, bf16[320,512]{1,0:T(8,128)(2,1)S(1)}, u32[]{:S(2)}, u32[]{:S(2)}) %collective-permute-start.9) | collective-permute-done | bytes 327712 | tf_op jit(solution)/shard_map/ppermute | solution.py:324
  36.9 0.4 shard_map.118
  37.3 1.6 %collective-permute-start.13 = (bf16[320,640]{1,0:T(8,128)(2,1)S(1)}, bf16[320,640]{1,0:T(8,128)(2,1)S(1)}, u32[]{:S(2)}, u32[]{:S(2)}) collective-permute-start(bf16[320,640]{1,0:T(8,128)(2,1)S(1)} %get-tuple-element.55), channel_id=1, source_target_pairs={{0,8},{4,20},{8,0},{12,28},{16,24},{20,4},{24,16},{28,12},{1,9},{5... | collective-permute-start | bytes 1228808 | tf_op jit(solution)/shard_map/ppermute | solution.py:321
  38.9 0.0 collective-permute-done.12.refs_3_
  39.0 0.5 shard_map.119
  39.4 1.8 %collective-permute-start.14 = (bf16[320,512]{1,0:T(8,128)(2,1)S(1)}, bf16[320,512]{1,0:T(8,128)(2,1)S(1)}, u32[]{:S(2)}, u32[]{:S(2)}) collective-permute-start(bf16[320,512]{1,0:T(8,128)(2,1)S(1)} %shard_map.119), channel_id=1, source_target_pairs={{0,1},{1,0},{2,3},{3,2},{4,5},{5,4},{6,7},{7,6},{8,9},{9,8},{10,11... | collective-permute-start | bytes 983048 | tf_op jit(solution)/shard_map/ppermute | solution.py:324
  41.2 0.0 collective-permute-done.10.refs_1_
  41.2 0.0 collective-permute-done.11.refs_2_
  41.2 0.5 shard_map.121
  41.7 0.1 collective-permute-start.15
  41.8 3.6 %collective-permute-done.13.refs_4_ = bf16[320,640]{1,0:T(8,128)(2,1)S(1)} collective-permute-done((bf16[320,640]{1,0:T(8,128)(2,1)S(1)}, bf16[320,640]{1,0:T(8,128)(2,1)S(1)}, u32[]{:S(2)}, u32[]{:S(2)}) %collective-permute-start.13) | collective-permute-done | bytes 409632 | tf_op jit(solution)/shard_map/ppermute | solution.py:321
  45.3 0.2 shard_map.120
  45.6 1.7 %collective-permute-start.17 = (bf16[320,640]{1,0:T(8,128)(2,1)S(1)}, bf16[320,640]{1,0:T(8,128)(2,1)S(1)}, u32[]{:S(2)}, u32[]{:S(2)}) collective-permute-start(bf16[320,640]{1,0:T(8,128)(2,1)S(1)} %get-tuple-element.72), channel_id=1, source_target_pairs={{0,16},{4,12},{8,24},{12,4},{16,0},{20,28},{24,8},{28,20},{1,17},{... | collective-permute-start | bytes 1228808 | tf_op jit(solution)/shard_map/ppermute | solution.py:321
  47.3 0.6 %shard_map.122 = (f32[256,640]{1,0:T(8,128)S(1)}, bf16[256,640]{1,0:T(8,128)(2,1)S(1)}) custom-call(bf16[320,512]{1,0:T(8,128)(2,1)S(1)} %collective-permute-done.2.refs_5_.refs_0_, bf16[320,512]{1,0:T(8,128)(2,1)S(1)} %collective-permute-done.9.refs_1_.refs_3_, bf16[4,320,640]{2,1,0:T(8,128)(2,1)S(1)} %shard_map.112.refs_0_.refs_4_.refs_2_, ...), custom_call_target="tpu_custom_call" | custom-call | flops 209715200 | bytes 4587520 | tf_op jit(solution)/shard_map/pallas_call | solution.py:25
  47.9 0.1 collective-permute-start.18
  48.0 0.0 collective-permute-done.14.refs_3_
  48.0 0.0 collective-permute-done.15.refs_4_
  48.0 0.5 shard_map.123
  48.4 0.5 %collective-permute-start.16 = (f32[320,256]{1,0:T(8,128)S(1)}, f32[320,256]{1,0:T(8,128)S(1)}, u32[]{:S(2)}, u32[]{:S(2)}) collective-permute-start(f32[320,256]{1,0:T(8,128)S(1)} %get-tuple-element.69), channel_id=1, source_target_pairs={{0,4},{4,0},{8,12},{12,8},{16,20},{20,16},{24,28},{28,24},{1,5},{5... | collective-permute-start | bytes 983048 | tf_op jit(solution)/shard_map/ppermute | solution.py:317
  49.0 0.6 %collective-permute-done.18.other_ref = bf16[256,640]{1,0:T(8,128)(2,1)S(1)} collective-permute-done((bf16[256,640]{1,0:T(8,128)(2,1)S(1)}, bf16[256,640]{1,0:T(8,128)(2,1)S(1)}, u32[]{:S(2)}, u32[]{:S(2)}) %collective-permute-start.18) | collective-permute-done | bytes 327712 | tf_op jit(solution)/shard_map/ppermute | solution.py:317
  49.6 2.5 %shard_map.126 = (bf16[256,640]{1,0:T(8,128)(2,1)}, bf16[256,640]{1,0:T(8,128)(2,1)}, bf16[256,640]{1,0:T(8,128)(2,1)}) custom-call(bf16[256,640]{1,0:T(8,128)(2,1)S(1)} %copy-done.1, bf16[256,640]{1,0:T(8,128)(2,1)S(1)} %copy-done.2, bf16[256,640]{1,0:T(8,128)(2,1)S(1)} %copy-done.3, f32[5,256,256]{2,1,0:T(8,128)S(1)} %get-tuple-element.73.probs_ref, ...), custom_call_target="tpu_custom_call" | custom-call | flops 419430400 | bytes 4259840 | tf_op jit(solution)/shard_map/pallas_call | solution.py:25
  52.1 0.0 collective-permute-done.16.other_ref
  52.1 0.0 copy-done.4
  52.1 1.0 %shard_map.124 = bf16[256,640]{1,0:T(8,128)(2,1)} custom-call(bf16[256,640]{1,0:T(8,128)(2,1)S(1)} %copy-done.4, f32[320,256]{1,0:T(8,128)S(1)} %get-tuple-element.68.keep_ref, f32[320,256]{1,0:T(8,128)S(1)} %collective-permute-done.16.other_ref), custom_call_target="tpu_custom_call" | custom-call | bytes 1310720 | tf_op jit(solution)/shard_map/pallas_call | solution.py:25
  53.1 0.5 collective-permute-done.17.refs_1_
  53.6 1.0 %shard_map.125 = f32[320,640]{1,0:T(8,128)} custom-call(f32[320,640]{1,0:T(8,128)S(1)} %get-tuple-element.71.refs_0_, bf16[320,640]{1,0:T(8,128)(2,1)S(1)} %collective-permute-done.17.refs_1_), custom_call_target="tpu_custom_call" | custom-call | bytes 2048000 | tf_op jit(solution)/shard_map/pallas_call | solution.py:25
  (6 shorter events, 0.0 us)
Async XLA Ops:
  0.6 9.2 %copy-start = (bf16[640,320]{0,1:T(8,128)(2,1)S(1)}, bf16[640,320]{0,1:T(8,128)(2,1)}, u32[]{:S(2)}) copy-start(bf16[640,320]{0,1:T(8,128)(2,1)} %param.12) | copy-start | bytes 1228804
  0.6 9.1 %collective-permute-start.3 = (bf16[320,640]{1,0:T(8,128)(2,1)}, bf16[320,640]{1,0:T(8,128)(2,1)S(1)}, u32[]{:S(2)}, u32[]{:S(2)}) collective-permute-start(bf16[320,640]{1,0:T(8,128)(2,1)} %bitcast.3), channel_id=1, source_target_pairs={{0,8},{4,20},{8,0},{12,28},{16,24},{20,4},{24,16},{28,12},{1,9},{5... | collective-permute-start | bytes 1228808 | tf_op jit(solution)/shard_map/ppermute | solution.py:321
  3.6 1.8 %collective-permute-start = (bf16[256,640]{1,0:T(8,128)(2,1)}, bf16[256,640]{1,0:T(8,128)(2,1)S(1)}, u32[]{:S(2)}, u32[]{:S(2)}) collective-permute-start(bf16[256,640]{1,0:T(8,128)(2,1)} %own_ref.1), channel_id=1, source_target_pairs={{0,4},{4,0},{8,12},{12,8},{16,20},{20,16},{24,28},{28,24},{1,5},{5... | collective-permute-start | bytes 983048 | tf_op jit(solution)/shard_map/ppermute | solution.py:317
  3.6 8.3 %copy-start.1 = (bf16[256,640]{1,0:T(8,128)(2,1)S(1)}, bf16[256,640]{1,0:T(8,128)(2,1)}, u32[]{:S(2)}) copy-start(bf16[256,640]{1,0:T(8,128)(2,1)} %q_ref.2) | copy-start | bytes 983044
  3.7 8.3 %copy-start.2 = (bf16[256,640]{1,0:T(8,128)(2,1)S(1)}, bf16[256,640]{1,0:T(8,128)(2,1)}, u32[]{:S(2)}) copy-start(bf16[256,640]{1,0:T(8,128)(2,1)} %k_ref.3) | copy-start | bytes 983044
  3.7 8.3 %copy-start.3 = (bf16[256,640]{1,0:T(8,128)(2,1)S(1)}, bf16[256,640]{1,0:T(8,128)(2,1)}, u32[]{:S(2)}) copy-start(bf16[256,640]{1,0:T(8,128)(2,1)} %v_ref.3) | copy-start | bytes 983044
  5.5 1.0 %copy-start.5 = (bf16[256,640]{1,0:T(8,128)(2,1)S(1)}, bf16[256,640]{1,0:T(8,128)(2,1)}, u32[]{:S(2)}) copy-start(bf16[256,640]{1,0:T(8,128)(2,1)} %own_ref.1) | copy-start | bytes 983044
  6.5 5.5 %copy-start.6 = (s32[1,256]{1,0:T(1,128)S(1)}, s32[1,256]{1,0:T(1,128)}, u32[]{:S(2)}) copy-start(s32[1,256]{1,0:T(1,128)} %seg_ref.1) | copy-start | bytes 3076
  6.7 9.8 %collective-permute-start.1 = (bf16[320,512]{1,0:T(8,128)(2,1)S(1)}, bf16[320,512]{1,0:T(8,128)(2,1)S(1)}, u32[]{:S(2)}, u32[]{:S(2)}) collective-permute-start(bf16[320,512]{1,0:T(8,128)(2,1)S(1)} %shard_map.110.refs_0_), channel_id=1, source_target_pairs={{0,1},{1,0},{2,3},{3,2},{4,5},{5,4},{6,7},{7,6},{8,9},{9,8},{10,11... | collective-permute-start | bytes 983048 | tf_op jit(solution)/shard_map/ppermute | solution.py:324
  8.4 8.2 %collective-permute-start.2 = (bf16[320,512]{1,0:T(8,128)(2,1)S(1)}, bf16[320,512]{1,0:T(8,128)(2,1)S(1)}, u32[]{:S(2)}, u32[]{:S(2)}) collective-permute-start(bf16[320,512]{1,0:T(8,128)(2,1)S(1)} %shard_map.110.refs_0_), channel_id=1, source_target_pairs={{1,2},{2,1},{0,4},{3,7},{5,6},{6,5},{4,0},{7,3},{9,10},{10,9},{8,1... | collective-permute-start | bytes 983048 | tf_op jit(solution)/shard_map/ppermute | solution.py:331
  9.9 8.2 %collective-permute-start.4 = (bf16[320,640]{1,0:T(8,128)(2,1)S(1)}, bf16[320,640]{1,0:T(8,128)(2,1)S(1)}, u32[]{:S(2)}, u32[]{:S(2)}) collective-permute-start(bf16[320,640]{1,0:T(8,128)(2,1)S(1)} %get-tuple-element.80), channel_id=1, source_target_pairs={{0,16},{4,12},{8,24},{12,4},{16,0},{20,28},{24,8},{28,20},{1,17},{... | collective-permute-start | bytes 1228808 | tf_op jit(solution)/shard_map/ppermute | solution.py:321
  16.5 1.6 %collective-permute-start.6 = (bf16[256,640]{1,0:T(8,128)(2,1)S(1)}, bf16[256,640]{1,0:T(8,128)(2,1)S(1)}, u32[]{:S(2)}, u32[]{:S(2)}) collective-permute-start(bf16[256,640]{1,0:T(8,128)(2,1)S(1)} %get-tuple-element.46.refs_1_.refs_3_.refs_4_.refs_2_), channel_id=1, source_target_pairs={{0,4},{4,0},{8,12},{12,8},{16,20},{20,16},{24,28},{28,24},{1,5},{5... | collective-permute-start | bytes 983048 | tf_op jit(solution)/shard_map/ppermute | solution.py:317
  16.5 8.0 %collective-permute-start.5 = (bf16[320,640]{1,0:T(8,128)(2,1)S(1)}, bf16[320,640]{1,0:T(8,128)(2,1)S(1)}, u32[]{:S(2)}, u32[]{:S(2)}) collective-permute-start(bf16[320,640]{1,0:T(8,128)(2,1)S(1)} %get-tuple-element.79), channel_id=1, source_target_pairs={{0,16},{4,12},{8,24},{12,4},{16,0},{20,28},{24,8},{28,20},{1,17},{... | collective-permute-start | bytes 1228808 | tf_op jit(solution)/shard_map/ppermute | solution.py:321
  18.1 6.6 %collective-permute-start.7 = (bf16[320,512]{1,0:T(8,128)(2,1)S(1)}, bf16[320,512]{1,0:T(8,128)(2,1)S(1)}, u32[]{:S(2)}, u32[]{:S(2)}) collective-permute-start(bf16[320,512]{1,0:T(8,128)(2,1)S(1)} %collective-permute-done.1.refs_1_), channel_id=1, source_target_pairs={{1,2},{2,1},{0,4},{3,7},{5,6},{6,5},{4,0},{7,3},{9,10},{10,9},{8,1... | collective-permute-start | bytes 983048 | tf_op jit(solution)/shard_map/ppermute | solution.py:331
  18.6 11.5 %collective-permute-start.8 = (bf16[320,512]{1,0:T(8,128)(2,1)S(1)}, bf16[320,512]{1,0:T(8,128)(2,1)S(1)}, u32[]{:S(2)}, u32[]{:S(2)}) collective-permute-start(bf16[320,512]{1,0:T(8,128)(2,1)S(1)} %shard_map.114), channel_id=1, source_target_pairs={{0,1},{1,0},{2,3},{3,2},{4,5},{5,4},{6,7},{7,6},{8,9},{9,8},{10,11... | collective-permute-start | bytes 983048 | tf_op jit(solution)/shard_map/ppermute | solution.py:324
  25.1 11.8 %collective-permute-start.9 = (bf16[320,512]{1,0:T(8,128)(2,1)S(1)}, bf16[320,512]{1,0:T(8,128)(2,1)S(1)}, u32[]{:S(2)}, u32[]{:S(2)}) collective-permute-start(bf16[320,512]{1,0:T(8,128)(2,1)S(1)} %shard_map.113), channel_id=1, source_target_pairs={{0,1},{1,0},{2,3},{3,2},{4,5},{5,4},{6,7},{7,6},{8,9},{9,8},{10,11... | collective-permute-start | bytes 983048 | tf_op jit(solution)/shard_map/ppermute | solution.py:324
  30.6 8.4 %collective-permute-start.12 = (bf16[320,512]{1,0:T(8,128)(2,1)S(1)}, bf16[320,512]{1,0:T(8,128)(2,1)S(1)}, u32[]{:S(2)}, u32[]{:S(2)}) collective-permute-start(bf16[320,512]{1,0:T(8,128)(2,1)S(1)} %shard_map.117), channel_id=1, source_target_pairs={{1,2},{2,1},{0,4},{3,7},{5,6},{6,5},{4,0},{7,3},{9,10},{10,9},{8,1... | collective-permute-start | bytes 983048 | tf_op jit(solution)/shard_map/ppermute | solution.py:331
  32.2 9.0 %collective-permute-start.10 = (bf16[160,640]{1,0:T(8,128)(2,1)S(1)}, bf16[160,640]{1,0:T(8,128)(2,1)S(1)}, u32[]{:S(2)}, u32[]{:S(2)}) collective-permute-start(bf16[160,640]{1,0:T(8,128)(2,1)S(1)} %get-tuple-element.52), channel_id=1, source_target_pairs={{0,8},{4,20},{8,0},{12,28},{16,24},{20,4},{24,16},{28,12},{1,9},{5... | collective-permute-start | bytes 614408 | tf_op jit(solution)/shard_map/ppermute | solution.py:321
  33.4 7.8 %collective-permute-start.11 = (bf16[160,640]{1,0:T(8,128)(2,1)S(1)}, bf16[160,640]{1,0:T(8,128)(2,1)S(1)}, u32[]{:S(2)}, u32[]{:S(2)}) collective-permute-start(bf16[160,640]{1,0:T(8,128)(2,1)S(1)} %get-tuple-element.53), channel_id=1, source_target_pairs={{0,8},{4,20},{8,0},{12,28},{16,24},{20,4},{24,16},{28,12},{1,9},{5... | collective-permute-start | bytes 614408 | tf_op jit(solution)/shard_map/ppermute | solution.py:321
  37.3 8.0 %collective-permute-start.13 = (bf16[320,640]{1,0:T(8,128)(2,1)S(1)}, bf16[320,640]{1,0:T(8,128)(2,1)S(1)}, u32[]{:S(2)}, u32[]{:S(2)}) collective-permute-start(bf16[320,640]{1,0:T(8,128)(2,1)S(1)} %get-tuple-element.55), channel_id=1, source_target_pairs={{0,8},{4,20},{8,0},{12,28},{16,24},{20,4},{24,16},{28,12},{1,9},{5... | collective-permute-start | bytes 1228808 | tf_op jit(solution)/shard_map/ppermute | solution.py:321
  39.4 8.6 %collective-permute-start.14 = (bf16[320,512]{1,0:T(8,128)(2,1)S(1)}, bf16[320,512]{1,0:T(8,128)(2,1)S(1)}, u32[]{:S(2)}, u32[]{:S(2)}) collective-permute-start(bf16[320,512]{1,0:T(8,128)(2,1)S(1)} %shard_map.119), channel_id=1, source_target_pairs={{0,1},{1,0},{2,3},{3,2},{4,5},{5,4},{6,7},{7,6},{8,9},{9,8},{10,11... | collective-permute-start | bytes 983048 | tf_op jit(solution)/shard_map/ppermute | solution.py:324
  41.7 6.3 %collective-permute-start.15 = (bf16[320,512]{1,0:T(8,128)(2,1)S(1)}, bf16[320,512]{1,0:T(8,128)(2,1)S(1)}, u32[]{:S(2)}, u32[]{:S(2)}) collective-permute-start(bf16[320,512]{1,0:T(8,128)(2,1)S(1)} %shard_map.121), channel_id=1, source_target_pairs={{1,2},{2,1},{0,4},{3,7},{5,6},{6,5},{4,0},{7,3},{9,10},{10,9},{8,1... | collective-permute-start | bytes 983048 | tf_op jit(solution)/shard_map/ppermute | solution.py:331
  45.6 8.0 %collective-permute-start.17 = (bf16[320,640]{1,0:T(8,128)(2,1)S(1)}, bf16[320,640]{1,0:T(8,128)(2,1)S(1)}, u32[]{:S(2)}, u32[]{:S(2)}) collective-permute-start(bf16[320,640]{1,0:T(8,128)(2,1)S(1)} %get-tuple-element.72), channel_id=1, source_target_pairs={{0,16},{4,12},{8,24},{12,4},{16,0},{20,28},{24,8},{28,20},{1,17},{... | collective-permute-start | bytes 1228808 | tf_op jit(solution)/shard_map/ppermute | solution.py:321
  47.9 1.7 %collective-permute-start.18 = (bf16[256,640]{1,0:T(8,128)(2,1)S(1)}, bf16[256,640]{1,0:T(8,128)(2,1)S(1)}, u32[]{:S(2)}, u32[]{:S(2)}) collective-permute-start(bf16[256,640]{1,0:T(8,128)(2,1)S(1)} %get-tuple-element.75), channel_id=1, source_target_pairs={{0,4},{4,0},{8,12},{12,8},{16,20},{20,16},{24,28},{28,24},{1,5},{5... | collective-permute-start | bytes 983048 | tf_op jit(solution)/shard_map/ppermute | solution.py:317
  48.4 3.7 %collective-permute-start.16 = (f32[320,256]{1,0:T(8,128)S(1)}, f32[320,256]{1,0:T(8,128)S(1)}, u32[]{:S(2)}, u32[]{:S(2)}) collective-permute-start(f32[320,256]{1,0:T(8,128)S(1)} %get-tuple-element.69), channel_id=1, source_target_pairs={{0,4},{4,0},{8,12},{12,8},{16,20},{20,16},{24,28},{28,24},{1,5},{5... | collective-permute-start | bytes 983048 | tf_op jit(solution)/shard_map/ppermute | solution.py:317
  49.6 2.5 %copy-start.4 = (bf16[256,640]{1,0:T(8,128)(2,1)S(1)}, bf16[256,640]{1,0:T(8,128)(2,1)}, u32[]{:S(2)}) copy-start(bf16[256,640]{1,0:T(8,128)(2,1)} %residual_ref.1) | copy-start | bytes 983044

commit v5 on v4

--- a/solution.py
+++ b/solution.py
@@ -51,13 +51,15 @@
     return weights / jnp.sum(weights, axis=-1, keepdims=True)
 
 
-def forward_kernel(q_ref, k_ref, v_ref, seg_ref, ctx_ref, probs_ref):
+def forward_kernel(q_ref, k_ref, v_ref, seg_ref, ctx_ref, low_ref, high_ref, probs_ref):
     allowed = visible_mask(seg_ref)
     for h in range(q_ref.shape[1] // HEAD):
         at = pl.ds(h * HEAD, HEAD)
         probs = head_probs(q_ref[:, at], k_ref[:, at], allowed)
         probs_ref[h] = probs
-        ctx_ref[:, at] = dot(probs.astype(BF16), v_ref[:, at], NN).astype(BF16)
+        ctx = dot(probs.astype(BF16), v_ref[:, at], NN).astype(BF16)
+        ctx_ref[:, at] = ctx
+        low_ref[:, at], high_ref[:, at] = jnp.split(ctx, 2, axis=0)
 
 
 def backward_kernel(q_ref, k_ref, v_ref, probs_ref, mine_ref, other_ref, dq_ref, dk_ref, dv_ref):
@@ -364,9 +366,10 @@
         w_soon = core_swap(jnp.where(far_soon, w_near, w_own), False)
         w_last = core_swap(jnp.where(far_soon, w_own, w_near), False)
         asked, w_near = together(queries, w_near)
-        ctx, probs = call(
+        part = shape(count // 2, width)
+        ctx, low, high, probs = call(
             forward_kernel,
-            (shape(count, width), shape(width // HEAD, count, count, dtype=F32)),
+            (shape(count, width), part, part, shape(width // HEAD, count, count, dtype=F32)),
             asked,
             key_rows,
             values,
@@ -374,7 +377,7 @@
             flops=4 * count * count * width,
         )
         near, inner_far, ctx = together(near, inner_far, ctx)
-        ctx_other = swap(ctx, 1)
+        ctx_other = jnp.concatenate([swap(low, 1), swap(high, 1)], axis=0)
 
         inner_next = mid_swap(near)
         out = call(

time: 54.7 us -> 52.8 us (0.965)
  starting transfers between devices: 25.3 us -> 22.4 us
  waiting for transfers between devices: 14.2 us -> 14.9 us
    ppermute x7, starting transfers between devices: 12.1 us -> 10.1 us  [core_swap(): lax.ppermute(value, 'blk', [(i, i ^ group * bits[i % 2]) for i in range(b...]
    ppermute x4, waiting for transfers between devices: 4.28 us -> 2.66 us  [pair_swap(): return lax.ppermute(value, 'shard', [(0, 1), (1, 0), (2, 3), (3, 2)])]
    ppermute x7, waiting for transfers between devices: 7.36 us -> 8.88 us  [core_swap(): lax.ppermute(value, 'blk', [(i, i ^ group * bits[i % 2]) for i in range(b...]
    ppermute x4, starting transfers between devices: 12.5 us -> 11.2 us  [pair_swap(): return lax.ppermute(value, 'shard', [(0, 1), (1, 0), (2, 3), (3, 2)])]
    ppermute x4 -> x5, waiting for transfers between devices: 2.51 us -> 3.3 us  [swap(): return lax.ppermute(value, 'blk', [(i, i ^ bit) for i in range(blk)])]
  transfers between devices with their start and end apart: 19 -> 20, of which waited for: 9 -> 11; matrix products, arithmetic and copies ran while one was open for 0% -> 0% of each run, Pallas kernels for 22% -> 23%
where the time goes in v5:
time: 52.8 us; the launch traced here: 52.4 us
  starting transfers between devices  22.4 us (42%)
  waiting for transfers between devices  14.9 us (28%)
  Pallas kernels  13.2 us (25%)
  local copies, waits for them, and re-layouts  1.03 us (2%)
  between operations  0.83 us (2%)
    pallas_call x17, Pallas kernels, call(): pl.pallas_call(kernel, out_shape=tuple(outs), in_specs=[pl.BlockSpec(memo...  13.2 us
    ppermute x4, starting transfers between devices, pair_swap(): return lax.ppermute(value, 'shard', [(0, 1), (1, 0), (2, 3), (3, 2)])  11.2 us
    ppermute x7, starting transfers between devices, core_swap(): lax.ppermute(value, 'blk', [(i, i ^ group * bits[i % 2]) for i in range(b...  10.1 us
    ppermute x7, waiting for transfers between devices, core_swap(): lax.ppermute(value, 'blk', [(i, i ^ group * bits[i % 2]) for i in range(b...  8.88 us
    ppermute x5, waiting for transfers between devices, swap(): return lax.ppermute(value, 'blk', [(i, i ^ bit) for i in range(blk)])  3.3 us
    ppermute x4, waiting for transfers between devices, pair_swap(): return lax.ppermute(value, 'shard', [(0, 1), (1, 0), (2, 3), (3, 2)])  2.66 us
  transfers between devices with their start and end apart: 20, of which 11 were waited for; matrix products, arithmetic and copies ran while one was open for 0% of the time, Pallas kernels for 23%

profile of v5, /device:TPU:0, one launch (start us, length us, event | category | flops | bytes accessed | tf_op | source)
XLA Modules:
  0.0 52.4 jit_solution(16625563346846495785)
XLA Ops:
  0.6 0.0 copy-start
  0.6 3.0 %collective-permute-start.3 = (bf16[320,640]{1,0:T(8,128)(2,1)}, bf16[320,640]{1,0:T(8,128)(2,1)S(1)}, u32[]{:S(2)}, u32[]{:S(2)}) collective-permute-start(bf16[320,640]{1,0:T(8,128)(2,1)} %bitcast.3), channel_id=1, source_target_pairs={{0,8},{4,20},{8,0},{12,28},{16,24},{20,4},{24,16},{28,12},{1,9},{5... | collective-permute-start | bytes 1228808 | tf_op jit(solution)/shard_map/ppermute | solution.py:323
  3.6 0.0 collective-permute-start
  3.7 1.8 %collective-permute-done.other_ref = bf16[256,640]{1,0:T(8,128)(2,1)S(1)} collective-permute-done((bf16[256,640]{1,0:T(8,128)(2,1)}, bf16[256,640]{1,0:T(8,128)(2,1)S(1)}, u32[]{:S(2)}, u32[]{:S(2)}) %collective-permute-start) | collective-permute-done | bytes 327712 | tf_op jit(solution)/shard_map/ppermute | solution.py:319
  5.5 1.0 %copy-done.5 = bf16[256,640]{1,0:T(8,128)(2,1)S(1)} copy-done((bf16[256,640]{1,0:T(8,128)(2,1)S(1)}, bf16[256,640]{1,0:T(8,128)(2,1)}, u32[]{:S(2)}) %copy-start.5) | copy-done | bytes 327704
  6.5 0.2 shard_map.110.refs_0_
  6.7 1.6 %collective-permute-start.1 = (bf16[320,512]{1,0:T(8,128)(2,1)S(1)}, bf16[320,512]{1,0:T(8,128)(2,1)S(1)}, u32[]{:S(2)}, u32[]{:S(2)}) collective-permute-start(bf16[320,512]{1,0:T(8,128)(2,1)S(1)} %shard_map.110.refs_0_), channel_id=1, source_target_pairs={{0,1},{1,0},{2,3},{3,2},{4,5},{5,4},{6,7},{7,6},{8,9},{9,8},{10,11... | collective-permute-start | bytes 983048 | tf_op jit(solution)/shard_map/ppermute | solution.py:326
  8.4 0.0 collective-permute-start.2
  8.4 1.4 %collective-permute-done.3.refs_1_ = bf16[320,640]{1,0:T(8,128)(2,1)S(1)} collective-permute-done((bf16[320,640]{1,0:T(8,128)(2,1)}, bf16[320,640]{1,0:T(8,128)(2,1)S(1)}, u32[]{:S(2)}, u32[]{:S(2)}) %collective-permute-start.3) | collective-permute-done | bytes 409632 | tf_op jit(solution)/shard_map/ppermute | solution.py:323
  9.8 0.0 copy-done
  9.8 0.1 broadcast_select_fusion
  9.9 2.1 %collective-permute-start.4 = (bf16[320,640]{1,0:T(8,128)(2,1)S(1)}, bf16[320,640]{1,0:T(8,128)(2,1)S(1)}, u32[]{:S(2)}, u32[]{:S(2)}) collective-permute-start(bf16[320,640]{1,0:T(8,128)(2,1)S(1)} %get-tuple-element.84), channel_id=1, source_target_pairs={{0,16},{4,12},{8,24},{12,4},{16,0},{20,28},{24,8},{28,20},{1,17},{... | collective-permute-start | bytes 1228808 | tf_op jit(solution)/shard_map/ppermute | solution.py:323
  12.0 0.0 copy-done.1
  12.0 0.0 copy-done.6
  12.0 1.3 %shard_map.111 = (bf16[256,640]{1,0:T(8,128)(2,1)S(1)}, bf16[128,640]{1,0:T(8,128)(2,1)S(1)}, bf16[128,640]{1,0:T(8,128)(2,1)S(1)}, f32[5,256,256]{2,1,0:T(8,128)S(1)}) custom-call(bf16[256,640]{1,0:T(8,128)(2,1)S(1)} %copy-done.1, bf16[256,640]{1,0:T(8,128)(2,1)S(1)} %copy-done.2, bf16[256,640]{1,0:T(8,128)(2,1)S(1)} %copy-done.3, s32[1,256]{1,0:T(1,128)S(1)} %copy-done.6), custom_call_target="tpu_custom_call" | custom-call | flops 167772160 | bytes 2950144 | tf_op jit(solution)/shard_map/pallas_call | solution.py:25
  13.3 0.1 collective-permute-start.6
  13.4 0.5 collective-permute-start.7
  13.9 0.9 %collective-permute-done.6 = bf16[128,640]{1,0:T(8,128)(2,1)S(1)} collective-permute-done((bf16[128,640]{1,0:T(8,128)(2,1)S(1)}, bf16[128,640]{1,0:T(8,128)(2,1)S(1)}, u32[]{:S(2)}, u32[]{:S(2)}) %collective-permute-start.6) | collective-permute-done | bytes 163872 | tf_op jit(solution)/shard_map/ppermute | solution.py:319
  14.7 0.0 collective-permute-start.5
  14.8 1.7 %collective-permute-done.1.refs_1_ = bf16[320,512]{1,0:T(8,128)(2,1)S(1)} collective-permute-done((bf16[320,512]{1,0:T(8,128)(2,1)S(1)}, bf16[320,512]{1,0:T(8,128)(2,1)S(1)}, u32[]{:S(2)}, u32[]{:S(2)}) %collective-permute-start.1) | collective-permute-done | bytes 327712 | tf_op jit(solution)/shard_map/ppermute | solution.py:326
  16.5 0.0 collective-permute-done.2.refs_5_.refs_0_
  16.5 0.0 collective-permute-start.8
  16.5 0.0 collective-permute-done.7
  16.6 1.4 %collective-permute-done.4.refs_2_ = bf16[320,640]{1,0:T(8,128)(2,1)S(1)} collective-permute-done((bf16[320,640]{1,0:T(8,128)(2,1)S(1)}, bf16[320,640]{1,0:T(8,128)(2,1)S(1)}, u32[]{:S(2)}, u32[]{:S(2)}) %collective-permute-start.4) | collective-permute-done | bytes 409632 | tf_op jit(solution)/shard_map/ppermute | solution.py:323
  17.9 0.5 shard_map.114
  18.4 2.8 %collective-permute-start.9 = (bf16[320,512]{1,0:T(8,128)(2,1)S(1)}, bf16[320,512]{1,0:T(8,128)(2,1)S(1)}, u32[]{:S(2)}, u32[]{:S(2)}) collective-permute-start(bf16[320,512]{1,0:T(8,128)(2,1)S(1)} %shard_map.114), channel_id=1, source_target_pairs={{0,1},{1,0},{2,3},{3,2},{4,5},{5,4},{6,7},{7,6},{8,9},{9,8},{10,11... | collective-permute-start | bytes 983048 | tf_op jit(solution)/shard_map/ppermute | solution.py:326
  21.1 1.5 %collective-permute-done.5.refs_3_ = bf16[320,640]{1,0:T(8,128)(2,1)S(1)} collective-permute-done((bf16[320,640]{1,0:T(8,128)(2,1)S(1)}, bf16[320,640]{1,0:T(8,128)(2,1)S(1)}, u32[]{:S(2)}, u32[]{:S(2)}) %collective-permute-start.5) | collective-permute-done | bytes 409632 | tf_op jit(solution)/shard_map/ppermute | solution.py:323
  22.7 0.1 shard_map.112.refs_0_.refs_4_.refs_2_
  22.8 0.0 collective-permute-done.8.refs_3_
  22.8 0.5 shard_map.113
  23.3 5.0 %collective-permute-start.10 = (bf16[320,512]{1,0:T(8,128)(2,1)S(1)}, bf16[320,512]{1,0:T(8,128)(2,1)S(1)}, u32[]{:S(2)}, u32[]{:S(2)}) collective-permute-start(bf16[320,512]{1,0:T(8,128)(2,1)S(1)} %shard_map.113), channel_id=1, source_target_pairs={{0,1},{1,0},{2,3},{3,2},{4,5},{5,4},{6,7},{7,6},{8,9},{9,8},{10,11... | collective-permute-start | bytes 983048 | tf_op jit(solution)/shard_map/ppermute | solution.py:326
  28.3 0.0 collective-permute-done.9.refs_2_.refs_3_
  28.3 0.4 shard_map.117
  28.7 0.1 collective-permute-start.13
  28.8 1.6 %shard_map.115 = (bf16[160,640]{1,0:T(8,128)(2,1)S(1)}, bf16[160,640]{1,0:T(8,128)(2,1)S(1)}, f32[320,640]{1,0:T(8,128)S(1)}, f32[320,640]{1,0:T(8,128)S(1)}) custom-call(bf16[320,512]{1,0:T(8,128)(2,1)S(1)} %shard_map.110.refs_0_, bf16[320,512]{1,0:T(8,128)(2,1)S(1)} %collective-permute-done.1.refs_1_, ...), custom_call_target="tpu_custom_call" | custom-call | flops 629145600 | bytes 4014080 | tf_op jit(solution)/shard_map/pallas_call | solution.py:25
  30.4 1.2 %collective-permute-start.11 = (bf16[160,640]{1,0:T(8,128)(2,1)S(1)}, bf16[160,640]{1,0:T(8,128)(2,1)S(1)}, u32[]{:S(2)}, u32[]{:S(2)}) collective-permute-start(bf16[160,640]{1,0:T(8,128)(2,1)S(1)} %get-tuple-element.56), channel_id=1, source_target_pairs={{0,8},{4,20},{8,0},{12,28},{16,24},{20,4},{24,16},{28,12},{1,9},{5... | collective-permute-start | bytes 614408 | tf_op jit(solution)/shard_map/ppermute | solution.py:323
  31.6 0.8 %collective-permute-start.12 = (bf16[160,640]{1,0:T(8,128)(2,1)S(1)}, bf16[160,640]{1,0:T(8,128)(2,1)S(1)}, u32[]{:S(2)}, u32[]{:S(2)}) collective-permute-start(bf16[160,640]{1,0:T(8,128)(2,1)S(1)} %get-tuple-element.57), channel_id=1, source_target_pairs={{0,8},{4,20},{8,0},{12,28},{16,24},{20,4},{24,16},{28,12},{1,9},{5... | collective-permute-start | bytes 614408 | tf_op jit(solution)/shard_map/ppermute | solution.py:323
  32.5 1.5 %shard_map.116.refs_3_ = f32[512,640]{1,0:T(8,128)S(1)} custom-call(bf16[320,512]{1,0:T(8,128)(2,1)S(1)} %shard_map.110.refs_0_, bf16[320,512]{1,0:T(8,128)(2,1)S(1)} %collective-permute-done.1.refs_1_, bf16[320,512]{1,0:T(8,128)(2,1)S(1)} %collective-permute-done.9.refs_2_.refs_3_, bf16[320,512]{1,0:T(8,128)(2,1)S(1)} %collective-permute-done.8.refs_3_, ...), custom_call_target="tpu_custom_call" | custom-call | flops 629145600 | bytes 4259840 | tf_op jit(solution)/shard_map/pallas_call | solution.py:25
  34.0 0.7 %collective-permute-done.10.refs_1_.refs_3_ = bf16[320,512]{1,0:T(8,128)(2,1)S(1)} collective-permute-done((bf16[320,512]{1,0:T(8,128)(2,1)S(1)}, bf16[320,512]{1,0:T(8,128)(2,1)S(1)}, u32[]{:S(2)}, u32[]{:S(2)}) %collective-permute-start.10) | collective-permute-done | bytes 327712 | tf_op jit(solution)/shard_map/ppermute | solution.py:326
  34.7 0.4 shard_map.118
  35.2 1.3 %collective-permute-start.14 = (bf16[320,640]{1,0:T(8,128)(2,1)S(1)}, bf16[320,640]{1,0:T(8,128)(2,1)S(1)}, u32[]{:S(2)}, u32[]{:S(2)}) collective-permute-start(bf16[320,640]{1,0:T(8,128)(2,1)S(1)} %get-tuple-element.59), channel_id=1, source_target_pairs={{0,8},{4,20},{8,0},{12,28},{16,24},{20,4},{24,16},{28,12},{1,9},{5... | collective-permute-start | bytes 1228808 | tf_op jit(solution)/shard_map/ppermute | solution.py:323
  36.5 0.0 collective-permute-done.13.refs_3_
  36.5 0.5 shard_map.119
  36.9 1.8 %collective-permute-start.15 = (bf16[320,512]{1,0:T(8,128)(2,1)S(1)}, bf16[320,512]{1,0:T(8,128)(2,1)S(1)}, u32[]{:S(2)}, u32[]{:S(2)}) collective-permute-start(bf16[320,512]{1,0:T(8,128)(2,1)S(1)} %shard_map.119), channel_id=1, source_target_pairs={{0,1},{1,0},{2,3},{3,2},{4,5},{5,4},{6,7},{7,6},{8,9},{9,8},{10,11... | collective-permute-start | bytes 983048 | tf_op jit(solution)/shard_map/ppermute | solution.py:326
  38.7 0.0 collective-permute-done.11.refs_1_
  38.7 0.0 collective-permute-done.12.refs_2_
  38.7 0.5 shard_map.121
  39.2 0.1 collective-permute-start.16
  39.3 3.9 %collective-permute-done.14.refs_4_ = bf16[320,640]{1,0:T(8,128)(2,1)S(1)} collective-permute-done((bf16[320,640]{1,0:T(8,128)(2,1)S(1)}, bf16[320,640]{1,0:T(8,128)(2,1)S(1)}, u32[]{:S(2)}, u32[]{:S(2)}) %collective-permute-start.14) | collective-permute-done | bytes 409632 | tf_op jit(solution)/shard_map/ppermute | solution.py:323
  43.2 0.2 shard_map.120
  43.4 1.6 %collective-permute-start.18 = (bf16[320,640]{1,0:T(8,128)(2,1)S(1)}, bf16[320,640]{1,0:T(8,128)(2,1)S(1)}, u32[]{:S(2)}, u32[]{:S(2)}) collective-permute-start(bf16[320,640]{1,0:T(8,128)(2,1)S(1)} %get-tuple-element.76), channel_id=1, source_target_pairs={{0,16},{4,12},{8,24},{12,4},{16,0},{20,28},{24,8},{28,20},{1,17},{... | collective-permute-start | bytes 1228808 | tf_op jit(solution)/shard_map/ppermute | solution.py:323
  45.0 0.6 %shard_map.122 = (f32[256,640]{1,0:T(8,128)S(1)}, bf16[256,640]{1,0:T(8,128)(2,1)S(1)}) custom-call(bf16[320,512]{1,0:T(8,128)(2,1)S(1)} %collective-permute-done.2.refs_5_.refs_0_, bf16[320,512]{1,0:T(8,128)(2,1)S(1)} %collective-permute-done.10.refs_1_.refs_3_, bf16[4,320,640]{2,1,0:T(8,128)(2,1)S(1)} %shard_map.112.refs_0_.refs_4_.refs_2_, ...), custom_call_target="tpu_custom_call" | custom-call | flops 209715200 | bytes 4587520 | tf_op jit(solution)/shard_map/pallas_call | solution.py:25
  45.6 0.1 collective-permute-start.19
  45.7 0.2 collective-permute-done.15.refs_3_
  45.9 0.0 collective-permute-done.16.refs_4_
  45.9 0.5 shard_map.123
  46.3 0.4 collective-permute-start.17
  46.7 0.6 %collective-permute-done.19.other_ref = bf16[256,640]{1,0:T(8,128)(2,1)S(1)} collective-permute-done((bf16[256,640]{1,0:T(8,128)(2,1)S(1)}, bf16[256,640]{1,0:T(8,128)(2,1)S(1)}, u32[]{:S(2)}, u32[]{:S(2)}) %collective-permute-start.19) | collective-permute-done | bytes 327712 | tf_op jit(solution)/shard_map/ppermute | solution.py:319
  47.3 2.5 %shard_map.126 = (bf16[256,640]{1,0:T(8,128)(2,1)}, bf16[256,640]{1,0:T(8,128)(2,1)}, bf16[256,640]{1,0:T(8,128)(2,1)}) custom-call(bf16[256,640]{1,0:T(8,128)(2,1)S(1)} %copy-done.1, bf16[256,640]{1,0:T(8,128)(2,1)S(1)} %copy-done.2, bf16[256,640]{1,0:T(8,128)(2,1)S(1)} %copy-done.3, f32[5,256,256]{2,1,0:T(8,128)S(1)} %get-tuple-element.77.probs_ref, ...), custom_call_target="tpu_custom_call" | custom-call | flops 419430400 | bytes 4259840 | tf_op jit(solution)/shard_map/pallas_call | solution.py:25
  49.8 0.0 collective-permute-done.17.other_ref
  49.8 0.0 copy-done.4
  49.8 1.0 %shard_map.124 = bf16[256,640]{1,0:T(8,128)(2,1)} custom-call(bf16[256,640]{1,0:T(8,128)(2,1)S(1)} %copy-done.4, f32[320,256]{1,0:T(8,128)S(1)} %get-tuple-element.72.keep_ref, f32[320,256]{1,0:T(8,128)S(1)} %collective-permute-done.17.other_ref), custom_call_target="tpu_custom_call" | custom-call | bytes 1310720 | tf_op jit(solution)/shard_map/pallas_call | solution.py:25
  50.8 0.6 %collective-permute-done.18.refs_1_ = bf16[320,640]{1,0:T(8,128)(2,1)S(1)} collective-permute-done((bf16[320,640]{1,0:T(8,128)(2,1)S(1)}, bf16[320,640]{1,0:T(8,128)(2,1)S(1)}, u32[]{:S(2)}, u32[]{:S(2)}) %collective-permute-start.18) | collective-permute-done | bytes 409632 | tf_op jit(solution)/shard_map/ppermute | solution.py:323
  51.4 1.0 %shard_map.125 = f32[320,640]{1,0:T(8,128)} custom-call(f32[320,640]{1,0:T(8,128)S(1)} %get-tuple-element.75.refs_0_, bf16[320,640]{1,0:T(8,128)(2,1)S(1)} %collective-permute-done.18.refs_1_), custom_call_target="tpu_custom_call" | custom-call | bytes 2048000 | tf_op jit(solution)/shard_map/pallas_call | solution.py:25
  (10 shorter events, 0.1 us)
Async XLA Ops:
  0.6 9.2 %copy-start = (bf16[640,320]{0,1:T(8,128)(2,1)S(1)}, bf16[640,320]{0,1:T(8,128)(2,1)}, u32[]{:S(2)}) copy-start(bf16[640,320]{0,1:T(8,128)(2,1)} %param.12) | copy-start | bytes 1228804
  0.6 9.1 %collective-permute-start.3 = (bf16[320,640]{1,0:T(8,128)(2,1)}, bf16[320,640]{1,0:T(8,128)(2,1)S(1)}, u32[]{:S(2)}, u32[]{:S(2)}) collective-permute-start(bf16[320,640]{1,0:T(8,128)(2,1)} %bitcast.3), channel_id=1, source_target_pairs={{0,8},{4,20},{8,0},{12,28},{16,24},{20,4},{24,16},{28,12},{1,9},{5... | collective-permute-start | bytes 1228808 | tf_op jit(solution)/shard_map/ppermute | solution.py:323
  3.6 1.8 %collective-permute-start = (bf16[256,640]{1,0:T(8,128)(2,1)}, bf16[256,640]{1,0:T(8,128)(2,1)S(1)}, u32[]{:S(2)}, u32[]{:S(2)}) collective-permute-start(bf16[256,640]{1,0:T(8,128)(2,1)} %own_ref.1), channel_id=1, source_target_pairs={{0,4},{4,0},{8,12},{12,8},{16,20},{20,16},{24,28},{28,24},{1,5},{5... | collective-permute-start | bytes 983048 | tf_op jit(solution)/shard_map/ppermute | solution.py:319
  3.6 8.3 %copy-start.1 = (bf16[256,640]{1,0:T(8,128)(2,1)S(1)}, bf16[256,640]{1,0:T(8,128)(2,1)}, u32[]{:S(2)}) copy-start(bf16[256,640]{1,0:T(8,128)(2,1)} %q_ref.2) | copy-start | bytes 983044
  3.7 8.3 %copy-start.2 = (bf16[256,640]{1,0:T(8,128)(2,1)S(1)}, bf16[256,640]{1,0:T(8,128)(2,1)}, u32[]{:S(2)}) copy-start(bf16[256,640]{1,0:T(8,128)(2,1)} %k_ref.3) | copy-start | bytes 983044
  3.7 8.3 %copy-start.3 = (bf16[256,640]{1,0:T(8,128)(2,1)S(1)}, bf16[256,640]{1,0:T(8,128)(2,1)}, u32[]{:S(2)}) copy-start(bf16[256,640]{1,0:T(8,128)(2,1)} %v_ref.3) | copy-start | bytes 983044
  5.5 1.0 %copy-start.5 = (bf16[256,640]{1,0:T(8,128)(2,1)S(1)}, bf16[256,640]{1,0:T(8,128)(2,1)}, u32[]{:S(2)}) copy-start(bf16[256,640]{1,0:T(8,128)(2,1)} %own_ref.1) | copy-start | bytes 983044
  6.5 5.5 %copy-start.6 = (s32[1,256]{1,0:T(1,128)S(1)}, s32[1,256]{1,0:T(1,128)}, u32[]{:S(2)}) copy-start(s32[1,256]{1,0:T(1,128)} %seg_ref.1) | copy-start | bytes 3076
  6.7 9.8 %collective-permute-start.1 = (bf16[320,512]{1,0:T(8,128)(2,1)S(1)}, bf16[320,512]{1,0:T(8,128)(2,1)S(1)}, u32[]{:S(2)}, u32[]{:S(2)}) collective-permute-start(bf16[320,512]{1,0:T(8,128)(2,1)S(1)} %shard_map.110.refs_0_), channel_id=1, source_target_pairs={{0,1},{1,0},{2,3},{3,2},{4,5},{5,4},{6,7},{7,6},{8,9},{9,8},{10,11... | collective-permute-start | bytes 983048 | tf_op jit(solution)/shard_map/ppermute | solution.py:326
  8.4 8.2 %collective-permute-start.2 = (bf16[320,512]{1,0:T(8,128)(2,1)S(1)}, bf16[320,512]{1,0:T(8,128)(2,1)S(1)}, u32[]{:S(2)}, u32[]{:S(2)}) collective-permute-start(bf16[320,512]{1,0:T(8,128)(2,1)S(1)} %shard_map.110.refs_0_), channel_id=1, source_target_pairs={{1,2},{2,1},{0,4},{3,7},{5,6},{6,5},{4,0},{7,3},{9,10},{10,9},{8,1... | collective-permute-start | bytes 983048 | tf_op jit(solution)/shard_map/ppermute | solution.py:333
  9.9 8.0 %collective-permute-start.4 = (bf16[320,640]{1,0:T(8,128)(2,1)S(1)}, bf16[320,640]{1,0:T(8,128)(2,1)S(1)}, u32[]{:S(2)}, u32[]{:S(2)}) collective-permute-start(bf16[320,640]{1,0:T(8,128)(2,1)S(1)} %get-tuple-element.84), channel_id=1, source_target_pairs={{0,16},{4,12},{8,24},{12,4},{16,0},{20,28},{24,8},{28,20},{1,17},{... | collective-permute-start | bytes 1228808 | tf_op jit(solution)/shard_map/ppermute | solution.py:323
  13.3 1.5 %collective-permute-start.6 = (bf16[128,640]{1,0:T(8,128)(2,1)S(1)}, bf16[128,640]{1,0:T(8,128)(2,1)S(1)}, u32[]{:S(2)}, u32[]{:S(2)}) collective-permute-start(bf16[128,640]{1,0:T(8,128)(2,1)S(1)} %get-tuple-element.49), channel_id=1, source_target_pairs={{0,4},{4,0},{8,12},{12,8},{16,20},{20,16},{24,28},{28,24},{1,5},{5... | collective-permute-start | bytes 491528 | tf_op jit(solution)/shard_map/ppermute | solution.py:319
  13.4 3.2 %collective-permute-start.7 = (bf16[128,640]{1,0:T(8,128)(2,1)S(1)}, bf16[128,640]{1,0:T(8,128)(2,1)S(1)}, u32[]{:S(2)}, u32[]{:S(2)}) collective-permute-start(bf16[128,640]{1,0:T(8,128)(2,1)S(1)} %get-tuple-element.50), channel_id=1, source_target_pairs={{0,4},{4,0},{8,12},{12,8},{16,20},{20,16},{24,28},{28,24},{1,5},{5... | collective-permute-start | bytes 491528 | tf_op jit(solution)/shard_map/ppermute | solution.py:319
  14.7 8.0 %collective-permute-start.5 = (bf16[320,640]{1,0:T(8,128)(2,1)S(1)}, bf16[320,640]{1,0:T(8,128)(2,1)S(1)}, u32[]{:S(2)}, u32[]{:S(2)}) collective-permute-start(bf16[320,640]{1,0:T(8,128)(2,1)S(1)} %get-tuple-element.83), channel_id=1, source_target_pairs={{0,16},{4,12},{8,24},{12,4},{16,0},{20,28},{24,8},{28,20},{1,17},{... | collective-permute-start | bytes 1228808 | tf_op jit(solution)/shard_map/ppermute | solution.py:323
  16.5 6.3 %collective-permute-start.8 = (bf16[320,512]{1,0:T(8,128)(2,1)S(1)}, bf16[320,512]{1,0:T(8,128)(2,1)S(1)}, u32[]{:S(2)}, u32[]{:S(2)}) collective-permute-start(bf16[320,512]{1,0:T(8,128)(2,1)S(1)} %collective-permute-done.1.refs_1_), channel_id=1, source_target_pairs={{1,2},{2,1},{0,4},{3,7},{5,6},{6,5},{4,0},{7,3},{9,10},{10,9},{8,1... | collective-permute-start | bytes 983048 | tf_op jit(solution)/shard_map/ppermute | solution.py:333
  18.4 9.9 %collective-permute-start.9 = (bf16[320,512]{1,0:T(8,128)(2,1)S(1)}, bf16[320,512]{1,0:T(8,128)(2,1)S(1)}, u32[]{:S(2)}, u32[]{:S(2)}) collective-permute-start(bf16[320,512]{1,0:T(8,128)(2,1)S(1)} %shard_map.114), channel_id=1, source_target_pairs={{0,1},{1,0},{2,3},{3,2},{4,5},{5,4},{6,7},{7,6},{8,9},{9,8},{10,11... | collective-permute-start | bytes 983048 | tf_op jit(solution)/shard_map/ppermute | solution.py:326
  23.3 11.4 %collective-permute-start.10 = (bf16[320,512]{1,0:T(8,128)(2,1)S(1)}, bf16[320,512]{1,0:T(8,128)(2,1)S(1)}, u32[]{:S(2)}, u32[]{:S(2)}) collective-permute-start(bf16[320,512]{1,0:T(8,128)(2,1)S(1)} %shard_map.113), channel_id=1, source_target_pairs={{0,1},{1,0},{2,3},{3,2},{4,5},{5,4},{6,7},{7,6},{8,9},{9,8},{10,11... | collective-permute-start | bytes 983048 | tf_op jit(solution)/shard_map/ppermute | solution.py:326
  28.7 7.7 %collective-permute-start.13 = (bf16[320,512]{1,0:T(8,128)(2,1)S(1)}, bf16[320,512]{1,0:T(8,128)(2,1)S(1)}, u32[]{:S(2)}, u32[]{:S(2)}) collective-permute-start(bf16[320,512]{1,0:T(8,128)(2,1)S(1)} %shard_map.117), channel_id=1, source_target_pairs={{1,2},{2,1},{0,4},{3,7},{5,6},{6,5},{4,0},{7,3},{9,10},{10,9},{8,1... | collective-permute-start | bytes 983048 | tf_op jit(solution)/shard_map/ppermute | solution.py:333
  30.4 8.4 %collective-permute-start.11 = (bf16[160,640]{1,0:T(8,128)(2,1)S(1)}, bf16[160,640]{1,0:T(8,128)(2,1)S(1)}, u32[]{:S(2)}, u32[]{:S(2)}) collective-permute-start(bf16[160,640]{1,0:T(8,128)(2,1)S(1)} %get-tuple-element.56), channel_id=1, source_target_pairs={{0,8},{4,20},{8,0},{12,28},{16,24},{20,4},{24,16},{28,12},{1,9},{5... | collective-permute-start | bytes 614408 | tf_op jit(solution)/shard_map/ppermute | solution.py:323
  31.6 7.1 %collective-permute-start.12 = (bf16[160,640]{1,0:T(8,128)(2,1)S(1)}, bf16[160,640]{1,0:T(8,128)(2,1)S(1)}, u32[]{:S(2)}, u32[]{:S(2)}) collective-permute-start(bf16[160,640]{1,0:T(8,128)(2,1)S(1)} %get-tuple-element.57), channel_id=1, source_target_pairs={{0,8},{4,20},{8,0},{12,28},{16,24},{20,4},{24,16},{28,12},{1,9},{5... | collective-permute-start | bytes 614408 | tf_op jit(solution)/shard_map/ppermute | solution.py:323
  35.2 8.0 %collective-permute-start.14 = (bf16[320,640]{1,0:T(8,128)(2,1)S(1)}, bf16[320,640]{1,0:T(8,128)(2,1)S(1)}, u32[]{:S(2)}, u32[]{:S(2)}) collective-permute-start(bf16[320,640]{1,0:T(8,128)(2,1)S(1)} %get-tuple-element.59), channel_id=1, source_target_pairs={{0,8},{4,20},{8,0},{12,28},{16,24},{20,4},{24,16},{28,12},{1,9},{5... | collective-permute-start | bytes 1228808 | tf_op jit(solution)/shard_map/ppermute | solution.py:323
  36.9 8.9 %collective-permute-start.15 = (bf16[320,512]{1,0:T(8,128)(2,1)S(1)}, bf16[320,512]{1,0:T(8,128)(2,1)S(1)}, u32[]{:S(2)}, u32[]{:S(2)}) collective-permute-start(bf16[320,512]{1,0:T(8,128)(2,1)S(1)} %shard_map.119), channel_id=1, source_target_pairs={{0,1},{1,0},{2,3},{3,2},{4,5},{5,4},{6,7},{7,6},{8,9},{9,8},{10,11... | collective-permute-start | bytes 983048 | tf_op jit(solution)/shard_map/ppermute | solution.py:326
  39.2 6.7 %collective-permute-start.16 = (bf16[320,512]{1,0:T(8,128)(2,1)S(1)}, bf16[320,512]{1,0:T(8,128)(2,1)S(1)}, u32[]{:S(2)}, u32[]{:S(2)}) collective-permute-start(bf16[320,512]{1,0:T(8,128)(2,1)S(1)} %shard_map.121), channel_id=1, source_target_pairs={{1,2},{2,1},{0,4},{3,7},{5,6},{6,5},{4,0},{7,3},{9,10},{10,9},{8,1... | collective-permute-start | bytes 983048 | tf_op jit(solution)/shard_map/ppermute | solution.py:333
  43.4 8.0 %collective-permute-start.18 = (bf16[320,640]{1,0:T(8,128)(2,1)S(1)}, bf16[320,640]{1,0:T(8,128)(2,1)S(1)}, u32[]{:S(2)}, u32[]{:S(2)}) collective-permute-start(bf16[320,640]{1,0:T(8,128)(2,1)S(1)} %get-tuple-element.76), channel_id=1, source_target_pairs={{0,16},{4,12},{8,24},{12,4},{16,0},{20,28},{24,8},{28,20},{1,17},{... | collective-permute-start | bytes 1228808 | tf_op jit(solution)/shard_map/ppermute | solution.py:323
  45.6 1.7 %collective-permute-start.19 = (bf16[256,640]{1,0:T(8,128)(2,1)S(1)}, bf16[256,640]{1,0:T(8,128)(2,1)S(1)}, u32[]{:S(2)}, u32[]{:S(2)}) collective-permute-start(bf16[256,640]{1,0:T(8,128)(2,1)S(1)} %get-tuple-element.79), channel_id=1, source_target_pairs={{0,4},{4,0},{8,12},{12,8},{16,20},{20,16},{24,28},{28,24},{1,5},{5... | collective-permute-start | bytes 983048 | tf_op jit(solution)/shard_map/ppermute | solution.py:319
  46.3 3.5 %collective-permute-start.17 = (f32[320,256]{1,0:T(8,128)S(1)}, f32[320,256]{1,0:T(8,128)S(1)}, u32[]{:S(2)}, u32[]{:S(2)}) collective-permute-start(f32[320,256]{1,0:T(8,128)S(1)} %get-tuple-element.73), channel_id=1, source_target_pairs={{0,4},{4,0},{8,12},{12,8},{16,20},{20,16},{24,28},{28,24},{1,5},{5... | collective-permute-start | bytes 983048 | tf_op jit(solution)/shard_map/ppermute | solution.py:319
  47.3 2.5 %copy-start.4 = (bf16[256,640]{1,0:T(8,128)(2,1)S(1)}, bf16[256,640]{1,0:T(8,128)(2,1)}, u32[]{:S(2)}) copy-start(bf16[256,640]{1,0:T(8,128)(2,1)} %residual_ref.1) | copy-start | bytes 983044

commit v6 on v5

--- a/solution.py
+++ b/solution.py
@@ -81,24 +81,34 @@
     return plane ^ (lax.axis_index("blk") // group)
 
 
+def own_half_kernel(own_ref, out_ref):
+    half = out_ref.shape[0]
+    own = own_ref[...].T
+    for side in range(2):
+
+        @pl.when(lax.rem(lax.axis_index("blk"), 2) == side)
+        def _():
+            out_ref[...] = own[side * half : (side + 1) * half]
+
+
 def unit_kernel(own_ref, other_ref, unit_ref):
-    half, count = unit_ref.shape[0], own_ref.shape[0]
-    core = lax.rem(lax.axis_index("blk"), 2)
-    own, other = own_ref[...].T, other_ref[...].T
+    half, count = own_ref.shape
+    other = other_ref[...].T
+    unit_ref[:, :count] = own_ref[...]
     for side in range(2):
 
-        @pl.when(core == side)
+        @pl.when(lax.rem(lax.axis_index("blk"), 2) == side)
         def _():
-            rows = slice(side * half, (side + 1) * half)
-            unit_ref[:, :count] = own[rows]
-            unit_ref[:, count:] = other[rows]
+            unit_ref[:, count:] = other[side * half : (side + 1) * half]
 
 
 def make_unit(own, other, strips):
     count, width = own.shape
     half = width // 2
     if strips == 1:
-        return call(unit_kernel, (shape(half, 2 * count),), own, other)[0]
+        kept = call(own_half_kernel, (shape(half, count),), own)[0]
+        kept, other = lax.optimization_barrier((kept, other))
+        return call(unit_kernel, (shape(half, 2 * count),), kept, other)[0]
     core = lax.rem(lax.axis_index("blk"), 2)
     both = jnp.concatenate([own, other], axis=0).T.reshape(strips, 2, half // strips, 2 * count)
     return lax.dynamic_index_in_dim(both, core, 1, keepdims=False).reshape(half, 2 * count)
@@ -212,40 +222,30 @@
     return (residual.astype(F32) + total.T).astype(BF16)
 
 
-def early_planes(unit_ref, near_ref, outer_ref, inner_ref, body):
-    z = lax.axis_index("shard")
-    body(z, unit_ref)
-    body(z ^ 1, near_ref)
-    pl.when(is_inner(z))(lambda: body(z ^ 2, inner_ref))
-    pl.when(~is_inner(z))(lambda: body(z ^ 2, outer_ref))
-
-
 def late_plane(inner_ref, outer_ref, body):
     z = lax.axis_index("shard")
     pl.when(is_inner(z))(lambda: body(z ^ 3, inner_ref))
     pl.when(~is_inner(z))(lambda: body(z ^ 3, outer_ref))
 
 
-def d_context_early_kernel(group, *refs):
-    *unit_refs, w_ref, total_ref = refs
-    total_ref[...] = jnp.zeros_like(total_ref)
-
-    def body(plane, unit_ref):
-        total_ref[...] += dot(unit_ref[...], w_ref[plane_slot(plane, group)], TN)
-
-    early_planes(*unit_refs, body)
+def d_context_early_kernel(group, unit_ref, near_ref, w_ref, total_ref):
+    z = lax.axis_index("shard")
+    total_ref[...] = dot(unit_ref[...], w_ref[plane_slot(z, group)], TN)
+    total_ref[...] += dot(near_ref[...], w_ref[plane_slot(z ^ 1, group)], TN)
 
 
 def d_context_late_kernel(group, *refs):
-    inner_ref, outer_ref, w_ref, total_ref, mine_ref, send_ref = refs
+    outer_next, inner_next, inner_far, outer_far, w_ref, total_ref, mine_ref, send_ref = refs
     count = mine_ref.shape[0]
-
-    def body(plane, unit_ref):
-        part = dot(unit_ref[...], w_ref[plane_slot(plane, group)], TN)
+    z = lax.axis_index("shard")
+
+    def finish(next_ref, far_ref):
+        part = dot(next_ref[...], w_ref[plane_slot(z ^ 2, group)], TN)
+        part = part + dot(far_ref[...], w_ref[plane_slot(z ^ 3, group)], TN)
         mine_ref[...] = total_ref[:count] + part[:count]
         send_ref[...] = (total_ref[count:] + part[count:]).astype(BF16)
 
-    late_plane(inner_ref, outer_ref, body)
+    choose(is_inner(z), lambda: finish(inner_next, inner_far), lambda: finish(outer_next, outer_far))
 
 
 def weight_part(unit_ref, own_ref, other_ref):
@@ -254,54 +254,64 @@
     return part + dot(unit_ref[:, count:], other_ref[...], NN)
 
 
+def first_pair(group):
+    core, first = lax.rem(lax.axis_index("blk"), 2), own_bits()[0]
+    slot = plane_slot(lax.axis_index("shard"), group)
+    return (slot & first) == first, core == 0
+
+
+def weight_first_kernel(unit_ref, near_ref, own_ref, other_ref, here_ref, near_out):
+    here_ref[...] = weight_part(unit_ref, own_ref, other_ref)
+    near_out[...] = weight_part(near_ref, own_ref, other_ref)
+
+
 def weight_early_kernel(group, *refs):
-    *unit_refs, own_ref, other_ref, send_a, send_b, keep, rest = refs
+    outer_ref, inner_ref, own_ref, other_ref, here, near, send_a, send_b, beyond = refs
     rows = send_a.shape[0]
-    late, first = late_slot(group), own_bits()[0]
-
-    def body(plane, unit_ref):
-        slot = plane_slot(plane, group)
-        part = weight_part(unit_ref, own_ref, other_ref)
-
-        def into_rest():
-            rest[...] = part
-
-        def into_send():
-            send_a[...] = part[:rows].astype(BF16)
-            send_b[...] = part[rows:].astype(BF16)
-
-        def into_keep():
-            keep[...] = part
-
-        def early():
-            choose((slot & first) == first, into_send, into_keep)
-
-        choose(slot == (late ^ first), into_rest, early)
-
-    early_planes(*unit_refs, body)
-
-
-def weight_late_kernel(group, inner_ref, outer_ref, own_ref, other_ref, rest, send, keep):
+
+    def body(unit_ref):
+        beyond[...] = weight_part(unit_ref, own_ref, other_ref)
+
+    def send(block):
+        send_a[...] = block[:rows].astype(BF16)
+        send_b[...] = block[rows:].astype(BF16)
+
+    choose(is_inner(lax.axis_index("shard")), lambda: body(inner_ref), lambda: body(outer_ref))
+    here_goes, with_near = first_pair(group)
+    pl.when(here_goes)(lambda: send(here))
+    pl.when(~here_goes & with_near)(lambda: send(near))
+    pl.when(~here_goes & ~with_near)(lambda: send(beyond))
+
+
+def weight_late_kernel(group, inner_ref, outer_ref, own_ref, other_ref, near, beyond, send, keep):
     late, first = late_slot(group), own_bits()[0]
     sends = (late & first) == first
+    rest = jnp.where(first_pair(group)[1], beyond[...], near[...])
 
     def body(plane, unit_ref):
         part = weight_part(unit_ref, own_ref, other_ref)
-        send[...] = jnp.where(sends, part, rest[...]).astype(BF16)
-        keep[...] = jnp.where(sends, rest[...], part)
+        send[...] = jnp.where(sends, part, rest).astype(BF16)
+        keep[...] = jnp.where(sends, rest, part)
 
     late_plane(inner_ref, outer_ref, body)
 
 
-def half_sum_kernel(group, early_keep, early_from_a, early_from_b, late_keep, late_from, send, left):
-    rows = early_from_a.shape[0]
+def half_sum_kernel(group, here, near, beyond, from_a, from_b, late_keep, late_from, send, left):
+    rows = from_a.shape[0]
     second = own_bits()[1]
     goes = (late_slot(group) & second) == second
-    for at, early_from in ((pl.ds(0, rows), early_from_a), (pl.ds(rows, rows), early_from_b)):
-        early_sum = early_keep[at] + early_from[...].astype(F32)
-        late_sum = late_keep[at] + late_from[at].astype(F32)
-        send[at] = jnp.where(goes, late_sum, early_sum).astype(BF16)
-        left[at] = jnp.where(goes, early_sum, late_sum)
+    here_goes, with_near = first_pair(group)
+
+    def add(early_keep):
+        for at, early_from in ((pl.ds(0, rows), from_a), (pl.ds(rows, rows), from_b)):
+            early_sum = early_keep[at] + early_from[...].astype(F32)
+            late_sum = late_keep[at] + late_from[at].astype(F32)
+            send[at] = jnp.where(goes, late_sum, early_sum).astype(BF16)
+            left[at] = jnp.where(goes, early_sum, late_sum)
+
+    pl.when(~here_goes)(lambda: add(here))
+    pl.when(here_goes & with_near)(lambda: add(near))
+    pl.when(here_goes & ~with_near)(lambda: add(beyond))
 
 
 def grad_sum_kernel(scale, left_ref, from_ref, out_ref):
@@ -401,6 +411,19 @@
             w_last,
         )[0]
         sources = (w_all, ctx, ctx_other)
+        d_ctx_early = call(
+            bound(d_context_early_kernel, group),
+            (shape(2 * count, width, dtype=F32),),
+            unit,
+            near,
+            w_all,
+            flops=2 * unit_flops,
+        )[0]
+        block, rest = shape(half, width), shape(half, width, dtype=F32)
+        here_part, near_part = call(
+            weight_first_kernel, (rest, rest), unit, near, ctx, ctx_other, flops=2 * unit_flops
+        )
+        inner_next, d_ctx_early, here_part = together(inner_next, d_ctx_early, here_part)
 
         out = call(
             bound(second_message_kernel, group), (message,), *sources, inner_next, flops=unit_flops
@@ -411,26 +434,20 @@
             bound(message_kernel, 2, group), (message,), *sources, pair_two, flops=unit_flops
         )[0]
         mid_three = mid_swap(out)
-        block, rest = shape(half, width), shape(half, width, dtype=F32)
-        ready = (unit, near, pair_two, inner_next)
         piece = shape(half // 2, width)
-        early_send_a, early_send_b, early_keep, early_rest = call(
+        early_send_a, early_send_b, beyond_part = call(
             bound(weight_early_kernel, group),
-            (piece, piece, rest, rest),
-            *ready,
+            (piece, piece, rest),
+            pair_two,
+            inner_next,
             ctx,
             ctx_other,
-            flops=3 * unit_flops,
+            here_part,
+            near_part,
+            flops=unit_flops,
         )
         early_from_a, early_from_b = core_swap(early_send_a, True), core_swap(early_send_b, True)
-        d_ctx_early = call(
-            bound(d_context_early_kernel, group),
-            (shape(2 * count, width, dtype=F32),),
-            *ready,
-            w_all,
-            flops=3 * unit_flops,
-        )[0]
-        pair_three, d_ctx_early, early_rest = together(pair_three, d_ctx_early, early_rest)
+        pair_three, beyond_part = together(pair_three, beyond_part)
 
         late_send, late_keep = call(
             bound(weight_late_kernel, group),
@@ -439,7 +456,8 @@
             pair_three,
             ctx,
             ctx_other,
-            early_rest,
+            near_part,
+            beyond_part,
             flops=unit_flops,
         )
         late_from = core_swap(late_send, True)
@@ -457,16 +475,26 @@
         mine, send = call(
             bound(d_context_late_kernel, group),
             (shape(count, width, dtype=F32), shape(count, width)),
+            pair_two,
+            inner_next,
             inner_far,
             pair_three,
             w_all,
             d_ctx_early,
-            flops=unit_flops,
+            flops=2 * unit_flops,
         )
         d_ctx_other = swap(send, 1)
         late_from, out = together(late_from, out)
         send, left = call(
-            bound(half_sum_kernel, group), (block, rest), early_keep, early_from_a, early_from_b, late_keep, late_from
+            bound(half_sum_kernel, group),
+            (block, rest),
+            here_part,
+            near_part,
+            beyond_part,
+            early_from_a,
+            early_from_b,
+            late_keep,
+            late_from,
         )
         second_from = core_swap(send, False)
 

time: 52.8 us -> 52 us (0.985)
  starting transfers between devices: 22.4 us -> 19.7 us
  waiting for transfers between devices: 14.9 us -> 17.5 us
    ppermute x4, starting transfers between devices: 11.2 us -> 8.11 us  [pair_swap(): return lax.ppermute(value, 'shard', [(0, 1), (1, 0), (2, 3), (3, 2)])]
    ppermute x7, waiting for transfers between devices: 8.88 us -> 11.2 us  [core_swap(): lax.ppermute(value, 'blk', [(i, i ^ group * bits[i % 2]) for i in range(b...]
    ppermute x4, waiting for transfers between devices: 2.66 us -> 4.19 us  [pair_swap(): return lax.ppermute(value, 'shard', [(0, 1), (1, 0), (2, 3), (3, 2)])]
    ppermute x5, waiting for transfers between devices: 3.3 us -> 2.11 us  [swap(): return lax.ppermute(value, 'blk', [(i, i ^ bit) for i in range(blk)])]
    ppermute x4, starting transfers between devices: 0.15 us -> 0.88 us  [mid_swap(): return lax.ppermute(value, ('blk', 'shard'), pairs)]
    ppermute x7, starting transfers between devices: 10.1 us -> 9.55 us  [core_swap(): lax.ppermute(value, 'blk', [(i, i ^ group * bits[i % 2]) for i in range(b...]
    pallas_call x17 -> x19, Pallas kernels: 13.2 us -> 12.7 us  [call(): pl.pallas_call(kernel, out_shape=tuple(outs), in_specs=[pl.BlockSpec(memo...]
  transfers between devices with their start and end apart: 20 -> 20, of which waited for: 11 -> 10; matrix products, arithmetic and copies ran while one was open for 0% -> 0% of each run, Pallas kernels for 23% -> 23%
where the time goes in v6:
time: 52 us; the launch traced here: 51.9 us
  starting transfers between devices  19.7 us (38%)
  waiting for transfers between devices  17.5 us (34%)
  Pallas kernels  12.7 us (24%)
  local copies, waits for them, and re-layouts  1.04 us (2%)
  between operations  0.9 us (2%)
    pallas_call x19, Pallas kernels, call(): pl.pallas_call(kernel, out_shape=tuple(outs), in_specs=[pl.BlockSpec(memo...  12.7 us
    ppermute x7, waiting for transfers between devices, core_swap(): lax.ppermute(value, 'blk', [(i, i ^ group * bits[i % 2]) for i in range(b...  11.2 us
    ppermute x7, starting transfers between devices, core_swap(): lax.ppermute(value, 'blk', [(i, i ^ group * bits[i % 2]) for i in range(b...  9.55 us
    ppermute x4, starting transfers between devices, pair_swap(): return lax.ppermute(value, 'shard', [(0, 1), (1, 0), (2, 3), (3, 2)])  8.11 us
    ppermute x4, waiting for transfers between devices, pair_swap(): return lax.ppermute(value, 'shard', [(0, 1), (1, 0), (2, 3), (3, 2)])  4.19 us
    ppermute x5, waiting for transfers between devices, swap(): return lax.ppermute(value, 'blk', [(i, i ^ bit) for i in range(blk)])  2.11 us
    ppermute x5, starting transfers between devices, swap(): return lax.ppermute(value, 'blk', [(i, i ^ bit) for i in range(blk)])  1.19 us
  transfers between devices with their start and end apart: 20, of which 10 were waited for; matrix products, arithmetic and copies ran while one was open for 0% of the time, Pallas kernels for 23%

profile of v6, /device:TPU:0, one launch (start us, length us, event | category | flops | bytes accessed | tf_op | source)
XLA Modules:
  0.0 51.9 jit_solution(12407737792092897194)
XLA Ops:
  0.6 3.0 %collective-permute-start.3 = (bf16[320,640]{1,0:T(8,128)(2,1)}, bf16[320,640]{1,0:T(8,128)(2,1)S(1)}, u32[]{:S(2)}, u32[]{:S(2)}) collective-permute-start(bf16[320,640]{1,0:T(8,128)(2,1)} %bitcast.3), channel_id=1, source_target_pairs={{0,8},{4,20},{8,0},{12,28},{16,24},{20,4},{24,16},{28,12},{1,9},{5... | collective-permute-start | bytes 1228808 | tf_op jit(solution)/shard_map/ppermute | solution.py:333
  3.6 0.0 collective-permute-start
  3.7 1.0 %copy-done.5 = bf16[256,640]{1,0:T(8,128)(2,1)S(1)} copy-done((bf16[256,640]{1,0:T(8,128)(2,1)S(1)}, bf16[256,640]{1,0:T(8,128)(2,1)}, u32[]{:S(2)}) %copy-start.5) | copy-done | bytes 327704
  4.6 0.1 shard_map.110.own_ref
  4.8 0.0 copy-start.1
  4.8 0.0 copy-start.2
  4.8 0.0 copy-start.3
  4.8 0.0 copy-start.6
  4.8 0.6 %collective-permute-done.other_ref = bf16[256,640]{1,0:T(8,128)(2,1)S(1)} collective-permute-done((bf16[256,640]{1,0:T(8,128)(2,1)}, bf16[256,640]{1,0:T(8,128)(2,1)S(1)}, u32[]{:S(2)}, u32[]{:S(2)}) %collective-permute-start) | collective-permute-done | bytes 327712 | tf_op jit(solution)/shard_map/ppermute | solution.py:329
  5.5 0.1 shard_map.111.refs_0_.unit_ref
  5.6 1.6 %collective-permute-start.1 = (bf16[320,512]{1,0:T(8,128)(2,1)S(1)}, bf16[320,512]{1,0:T(8,128)(2,1)S(1)}, u32[]{:S(2)}, u32[]{:S(2)}) collective-permute-start(bf16[320,512]{1,0:T(8,128)(2,1)S(1)} %shard_map.111.refs_0_.unit_ref), channel_id=1, source_target_pairs={{0,1},{1,0},{2,3},{3,2},{4,5},{5,4},{6,7},{7,6},{8,9},{9,8},{10,11... | collective-permute-start | bytes 983048 | tf_op jit(solution)/shard_map/ppermute | solution.py:336
  7.3 0.0 collective-permute-start.2
  7.3 2.5 %collective-permute-done.3.refs_1_ = bf16[320,640]{1,0:T(8,128)(2,1)S(1)} collective-permute-done((bf16[320,640]{1,0:T(8,128)(2,1)}, bf16[320,640]{1,0:T(8,128)(2,1)S(1)}, u32[]{:S(2)}, u32[]{:S(2)}) %collective-permute-start.3) | collective-permute-done | bytes 409632 | tf_op jit(solution)/shard_map/ppermute | solution.py:333
  9.8 0.1 broadcast_select_fusion
  9.9 2.1 %collective-permute-start.5 = (bf16[320,640]{1,0:T(8,128)(2,1)S(1)}, bf16[320,640]{1,0:T(8,128)(2,1)S(1)}, u32[]{:S(2)}, u32[]{:S(2)}) collective-permute-start(bf16[320,640]{1,0:T(8,128)(2,1)S(1)} %get-tuple-element.94), channel_id=1, source_target_pairs={{0,16},{4,12},{8,24},{12,4},{16,0},{20,28},{24,8},{28,20},{1,17},{... | collective-permute-start | bytes 1228808 | tf_op jit(solution)/shard_map/ppermute | solution.py:333
  12.0 1.3 %shard_map.112 = (bf16[256,640]{1,0:T(8,128)(2,1)S(1)}, bf16[128,640]{1,0:T(8,128)(2,1)S(1)}, bf16[128,640]{1,0:T(8,128)(2,1)S(1)}, f32[5,256,256]{2,1,0:T(8,128)S(1)}) custom-call(bf16[256,640]{1,0:T(8,128)(2,1)S(1)} %copy-done.1, bf16[256,640]{1,0:T(8,128)(2,1)S(1)} %copy-done.2, bf16[256,640]{1,0:T(8,128)(2,1)S(1)} %copy-done.3, s32[1,256]{1,0:T(1,128)S(1)} %copy-done.6), custom_call_target="tpu_custom_call" | custom-call | flops 167772160 | bytes 2950144 | tf_op jit(solution)/shard_map/pallas_call | solution.py:25
  13.3 0.1 collective-permute-start.7
  13.4 0.5 collective-permute-start.8
  13.9 0.9 %collective-permute-done.7 = bf16[128,640]{1,0:T(8,128)(2,1)S(1)} collective-permute-done((bf16[128,640]{1,0:T(8,128)(2,1)S(1)}, bf16[128,640]{1,0:T(8,128)(2,1)S(1)}, u32[]{:S(2)}, u32[]{:S(2)}) %collective-permute-start.7) | collective-permute-done | bytes 163872 | tf_op jit(solution)/shard_map/ppermute | solution.py:329
  14.7 0.0 collective-permute-start.6
  14.8 0.7 %collective-permute-done.1.refs_1_.near_ref = bf16[320,512]{1,0:T(8,128)(2,1)S(1)} collective-permute-done((bf16[320,512]{1,0:T(8,128)(2,1)S(1)}, bf16[320,512]{1,0:T(8,128)(2,1)S(1)}, u32[]{:S(2)}, u32[]{:S(2)}) %collective-permute-start.1) | collective-permute-done | bytes 327712 | tf_op jit(solution)/shard_map/ppermute | solution.py:336
  15.5 0.0 collective-permute-done.2.refs_5_.refs_0_.refs_2_
  15.5 0.7 %collective-permute-start.4 = (bf16[320,512]{1,0:T(8,128)(2,1)S(1)}, bf16[320,512]{1,0:T(8,128)(2,1)S(1)}, u32[]{:S(2)}, u32[]{:S(2)}) collective-permute-start(bf16[320,512]{1,0:T(8,128)(2,1)S(1)} %collective-permute-done.1.refs_1_.near_ref), channel_id=1, source_target_pairs={{1,2},{2,1},{0,4},{3,7},{5,6},{6,5},{4,0},{7,3},{9,10},{10,9},{8,1... | collective-permute-start | bytes 983048 | tf_op jit(solution)/shard_map/ppermute | solution.py:343
  16.2 0.0 collective-permute-done.8
  16.2 1.7 %collective-permute-done.5.refs_2_ = bf16[320,640]{1,0:T(8,128)(2,1)S(1)} collective-permute-done((bf16[320,640]{1,0:T(8,128)(2,1)S(1)}, bf16[320,640]{1,0:T(8,128)(2,1)S(1)}, u32[]{:S(2)}, u32[]{:S(2)}) %collective-permute-start.5) | collective-permute-done | bytes 409632 | tf_op jit(solution)/shard_map/ppermute | solution.py:333
  17.9 0.4 shard_map.117
  18.4 1.7 %collective-permute-start.10 = (bf16[320,512]{1,0:T(8,128)(2,1)S(1)}, bf16[320,512]{1,0:T(8,128)(2,1)S(1)}, u32[]{:S(2)}, u32[]{:S(2)}) collective-permute-start(bf16[320,512]{1,0:T(8,128)(2,1)S(1)} %shard_map.117), channel_id=1, source_target_pairs={{0,1},{1,0},{2,3},{3,2},{4,5},{5,4},{6,7},{7,6},{8,9},{9,8},{10,11... | collective-permute-start | bytes 983048 | tf_op jit(solution)/shard_map/ppermute | solution.py:336
  20.1 0.7 %shard_map.115 = (f32[320,640]{1,0:T(8,128)S(1)}, f32[320,640]{1,0:T(8,128)S(1)}) custom-call(bf16[320,512]{1,0:T(8,128)(2,1)S(1)} %shard_map.111.refs_0_.unit_ref, bf16[320,512]{1,0:T(8,128)(2,1)S(1)} %collective-permute-done.1.refs_1_.near_ref, bf16[256,640]{1,0:T(8,128)(2,1)S(1)} %get-tuple-element.55.own_ref.refs_1_.refs_3_.refs_2_, ...), custom_call_target="tpu_custom_call" | custom-call | flops 419430400 | bytes 2949120 | tf_op jit(solution)/shard_map/pallas_call | solution.py:25
  20.8 1.9 %collective-permute-done.6.refs_3_ = bf16[320,640]{1,0:T(8,128)(2,1)S(1)} collective-permute-done((bf16[320,640]{1,0:T(8,128)(2,1)S(1)}, bf16[320,640]{1,0:T(8,128)(2,1)S(1)}, u32[]{:S(2)}, u32[]{:S(2)}) %collective-permute-start.6) | collective-permute-done | bytes 409632 | tf_op jit(solution)/shard_map/ppermute | solution.py:333
  22.7 0.1 shard_map.113.refs_2_.refs_0_.refs_4_
  22.8 0.9 %shard_map.114.refs_5_ = f32[512,640]{1,0:T(8,128)S(1)} custom-call(bf16[320,512]{1,0:T(8,128)(2,1)S(1)} %shard_map.111.refs_0_.unit_ref, bf16[320,512]{1,0:T(8,128)(2,1)S(1)} %collective-permute-done.1.refs_1_.near_ref, bf16[4,320,640]{2,1,0:T(8,128)(2,1)S(1)} %shard_map.113.refs_2_.refs_0_.refs_4_), custom_call_target="tpu_custom_call" | custom-call | flops 419430400 | bytes 3604480 | tf_op jit(solution)/shard_map/pallas_call | solution.py:25
  23.8 0.0 collective-permute-done.4.refs_3_.refs_1_
  23.8 0.5 shard_map.116
  24.3 3.2 %collective-permute-start.9 = (bf16[320,512]{1,0:T(8,128)(2,1)S(1)}, bf16[320,512]{1,0:T(8,128)(2,1)S(1)}, u32[]{:S(2)}, u32[]{:S(2)}) collective-permute-start(bf16[320,512]{1,0:T(8,128)(2,1)S(1)} %shard_map.116), channel_id=1, source_target_pairs={{0,1},{1,0},{2,3},{3,2},{4,5},{5,4},{6,7},{7,6},{8,9},{9,8},{10,11... | collective-permute-start | bytes 983048 | tf_op jit(solution)/shard_map/ppermute | solution.py:336
  27.5 0.0 collective-permute-done.10.refs_0_.refs_3_
  27.5 0.4 shard_map.119
  27.9 0.1 collective-permute-start.13
  28.0 0.5 shard_map.118
  28.5 1.0 %collective-permute-start.11 = (bf16[160,640]{1,0:T(8,128)(2,1)S(1)}, bf16[160,640]{1,0:T(8,128)(2,1)S(1)}, u32[]{:S(2)}, u32[]{:S(2)}) collective-permute-start(bf16[160,640]{1,0:T(8,128)(2,1)S(1)} %get-tuple-element.67), channel_id=1, source_target_pairs={{0,8},{4,20},{8,0},{12,28},{16,24},{20,4},{24,16},{28,12},{1,9},{5... | collective-permute-start | bytes 614408 | tf_op jit(solution)/shard_map/ppermute | solution.py:333
  29.5 1.1 %collective-permute-start.12 = (bf16[160,640]{1,0:T(8,128)(2,1)S(1)}, bf16[160,640]{1,0:T(8,128)(2,1)S(1)}, u32[]{:S(2)}, u32[]{:S(2)}) collective-permute-start(bf16[160,640]{1,0:T(8,128)(2,1)S(1)} %get-tuple-element.68), channel_id=1, source_target_pairs={{0,8},{4,20},{8,0},{12,28},{16,24},{20,4},{24,16},{28,12},{1,9},{5... | collective-permute-start | bytes 614408 | tf_op jit(solution)/shard_map/ppermute | solution.py:333
  30.6 3.5 %collective-permute-done.9.refs_1_.refs_3_ = bf16[320,512]{1,0:T(8,128)(2,1)S(1)} collective-permute-done((bf16[320,512]{1,0:T(8,128)(2,1)S(1)}, bf16[320,512]{1,0:T(8,128)(2,1)S(1)}, u32[]{:S(2)}, u32[]{:S(2)}) %collective-permute-start.9) | collective-permute-done | bytes 327712 | tf_op jit(solution)/shard_map/ppermute | solution.py:336
  34.1 0.5 shard_map.120
  34.6 1.1 %collective-permute-start.14 = (bf16[320,640]{1,0:T(8,128)(2,1)S(1)}, bf16[320,640]{1,0:T(8,128)(2,1)S(1)}, u32[]{:S(2)}, u32[]{:S(2)}) collective-permute-start(bf16[320,640]{1,0:T(8,128)(2,1)S(1)} %get-tuple-element.69), channel_id=1, source_target_pairs={{0,8},{4,20},{8,0},{12,28},{16,24},{20,4},{24,16},{28,12},{1,9},{5... | collective-permute-start | bytes 1228808 | tf_op jit(solution)/shard_map/ppermute | solution.py:333
  35.8 0.0 collective-permute-done.13.refs_3_
  35.8 0.5 shard_map.121
  36.2 1.5 %collective-permute-start.15 = (bf16[320,512]{1,0:T(8,128)(2,1)S(1)}, bf16[320,512]{1,0:T(8,128)(2,1)S(1)}, u32[]{:S(2)}, u32[]{:S(2)}) collective-permute-start(bf16[320,512]{1,0:T(8,128)(2,1)S(1)} %shard_map.121), channel_id=1, source_target_pairs={{0,1},{1,0},{2,3},{3,2},{4,5},{5,4},{6,7},{7,6},{8,9},{9,8},{10,11... | collective-permute-start | bytes 983048 | tf_op jit(solution)/shard_map/ppermute | solution.py:336
  37.8 0.0 collective-permute-done.11.refs_3_
  37.8 0.0 collective-permute-done.12.refs_4_
  37.8 0.4 shard_map.123
  38.2 0.1 collective-permute-start.16
  38.3 4.4 %collective-permute-done.14.refs_6_ = bf16[320,640]{1,0:T(8,128)(2,1)S(1)} collective-permute-done((bf16[320,640]{1,0:T(8,128)(2,1)S(1)}, bf16[320,640]{1,0:T(8,128)(2,1)S(1)}, u32[]{:S(2)}, u32[]{:S(2)}) %collective-permute-start.14) | collective-permute-done | bytes 409632 | tf_op jit(solution)/shard_map/ppermute | solution.py:333
  42.7 0.2 shard_map.122
  42.9 1.2 %collective-permute-start.18 = (bf16[320,640]{1,0:T(8,128)(2,1)S(1)}, bf16[320,640]{1,0:T(8,128)(2,1)S(1)}, u32[]{:S(2)}, u32[]{:S(2)}) collective-permute-start(bf16[320,640]{1,0:T(8,128)(2,1)S(1)} %get-tuple-element.86), channel_id=1, source_target_pairs={{0,16},{4,12},{8,24},{12,4},{16,0},{20,28},{24,8},{28,20},{1,17},{... | collective-permute-start | bytes 1228808 | tf_op jit(solution)/shard_map/ppermute | solution.py:333
  44.1 0.9 %shard_map.124 = (f32[256,640]{1,0:T(8,128)S(1)}, bf16[256,640]{1,0:T(8,128)(2,1)S(1)}) custom-call(bf16[320,512]{1,0:T(8,128)(2,1)S(1)} %collective-permute-done.10.refs_0_.refs_3_, bf16[320,512]{1,0:T(8,128)(2,1)S(1)} %collective-permute-done.4.refs_3_.refs_1_, bf16[320,512]{1,0:T(8,128)(2,1)S(1)} %collective-permute-done.2.refs_5_.refs_0_.refs_2_, ...), custom_call_target="tpu_custom_call" | custom-call | flops 419430400 | bytes 5242880 | tf_op jit(solution)/shard_map/pallas_call | solution.py:25
  45.0 0.1 collective-permute-start.19
  45.1 0.0 collective-permute-done.15.refs_3_
  45.1 0.5 shard_map.125
  45.6 0.5 %collective-permute-start.17 = (f32[320,256]{1,0:T(8,128)S(1)}, f32[320,256]{1,0:T(8,128)S(1)}, u32[]{:S(2)}, u32[]{:S(2)}) collective-permute-start(f32[320,256]{1,0:T(8,128)S(1)} %get-tuple-element.83), channel_id=1, source_target_pairs={{0,4},{4,0},{8,12},{12,8},{16,20},{20,16},{24,28},{28,24},{1,5},{5... | collective-permute-start | bytes 983048 | tf_op jit(solution)/shard_map/ppermute | solution.py:329
  46.1 0.6 %collective-permute-done.19.other_ref = bf16[256,640]{1,0:T(8,128)(2,1)S(1)} collective-permute-done((bf16[256,640]{1,0:T(8,128)(2,1)S(1)}, bf16[256,640]{1,0:T(8,128)(2,1)S(1)}, u32[]{:S(2)}, u32[]{:S(2)}) %collective-permute-start.19) | collective-permute-done | bytes 327712 | tf_op jit(solution)/shard_map/ppermute | solution.py:329
  46.7 2.5 %shard_map.128 = (bf16[256,640]{1,0:T(8,128)(2,1)}, bf16[256,640]{1,0:T(8,128)(2,1)}, bf16[256,640]{1,0:T(8,128)(2,1)}) custom-call(bf16[256,640]{1,0:T(8,128)(2,1)S(1)} %copy-done.1, bf16[256,640]{1,0:T(8,128)(2,1)S(1)} %copy-done.2, bf16[256,640]{1,0:T(8,128)(2,1)S(1)} %copy-done.3, f32[5,256,256]{2,1,0:T(8,128)S(1)} %get-tuple-element.87.probs_ref, ...), custom_call_target="tpu_custom_call" | custom-call | flops 419430400 | bytes 4259840 | tf_op jit(solution)/shard_map/pallas_call | solution.py:25
  49.2 0.0 collective-permute-done.17.other_ref
  49.3 1.0 %shard_map.126 = bf16[256,640]{1,0:T(8,128)(2,1)} custom-call(bf16[256,640]{1,0:T(8,128)(2,1)S(1)} %copy-done.4, f32[320,256]{1,0:T(8,128)S(1)} %get-tuple-element.82.keep_ref, f32[320,256]{1,0:T(8,128)S(1)} %collective-permute-done.17.other_ref), custom_call_target="tpu_custom_call" | custom-call | bytes 1310720 | tf_op jit(solution)/shard_map/pallas_call | solution.py:25
  50.2 0.7 %collective-permute-done.18.refs_1_ = bf16[320,640]{1,0:T(8,128)(2,1)S(1)} collective-permute-done((bf16[320,640]{1,0:T(8,128)(2,1)S(1)}, bf16[320,640]{1,0:T(8,128)(2,1)S(1)}, u32[]{:S(2)}, u32[]{:S(2)}) %collective-permute-start.18) | collective-permute-done | bytes 409632 | tf_op jit(solution)/shard_map/ppermute | solution.py:333
  50.9 1.0 %shard_map.127 = f32[320,640]{1,0:T(8,128)} custom-call(f32[320,640]{1,0:T(8,128)S(1)} %get-tuple-element.85.refs_0_, bf16[320,640]{1,0:T(8,128)(2,1)S(1)} %collective-permute-done.18.refs_1_), custom_call_target="tpu_custom_call" | custom-call | bytes 2048000 | tf_op jit(solution)/shard_map/pallas_call | solution.py:25
  (12 shorter events, 0.1 us)
Async XLA Ops:
  0.6 9.2 %copy-start = (bf16[640,320]{0,1:T(8,128)(2,1)S(1)}, bf16[640,320]{0,1:T(8,128)(2,1)}, u32[]{:S(2)}) copy-start(bf16[640,320]{0,1:T(8,128)(2,1)} %param.12) | copy-start | bytes 1228804
  0.6 9.1 %collective-permute-start.3 = (bf16[320,640]{1,0:T(8,128)(2,1)}, bf16[320,640]{1,0:T(8,128)(2,1)S(1)}, u32[]{:S(2)}, u32[]{:S(2)}) collective-permute-start(bf16[320,640]{1,0:T(8,128)(2,1)} %bitcast.3), channel_id=1, source_target_pairs={{0,8},{4,20},{8,0},{12,28},{16,24},{20,4},{24,16},{28,12},{1,9},{5... | collective-permute-start | bytes 1228808 | tf_op jit(solution)/shard_map/ppermute | solution.py:333
  3.6 1.8 %collective-permute-start = (bf16[256,640]{1,0:T(8,128)(2,1)}, bf16[256,640]{1,0:T(8,128)(2,1)S(1)}, u32[]{:S(2)}, u32[]{:S(2)}) collective-permute-start(bf16[256,640]{1,0:T(8,128)(2,1)} %own_ref.1), channel_id=1, source_target_pairs={{0,4},{4,0},{8,12},{12,8},{16,20},{20,16},{24,28},{28,24},{1,5},{5... | collective-permute-start | bytes 983048 | tf_op jit(solution)/shard_map/ppermute | solution.py:329
  3.6 1.0 %copy-start.5 = (bf16[256,640]{1,0:T(8,128)(2,1)S(1)}, bf16[256,640]{1,0:T(8,128)(2,1)}, u32[]{:S(2)}) copy-start(bf16[256,640]{1,0:T(8,128)(2,1)} %own_ref.1) | copy-start | bytes 983044
  4.8 7.2 %copy-start.1 = (bf16[256,640]{1,0:T(8,128)(2,1)S(1)}, bf16[256,640]{1,0:T(8,128)(2,1)}, u32[]{:S(2)}) copy-start(bf16[256,640]{1,0:T(8,128)(2,1)} %q_ref.2) | copy-start | bytes 983044
  4.8 7.2 %copy-start.2 = (bf16[256,640]{1,0:T(8,128)(2,1)S(1)}, bf16[256,640]{1,0:T(8,128)(2,1)}, u32[]{:S(2)}) copy-start(bf16[256,640]{1,0:T(8,128)(2,1)} %k_ref.3) | copy-start | bytes 983044
  4.8 7.2 %copy-start.3 = (bf16[256,640]{1,0:T(8,128)(2,1)S(1)}, bf16[256,640]{1,0:T(8,128)(2,1)}, u32[]{:S(2)}) copy-start(bf16[256,640]{1,0:T(8,128)(2,1)} %v_ref.3) | copy-start | bytes 983044
  4.8 7.2 %copy-start.6 = (s32[1,256]{1,0:T(1,128)S(1)}, s32[1,256]{1,0:T(1,128)}, u32[]{:S(2)}) copy-start(s32[1,256]{1,0:T(1,128)} %seg_ref.1) | copy-start | bytes 3076
  5.6 9.8 %collective-permute-start.1 = (bf16[320,512]{1,0:T(8,128)(2,1)S(1)}, bf16[320,512]{1,0:T(8,128)(2,1)S(1)}, u32[]{:S(2)}, u32[]{:S(2)}) collective-permute-start(bf16[320,512]{1,0:T(8,128)(2,1)S(1)} %shard_map.111.refs_0_.unit_ref), channel_id=1, source_target_pairs={{0,1},{1,0},{2,3},{3,2},{4,5},{5,4},{6,7},{7,6},{8,9},{9,8},{10,11... | collective-permute-start | bytes 983048 | tf_op jit(solution)/shard_map/ppermute | solution.py:336
  7.3 8.2 %collective-permute-start.2 = (bf16[320,512]{1,0:T(8,128)(2,1)S(1)}, bf16[320,512]{1,0:T(8,128)(2,1)S(1)}, u32[]{:S(2)}, u32[]{:S(2)}) collective-permute-start(bf16[320,512]{1,0:T(8,128)(2,1)S(1)} %shard_map.111.refs_0_.unit_ref), channel_id=1, source_target_pairs={{1,2},{2,1},{0,4},{3,7},{5,6},{6,5},{4,0},{7,3},{9,10},{10,9},{8,1... | collective-permute-start | bytes 983048 | tf_op jit(solution)/shard_map/ppermute | solution.py:343
  9.9 8.0 %collective-permute-start.5 = (bf16[320,640]{1,0:T(8,128)(2,1)S(1)}, bf16[320,640]{1,0:T(8,128)(2,1)S(1)}, u32[]{:S(2)}, u32[]{:S(2)}) collective-permute-start(bf16[320,640]{1,0:T(8,128)(2,1)S(1)} %get-tuple-element.94), channel_id=1, source_target_pairs={{0,16},{4,12},{8,24},{12,4},{16,0},{20,28},{24,8},{28,20},{1,17},{... | collective-permute-start | bytes 1228808 | tf_op jit(solution)/shard_map/ppermute | solution.py:333
  13.3 1.5 %collective-permute-start.7 = (bf16[128,640]{1,0:T(8,128)(2,1)S(1)}, bf16[128,640]{1,0:T(8,128)(2,1)S(1)}, u32[]{:S(2)}, u32[]{:S(2)}) collective-permute-start(bf16[128,640]{1,0:T(8,128)(2,1)S(1)} %get-tuple-element.56), channel_id=1, source_target_pairs={{0,4},{4,0},{8,12},{12,8},{16,20},{20,16},{24,28},{28,24},{1,5},{5... | collective-permute-start | bytes 491528 | tf_op jit(solution)/shard_map/ppermute | solution.py:329
  13.4 2.8 %collective-permute-start.8 = (bf16[128,640]{1,0:T(8,128)(2,1)S(1)}, bf16[128,640]{1,0:T(8,128)(2,1)S(1)}, u32[]{:S(2)}, u32[]{:S(2)}) collective-permute-start(bf16[128,640]{1,0:T(8,128)(2,1)S(1)} %get-tuple-element.57), channel_id=1, source_target_pairs={{0,4},{4,0},{8,12},{12,8},{16,20},{20,16},{24,28},{28,24},{1,5},{5... | collective-permute-start | bytes 491528 | tf_op jit(solution)/shard_map/ppermute | solution.py:329
  14.7 8.0 %collective-permute-start.6 = (bf16[320,640]{1,0:T(8,128)(2,1)S(1)}, bf16[320,640]{1,0:T(8,128)(2,1)S(1)}, u32[]{:S(2)}, u32[]{:S(2)}) collective-permute-start(bf16[320,640]{1,0:T(8,128)(2,1)S(1)} %get-tuple-element.93), channel_id=1, source_target_pairs={{0,16},{4,12},{8,24},{12,4},{16,0},{20,28},{24,8},{28,20},{1,17},{... | collective-permute-start | bytes 1228808 | tf_op jit(solution)/shard_map/ppermute | solution.py:333
  15.5 8.3 %collective-permute-start.4 = (bf16[320,512]{1,0:T(8,128)(2,1)S(1)}, bf16[320,512]{1,0:T(8,128)(2,1)S(1)}, u32[]{:S(2)}, u32[]{:S(2)}) collective-permute-start(bf16[320,512]{1,0:T(8,128)(2,1)S(1)} %collective-permute-done.1.refs_1_.near_ref), channel_id=1, source_target_pairs={{1,2},{2,1},{0,4},{3,7},{5,6},{6,5},{4,0},{7,3},{9,10},{10,9},{8,1... | collective-permute-start | bytes 983048 | tf_op jit(solution)/shard_map/ppermute | solution.py:343
  18.4 9.1 %collective-permute-start.10 = (bf16[320,512]{1,0:T(8,128)(2,1)S(1)}, bf16[320,512]{1,0:T(8,128)(2,1)S(1)}, u32[]{:S(2)}, u32[]{:S(2)}) collective-permute-start(bf16[320,512]{1,0:T(8,128)(2,1)S(1)} %shard_map.117), channel_id=1, source_target_pairs={{0,1},{1,0},{2,3},{3,2},{4,5},{5,4},{6,7},{7,6},{8,9},{9,8},{10,11... | collective-permute-start | bytes 983048 | tf_op jit(solution)/shard_map/ppermute | solution.py:336
  24.3 9.9 %collective-permute-start.9 = (bf16[320,512]{1,0:T(8,128)(2,1)S(1)}, bf16[320,512]{1,0:T(8,128)(2,1)S(1)}, u32[]{:S(2)}, u32[]{:S(2)}) collective-permute-start(bf16[320,512]{1,0:T(8,128)(2,1)S(1)} %shard_map.116), channel_id=1, source_target_pairs={{0,1},{1,0},{2,3},{3,2},{4,5},{5,4},{6,7},{7,6},{8,9},{9,8},{10,11... | collective-permute-start | bytes 983048 | tf_op jit(solution)/shard_map/ppermute | solution.py:336
  27.9 7.8 %collective-permute-start.13 = (bf16[320,512]{1,0:T(8,128)(2,1)S(1)}, bf16[320,512]{1,0:T(8,128)(2,1)S(1)}, u32[]{:S(2)}, u32[]{:S(2)}) collective-permute-start(bf16[320,512]{1,0:T(8,128)(2,1)S(1)} %shard_map.119), channel_id=1, source_target_pairs={{1,2},{2,1},{0,4},{3,7},{5,6},{6,5},{4,0},{7,3},{9,10},{10,9},{8,1... | collective-permute-start | bytes 983048 | tf_op jit(solution)/shard_map/ppermute | solution.py:343
  28.5 9.2 %collective-permute-start.11 = (bf16[160,640]{1,0:T(8,128)(2,1)S(1)}, bf16[160,640]{1,0:T(8,128)(2,1)S(1)}, u32[]{:S(2)}, u32[]{:S(2)}) collective-permute-start(bf16[160,640]{1,0:T(8,128)(2,1)S(1)} %get-tuple-element.67), channel_id=1, source_target_pairs={{0,8},{4,20},{8,0},{12,28},{16,24},{20,4},{24,16},{28,12},{1,9},{5... | collective-permute-start | bytes 614408 | tf_op jit(solution)/shard_map/ppermute | solution.py:333
  29.5 8.2 %collective-permute-start.12 = (bf16[160,640]{1,0:T(8,128)(2,1)S(1)}, bf16[160,640]{1,0:T(8,128)(2,1)S(1)}, u32[]{:S(2)}, u32[]{:S(2)}) collective-permute-start(bf16[160,640]{1,0:T(8,128)(2,1)S(1)} %get-tuple-element.68), channel_id=1, source_target_pairs={{0,8},{4,20},{8,0},{12,28},{16,24},{20,4},{24,16},{28,12},{1,9},{5... | collective-permute-start | bytes 614408 | tf_op jit(solution)/shard_map/ppermute | solution.py:333
  34.6 8.0 %collective-permute-start.14 = (bf16[320,640]{1,0:T(8,128)(2,1)S(1)}, bf16[320,640]{1,0:T(8,128)(2,1)S(1)}, u32[]{:S(2)}, u32[]{:S(2)}) collective-permute-start(bf16[320,640]{1,0:T(8,128)(2,1)S(1)} %get-tuple-element.69), channel_id=1, source_target_pairs={{0,8},{4,20},{8,0},{12,28},{16,24},{20,4},{24,16},{28,12},{1,9},{5... | collective-permute-start | bytes 1228808 | tf_op jit(solution)/shard_map/ppermute | solution.py:333
  36.2 8.9 %collective-permute-start.15 = (bf16[320,512]{1,0:T(8,128)(2,1)S(1)}, bf16[320,512]{1,0:T(8,128)(2,1)S(1)}, u32[]{:S(2)}, u32[]{:S(2)}) collective-permute-start(bf16[320,512]{1,0:T(8,128)(2,1)S(1)} %shard_map.121), channel_id=1, source_target_pairs={{0,1},{1,0},{2,3},{3,2},{4,5},{5,4},{6,7},{7,6},{8,9},{9,8},{10,11... | collective-permute-start | bytes 983048 | tf_op jit(solution)/shard_map/ppermute | solution.py:336
  38.2 6.9 %collective-permute-start.16 = (bf16[320,512]{1,0:T(8,128)(2,1)S(1)}, bf16[320,512]{1,0:T(8,128)(2,1)S(1)}, u32[]{:S(2)}, u32[]{:S(2)}) collective-permute-start(bf16[320,512]{1,0:T(8,128)(2,1)S(1)} %shard_map.123), channel_id=1, source_target_pairs={{1,2},{2,1},{0,4},{3,7},{5,6},{6,5},{4,0},{7,3},{9,10},{10,9},{8,1... | collective-permute-start | bytes 983048 | tf_op jit(solution)/shard_map/ppermute | solution.py:343
  42.9 8.0 %collective-permute-start.18 = (bf16[320,640]{1,0:T(8,128)(2,1)S(1)}, bf16[320,640]{1,0:T(8,128)(2,1)S(1)}, u32[]{:S(2)}, u32[]{:S(2)}) collective-permute-start(bf16[320,640]{1,0:T(8,128)(2,1)S(1)} %get-tuple-element.86), channel_id=1, source_target_pairs={{0,16},{4,12},{8,24},{12,4},{16,0},{20,28},{24,8},{28,20},{1,17},{... | collective-permute-start | bytes 1228808 | tf_op jit(solution)/shard_map/ppermute | solution.py:333
  45.0 1.7 %collective-permute-start.19 = (bf16[256,640]{1,0:T(8,128)(2,1)S(1)}, bf16[256,640]{1,0:T(8,128)(2,1)S(1)}, u32[]{:S(2)}, u32[]{:S(2)}) collective-permute-start(bf16[256,640]{1,0:T(8,128)(2,1)S(1)} %get-tuple-element.89), channel_id=1, source_target_pairs={{0,4},{4,0},{8,12},{12,8},{16,20},{20,16},{24,28},{28,24},{1,5},{5... | collective-permute-start | bytes 983048 | tf_op jit(solution)/shard_map/ppermute | solution.py:329
  45.6 3.7 %collective-permute-start.17 = (f32[320,256]{1,0:T(8,128)S(1)}, f32[320,256]{1,0:T(8,128)S(1)}, u32[]{:S(2)}, u32[]{:S(2)}) collective-permute-start(f32[320,256]{1,0:T(8,128)S(1)} %get-tuple-element.83), channel_id=1, source_target_pairs={{0,4},{4,0},{8,12},{12,8},{16,20},{20,16},{24,28},{28,24},{1,5},{5... | collective-permute-start | bytes 983048 | tf_op jit(solution)/shard_map/ppermute | solution.py:329
  46.7 2.5 %copy-start.4 = (bf16[256,640]{1,0:T(8,128)(2,1)S(1)}, bf16[256,640]{1,0:T(8,128)(2,1)}, u32[]{:S(2)}) copy-start(bf16[256,640]{1,0:T(8,128)(2,1)} %residual_ref.1) | copy-start | bytes 983044

commit v7 on v6

--- a/solution.py
+++ b/solution.py
@@ -369,7 +369,7 @@
 
         w_near = core_swap(w_own, True)
         unit = make_unit(cotangent, cot_other, strips)
-        near, inner_far = pair_swap(unit), mid_swap(unit)
+        inner_far, near = mid_swap(unit), pair_swap(unit)
 
         first = own_bits()[0]
         far_soon = (late_slot(group) & first) == first

time: 52 us -> 52 us (level)
  no operation moved by 1% of the time
where the time goes in v7:
time: 52 us; the launch traced here: 51.9 us
  starting transfers between devices  19.7 us (38%)
  waiting for transfers between devices  17.5 us (34%)
  Pallas kernels  12.7 us (24%)
  local copies, waits for them, and re-layouts  1.04 us (2%)
  between operations  0.9 us (2%)
    pallas_call x19, Pallas kernels, call(): pl.pallas_call(kernel, out_shape=tuple(outs), in_specs=[pl.BlockSpec(memo...  12.7 us
    ppermute x7, waiting for transfers between devices, core_swap(): lax.ppermute(value, 'blk', [(i, i ^ group * bits[i % 2]) for i in range(b...  11.2 us
    ppermute x7, starting transfers between devices, core_swap(): lax.ppermute(value, 'blk', [(i, i ^ group * bits[i % 2]) for i in range(b...  9.55 us
    ppermute x4, starting transfers between devices, pair_swap(): return lax.ppermute(value, 'shard', [(0, 1), (1, 0), (2, 3), (3, 2)])  8.11 us
    ppermute x4, waiting for transfers between devices, pair_swap(): return lax.ppermute(value, 'shard', [(0, 1), (1, 0), (2, 3), (3, 2)])  4.19 us
    ppermute x5, waiting for transfers between devices, swap(): return lax.ppermute(value, 'blk', [(i, i ^ bit) for i in range(blk)])  2.11 us
    ppermute x5, starting transfers between devices, swap(): return lax.ppermute(value, 'blk', [(i, i ^ bit) for i in range(blk)])  1.19 us
  transfers between devices with their start and end apart: 20, of which 10 were waited for; matrix products, arithmetic and copies ran while one was open for 0% of the time, Pallas kernels for 23%

profile of v7, /device:TPU:0, one launch (start us, length us, event | category | flops | bytes accessed | tf_op | source)
XLA Modules:
  0.0 51.9 jit_solution(12407737792092897194)
XLA Ops:
  0.6 3.0 %collective-permute-start.3 = (bf16[320,640]{1,0:T(8,128)(2,1)}, bf16[320,640]{1,0:T(8,128)(2,1)S(1)}, u32[]{:S(2)}, u32[]{:S(2)}) collective-permute-start(bf16[320,640]{1,0:T(8,128)(2,1)} %bitcast.3), channel_id=1, source_target_pairs={{0,8},{4,20},{8,0},{12,28},{16,24},{20,4},{24,16},{28,12},{1,9},{5... | collective-permute-start | bytes 1228808 | tf_op jit(solution)/shard_map/ppermute | solution.py:333
  3.6 0.0 collective-permute-start
  3.7 1.0 %copy-done.5 = bf16[256,640]{1,0:T(8,128)(2,1)S(1)} copy-done((bf16[256,640]{1,0:T(8,128)(2,1)S(1)}, bf16[256,640]{1,0:T(8,128)(2,1)}, u32[]{:S(2)}) %copy-start.5) | copy-done | bytes 327704
  4.6 0.1 shard_map.110.own_ref
  4.8 0.0 copy-start.1
  4.8 0.0 copy-start.2
  4.8 0.0 copy-start.3
  4.8 0.0 copy-start.6
  4.8 0.6 %collective-permute-done.other_ref = bf16[256,640]{1,0:T(8,128)(2,1)S(1)} collective-permute-done((bf16[256,640]{1,0:T(8,128)(2,1)}, bf16[256,640]{1,0:T(8,128)(2,1)S(1)}, u32[]{:S(2)}, u32[]{:S(2)}) %collective-permute-start) | collective-permute-done | bytes 327712 | tf_op jit(solution)/shard_map/ppermute | solution.py:329
  5.5 0.1 shard_map.111.refs_0_.unit_ref
  5.6 1.6 %collective-permute-start.1 = (bf16[320,512]{1,0:T(8,128)(2,1)S(1)}, bf16[320,512]{1,0:T(8,128)(2,1)S(1)}, u32[]{:S(2)}, u32[]{:S(2)}) collective-permute-start(bf16[320,512]{1,0:T(8,128)(2,1)S(1)} %shard_map.111.refs_0_.unit_ref), channel_id=1, source_target_pairs={{0,1},{1,0},{2,3},{3,2},{4,5},{5,4},{6,7},{7,6},{8,9},{9,8},{10,11... | collective-permute-start | bytes 983048 | tf_op jit(solution)/shard_map/ppermute | solution.py:336
  7.3 0.0 collective-permute-start.2
  7.3 2.5 %collective-permute-done.3.refs_1_ = bf16[320,640]{1,0:T(8,128)(2,1)S(1)} collective-permute-done((bf16[320,640]{1,0:T(8,128)(2,1)}, bf16[320,640]{1,0:T(8,128)(2,1)S(1)}, u32[]{:S(2)}, u32[]{:S(2)}) %collective-permute-start.3) | collective-permute-done | bytes 409632 | tf_op jit(solution)/shard_map/ppermute | solution.py:333
  9.8 0.1 broadcast_select_fusion
  9.9 2.1 %collective-permute-start.5 = (bf16[320,640]{1,0:T(8,128)(2,1)S(1)}, bf16[320,640]{1,0:T(8,128)(2,1)S(1)}, u32[]{:S(2)}, u32[]{:S(2)}) collective-permute-start(bf16[320,640]{1,0:T(8,128)(2,1)S(1)} %get-tuple-element.94), channel_id=1, source_target_pairs={{0,16},{4,12},{8,24},{12,4},{16,0},{20,28},{24,8},{28,20},{1,17},{... | collective-permute-start | bytes 1228808 | tf_op jit(solution)/shard_map/ppermute | solution.py:333
  12.0 1.3 %shard_map.112 = (bf16[256,640]{1,0:T(8,128)(2,1)S(1)}, bf16[128,640]{1,0:T(8,128)(2,1)S(1)}, bf16[128,640]{1,0:T(8,128)(2,1)S(1)}, f32[5,256,256]{2,1,0:T(8,128)S(1)}) custom-call(bf16[256,640]{1,0:T(8,128)(2,1)S(1)} %copy-done.1, bf16[256,640]{1,0:T(8,128)(2,1)S(1)} %copy-done.2, bf16[256,640]{1,0:T(8,128)(2,1)S(1)} %copy-done.3, s32[1,256]{1,0:T(1,128)S(1)} %copy-done.6), custom_call_target="tpu_custom_call" | custom-call | flops 167772160 | bytes 2950144 | tf_op jit(solution)/shard_map/pallas_call | solution.py:25
  13.3 0.1 collective-permute-start.7
  13.4 0.5 collective-permute-start.8
  13.9 0.9 %collective-permute-done.7 = bf16[128,640]{1,0:T(8,128)(2,1)S(1)} collective-permute-done((bf16[128,640]{1,0:T(8,128)(2,1)S(1)}, bf16[128,640]{1,0:T(8,128)(2,1)S(1)}, u32[]{:S(2)}, u32[]{:S(2)}) %collective-permute-start.7) | collective-permute-done | bytes 163872 | tf_op jit(solution)/shard_map/ppermute | solution.py:329
  14.7 0.0 collective-permute-start.6
  14.8 0.7 %collective-permute-done.1.refs_1_.near_ref = bf16[320,512]{1,0:T(8,128)(2,1)S(1)} collective-permute-done((bf16[320,512]{1,0:T(8,128)(2,1)S(1)}, bf16[320,512]{1,0:T(8,128)(2,1)S(1)}, u32[]{:S(2)}, u32[]{:S(2)}) %collective-permute-start.1) | collective-permute-done | bytes 327712 | tf_op jit(solution)/shard_map/ppermute | solution.py:336
  15.5 0.0 collective-permute-done.2.refs_5_.refs_0_.refs_2_
  15.5 0.7 %collective-permute-start.4 = (bf16[320,512]{1,0:T(8,128)(2,1)S(1)}, bf16[320,512]{1,0:T(8,128)(2,1)S(1)}, u32[]{:S(2)}, u32[]{:S(2)}) collective-permute-start(bf16[320,512]{1,0:T(8,128)(2,1)S(1)} %collective-permute-done.1.refs_1_.near_ref), channel_id=1, source_target_pairs={{1,2},{2,1},{0,4},{3,7},{5,6},{6,5},{4,0},{7,3},{9,10},{10,9},{8,1... | collective-permute-start | bytes 983048 | tf_op jit(solution)/shard_map/ppermute | solution.py:343
  16.2 0.0 collective-permute-done.8
  16.2 1.7 %collective-permute-done.5.refs_2_ = bf16[320,640]{1,0:T(8,128)(2,1)S(1)} collective-permute-done((bf16[320,640]{1,0:T(8,128)(2,1)S(1)}, bf16[320,640]{1,0:T(8,128)(2,1)S(1)}, u32[]{:S(2)}, u32[]{:S(2)}) %collective-permute-start.5) | collective-permute-done | bytes 409632 | tf_op jit(solution)/shard_map/ppermute | solution.py:333
  17.9 0.4 shard_map.117
  18.4 1.7 %collective-permute-start.10 = (bf16[320,512]{1,0:T(8,128)(2,1)S(1)}, bf16[320,512]{1,0:T(8,128)(2,1)S(1)}, u32[]{:S(2)}, u32[]{:S(2)}) collective-permute-start(bf16[320,512]{1,0:T(8,128)(2,1)S(1)} %shard_map.117), channel_id=1, source_target_pairs={{0,1},{1,0},{2,3},{3,2},{4,5},{5,4},{6,7},{7,6},{8,9},{9,8},{10,11... | collective-permute-start | bytes 983048 | tf_op jit(solution)/shard_map/ppermute | solution.py:336
  20.1 0.7 %shard_map.115 = (f32[320,640]{1,0:T(8,128)S(1)}, f32[320,640]{1,0:T(8,128)S(1)}) custom-call(bf16[320,512]{1,0:T(8,128)(2,1)S(1)} %shard_map.111.refs_0_.unit_ref, bf16[320,512]{1,0:T(8,128)(2,1)S(1)} %collective-permute-done.1.refs_1_.near_ref, bf16[256,640]{1,0:T(8,128)(2,1)S(1)} %get-tuple-element.55.own_ref.refs_1_.refs_3_.refs_2_, ...), custom_call_target="tpu_custom_call" | custom-call | flops 419430400 | bytes 2949120 | tf_op jit(solution)/shard_map/pallas_call | solution.py:25
  20.8 1.9 %collective-permute-done.6.refs_3_ = bf16[320,640]{1,0:T(8,128)(2,1)S(1)} collective-permute-done((bf16[320,640]{1,0:T(8,128)(2,1)S(1)}, bf16[320,640]{1,0:T(8,128)(2,1)S(1)}, u32[]{:S(2)}, u32[]{:S(2)}) %collective-permute-start.6) | collective-permute-done | bytes 409632 | tf_op jit(solution)/shard_map/ppermute | solution.py:333
  22.7 0.1 shard_map.113.refs_2_.refs_0_.refs_4_
  22.8 0.9 %shard_map.114.refs_5_ = f32[512,640]{1,0:T(8,128)S(1)} custom-call(bf16[320,512]{1,0:T(8,128)(2,1)S(1)} %shard_map.111.refs_0_.unit_ref, bf16[320,512]{1,0:T(8,128)(2,1)S(1)} %collective-permute-done.1.refs_1_.near_ref, bf16[4,320,640]{2,1,0:T(8,128)(2,1)S(1)} %shard_map.113.refs_2_.refs_0_.refs_4_), custom_call_target="tpu_custom_call" | custom-call | flops 419430400 | bytes 3604480 | tf_op jit(solution)/shard_map/pallas_call | solution.py:25
  23.8 0.0 collective-permute-done.4.refs_3_.refs_1_
  23.8 0.5 shard_map.116
  24.3 3.2 %collective-permute-start.9 = (bf16[320,512]{1,0:T(8,128)(2,1)S(1)}, bf16[320,512]{1,0:T(8,128)(2,1)S(1)}, u32[]{:S(2)}, u32[]{:S(2)}) collective-permute-start(bf16[320,512]{1,0:T(8,128)(2,1)S(1)} %shard_map.116), channel_id=1, source_target_pairs={{0,1},{1,0},{2,3},{3,2},{4,5},{5,4},{6,7},{7,6},{8,9},{9,8},{10,11... | collective-permute-start | bytes 983048 | tf_op jit(solution)/shard_map/ppermute | solution.py:336
  27.5 0.0 collective-permute-done.10.refs_0_.refs_3_
  27.5 0.4 shard_map.119
  27.9 0.1 collective-permute-start.13
  28.0 0.5 shard_map.118
  28.5 1.0 %collective-permute-start.11 = (bf16[160,640]{1,0:T(8,128)(2,1)S(1)}, bf16[160,640]{1,0:T(8,128)(2,1)S(1)}, u32[]{:S(2)}, u32[]{:S(2)}) collective-permute-start(bf16[160,640]{1,0:T(8,128)(2,1)S(1)} %get-tuple-element.67), channel_id=1, source_target_pairs={{0,8},{4,20},{8,0},{12,28},{16,24},{20,4},{24,16},{28,12},{1,9},{5... | collective-permute-start | bytes 614408 | tf_op jit(solution)/shard_map/ppermute | solution.py:333
  29.5 1.1 %collective-permute-start.12 = (bf16[160,640]{1,0:T(8,128)(2,1)S(1)}, bf16[160,640]{1,0:T(8,128)(2,1)S(1)}, u32[]{:S(2)}, u32[]{:S(2)}) collective-permute-start(bf16[160,640]{1,0:T(8,128)(2,1)S(1)} %get-tuple-element.68), channel_id=1, source_target_pairs={{0,8},{4,20},{8,0},{12,28},{16,24},{20,4},{24,16},{28,12},{1,9},{5... | collective-permute-start | bytes 614408 | tf_op jit(solution)/shard_map/ppermute | solution.py:333
  30.6 3.5 %collective-permute-done.9.refs_1_.refs_3_ = bf16[320,512]{1,0:T(8,128)(2,1)S(1)} collective-permute-done((bf16[320,512]{1,0:T(8,128)(2,1)S(1)}, bf16[320,512]{1,0:T(8,128)(2,1)S(1)}, u32[]{:S(2)}, u32[]{:S(2)}) %collective-permute-start.9) | collective-permute-done | bytes 327712 | tf_op jit(solution)/shard_map/ppermute | solution.py:336
  34.1 0.5 shard_map.120
  34.6 1.1 %collective-permute-start.14 = (bf16[320,640]{1,0:T(8,128)(2,1)S(1)}, bf16[320,640]{1,0:T(8,128)(2,1)S(1)}, u32[]{:S(2)}, u32[]{:S(2)}) collective-permute-start(bf16[320,640]{1,0:T(8,128)(2,1)S(1)} %get-tuple-element.69), channel_id=1, source_target_pairs={{0,8},{4,20},{8,0},{12,28},{16,24},{20,4},{24,16},{28,12},{1,9},{5... | collective-permute-start | bytes 1228808 | tf_op jit(solution)/shard_map/ppermute | solution.py:333
  35.8 0.0 collective-permute-done.13.refs_3_
  35.8 0.5 shard_map.121
  36.2 1.5 %collective-permute-start.15 = (bf16[320,512]{1,0:T(8,128)(2,1)S(1)}, bf16[320,512]{1,0:T(8,128)(2,1)S(1)}, u32[]{:S(2)}, u32[]{:S(2)}) collective-permute-start(bf16[320,512]{1,0:T(8,128)(2,1)S(1)} %shard_map.121), channel_id=1, source_target_pairs={{0,1},{1,0},{2,3},{3,2},{4,5},{5,4},{6,7},{7,6},{8,9},{9,8},{10,11... | collective-permute-start | bytes 983048 | tf_op jit(solution)/shard_map/ppermute | solution.py:336
  37.8 0.0 collective-permute-done.11.refs_3_
  37.8 0.0 collective-permute-done.12.refs_4_
  37.8 0.4 shard_map.123
  38.2 0.1 collective-permute-start.16
  38.3 4.4 %collective-permute-done.14.refs_6_ = bf16[320,640]{1,0:T(8,128)(2,1)S(1)} collective-permute-done((bf16[320,640]{1,0:T(8,128)(2,1)S(1)}, bf16[320,640]{1,0:T(8,128)(2,1)S(1)}, u32[]{:S(2)}, u32[]{:S(2)}) %collective-permute-start.14) | collective-permute-done | bytes 409632 | tf_op jit(solution)/shard_map/ppermute | solution.py:333
  42.7 0.2 shard_map.122
  42.9 1.2 %collective-permute-start.18 = (bf16[320,640]{1,0:T(8,128)(2,1)S(1)}, bf16[320,640]{1,0:T(8,128)(2,1)S(1)}, u32[]{:S(2)}, u32[]{:S(2)}) collective-permute-start(bf16[320,640]{1,0:T(8,128)(2,1)S(1)} %get-tuple-element.86), channel_id=1, source_target_pairs={{0,16},{4,12},{8,24},{12,4},{16,0},{20,28},{24,8},{28,20},{1,17},{... | collective-permute-start | bytes 1228808 | tf_op jit(solution)/shard_map/ppermute | solution.py:333
  44.1 0.9 %shard_map.124 = (f32[256,640]{1,0:T(8,128)S(1)}, bf16[256,640]{1,0:T(8,128)(2,1)S(1)}) custom-call(bf16[320,512]{1,0:T(8,128)(2,1)S(1)} %collective-permute-done.10.refs_0_.refs_3_, bf16[320,512]{1,0:T(8,128)(2,1)S(1)} %collective-permute-done.4.refs_3_.refs_1_, bf16[320,512]{1,0:T(8,128)(2,1)S(1)} %collective-permute-done.2.refs_5_.refs_0_.refs_2_, ...), custom_call_target="tpu_custom_call" | custom-call | flops 419430400 | bytes 5242880 | tf_op jit(solution)/shard_map/pallas_call | solution.py:25
  45.0 0.1 collective-permute-start.19
  45.1 0.0 collective-permute-done.15.refs_3_
  45.1 0.5 shard_map.125
  45.6 0.5 %collective-permute-start.17 = (f32[320,256]{1,0:T(8,128)S(1)}, f32[320,256]{1,0:T(8,128)S(1)}, u32[]{:S(2)}, u32[]{:S(2)}) collective-permute-start(f32[320,256]{1,0:T(8,128)S(1)} %get-tuple-element.83), channel_id=1, source_target_pairs={{0,4},{4,0},{8,12},{12,8},{16,20},{20,16},{24,28},{28,24},{1,5},{5... | collective-permute-start | bytes 983048 | tf_op jit(solution)/shard_map/ppermute | solution.py:329
  46.1 0.6 %collective-permute-done.19.other_ref = bf16[256,640]{1,0:T(8,128)(2,1)S(1)} collective-permute-done((bf16[256,640]{1,0:T(8,128)(2,1)S(1)}, bf16[256,640]{1,0:T(8,128)(2,1)S(1)}, u32[]{:S(2)}, u32[]{:S(2)}) %collective-permute-start.19) | collective-permute-done | bytes 327712 | tf_op jit(solution)/shard_map/ppermute | solution.py:329
  46.7 2.5 %shard_map.128 = (bf16[256,640]{1,0:T(8,128)(2,1)}, bf16[256,640]{1,0:T(8,128)(2,1)}, bf16[256,640]{1,0:T(8,128)(2,1)}) custom-call(bf16[256,640]{1,0:T(8,128)(2,1)S(1)} %copy-done.1, bf16[256,640]{1,0:T(8,128)(2,1)S(1)} %copy-done.2, bf16[256,640]{1,0:T(8,128)(2,1)S(1)} %copy-done.3, f32[5,256,256]{2,1,0:T(8,128)S(1)} %get-tuple-element.87.probs_ref, ...), custom_call_target="tpu_custom_call" | custom-call | flops 419430400 | bytes 4259840 | tf_op jit(solution)/shard_map/pallas_call | solution.py:25
  49.2 0.0 collective-permute-done.17.other_ref
  49.3 1.0 %shard_map.126 = bf16[256,640]{1,0:T(8,128)(2,1)} custom-call(bf16[256,640]{1,0:T(8,128)(2,1)S(1)} %copy-done.4, f32[320,256]{1,0:T(8,128)S(1)} %get-tuple-element.82.keep_ref, f32[320,256]{1,0:T(8,128)S(1)} %collective-permute-done.17.other_ref), custom_call_target="tpu_custom_call" | custom-call | bytes 1310720 | tf_op jit(solution)/shard_map/pallas_call | solution.py:25
  50.2 0.7 %collective-permute-done.18.refs_1_ = bf16[320,640]{1,0:T(8,128)(2,1)S(1)} collective-permute-done((bf16[320,640]{1,0:T(8,128)(2,1)S(1)}, bf16[320,640]{1,0:T(8,128)(2,1)S(1)}, u32[]{:S(2)}, u32[]{:S(2)}) %collective-permute-start.18) | collective-permute-done | bytes 409632 | tf_op jit(solution)/shard_map/ppermute | solution.py:333
  50.9 1.0 %shard_map.127 = f32[320,640]{1,0:T(8,128)} custom-call(f32[320,640]{1,0:T(8,128)S(1)} %get-tuple-element.85.refs_0_, bf16[320,640]{1,0:T(8,128)(2,1)S(1)} %collective-permute-done.18.refs_1_), custom_call_target="tpu_custom_call" | custom-call | bytes 2048000 | tf_op jit(solution)/shard_map/pallas_call | solution.py:25
  (12 shorter events, 0.1 us)
Async XLA Ops:
  0.6 9.2 %copy-start = (bf16[640,320]{0,1:T(8,128)(2,1)S(1)}, bf16[640,320]{0,1:T(8,128)(2,1)}, u32[]{:S(2)}) copy-start(bf16[640,320]{0,1:T(8,128)(2,1)} %param.12) | copy-start | bytes 1228804
  0.6 9.1 %collective-permute-start.3 = (bf16[320,640]{1,0:T(8,128)(2,1)}, bf16[320,640]{1,0:T(8,128)(2,1)S(1)}, u32[]{:S(2)}, u32[]{:S(2)}) collective-permute-start(bf16[320,640]{1,0:T(8,128)(2,1)} %bitcast.3), channel_id=1, source_target_pairs={{0,8},{4,20},{8,0},{12,28},{16,24},{20,4},{24,16},{28,12},{1,9},{5... | collective-permute-start | bytes 1228808 | tf_op jit(solution)/shard_map/ppermute | solution.py:333
  3.6 1.8 %collective-permute-start = (bf16[256,640]{1,0:T(8,128)(2,1)}, bf16[256,640]{1,0:T(8,128)(2,1)S(1)}, u32[]{:S(2)}, u32[]{:S(2)}) collective-permute-start(bf16[256,640]{1,0:T(8,128)(2,1)} %own_ref.1), channel_id=1, source_target_pairs={{0,4},{4,0},{8,12},{12,8},{16,20},{20,16},{24,28},{28,24},{1,5},{5... | collective-permute-start | bytes 983048 | tf_op jit(solution)/shard_map/ppermute | solution.py:329
  3.6 1.0 %copy-start.5 = (bf16[256,640]{1,0:T(8,128)(2,1)S(1)}, bf16[256,640]{1,0:T(8,128)(2,1)}, u32[]{:S(2)}) copy-start(bf16[256,640]{1,0:T(8,128)(2,1)} %own_ref.1) | copy-start | bytes 983044
  4.8 7.2 %copy-start.1 = (bf16[256,640]{1,0:T(8,128)(2,1)S(1)}, bf16[256,640]{1,0:T(8,128)(2,1)}, u32[]{:S(2)}) copy-start(bf16[256,640]{1,0:T(8,128)(2,1)} %q_ref.2) | copy-start | bytes 983044
  4.8 7.2 %copy-start.2 = (bf16[256,640]{1,0:T(8,128)(2,1)S(1)}, bf16[256,640]{1,0:T(8,128)(2,1)}, u32[]{:S(2)}) copy-start(bf16[256,640]{1,0:T(8,128)(2,1)} %k_ref.3) | copy-start | bytes 983044
  4.8 7.2 %copy-start.3 = (bf16[256,640]{1,0:T(8,128)(2,1)S(1)}, bf16[256,640]{1,0:T(8,128)(2,1)}, u32[]{:S(2)}) copy-start(bf16[256,640]{1,0:T(8,128)(2,1)} %v_ref.3) | copy-start | bytes 983044
  4.8 7.2 %copy-start.6 = (s32[1,256]{1,0:T(1,128)S(1)}, s32[1,256]{1,0:T(1,128)}, u32[]{:S(2)}) copy-start(s32[1,256]{1,0:T(1,128)} %seg_ref.1) | copy-start | bytes 3076
  5.6 9.8 %collective-permute-start.1 = (bf16[320,512]{1,0:T(8,128)(2,1)S(1)}, bf16[320,512]{1,0:T(8,128)(2,1)S(1)}, u32[]{:S(2)}, u32[]{:S(2)}) collective-permute-start(bf16[320,512]{1,0:T(8,128)(2,1)S(1)} %shard_map.111.refs_0_.unit_ref), channel_id=1, source_target_pairs={{0,1},{1,0},{2,3},{3,2},{4,5},{5,4},{6,7},{7,6},{8,9},{9,8},{10,11... | collective-permute-start | bytes 983048 | tf_op jit(solution)/shard_map/ppermute | solution.py:336
  7.3 8.2 %collective-permute-start.2 = (bf16[320,512]{1,0:T(8,128)(2,1)S(1)}, bf16[320,512]{1,0:T(8,128)(2,1)S(1)}, u32[]{:S(2)}, u32[]{:S(2)}) collective-permute-start(bf16[320,512]{1,0:T(8,128)(2,1)S(1)} %shard_map.111.refs_0_.unit_ref), channel_id=1, source_target_pairs={{1,2},{2,1},{0,4},{3,7},{5,6},{6,5},{4,0},{7,3},{9,10},{10,9},{8,1... | collective-permute-start | bytes 983048 | tf_op jit(solution)/shard_map/ppermute | solution.py:343
  9.9 8.0 %collective-permute-start.5 = (bf16[320,640]{1,0:T(8,128)(2,1)S(1)}, bf16[320,640]{1,0:T(8,128)(2,1)S(1)}, u32[]{:S(2)}, u32[]{:S(2)}) collective-permute-start(bf16[320,640]{1,0:T(8,128)(2,1)S(1)} %get-tuple-element.94), channel_id=1, source_target_pairs={{0,16},{4,12},{8,24},{12,4},{16,0},{20,28},{24,8},{28,20},{1,17},{... | collective-permute-start | bytes 1228808 | tf_op jit(solution)/shard_map/ppermute | solution.py:333
  13.3 1.5 %collective-permute-start.7 = (bf16[128,640]{1,0:T(8,128)(2,1)S(1)}, bf16[128,640]{1,0:T(8,128)(2,1)S(1)}, u32[]{:S(2)}, u32[]{:S(2)}) collective-permute-start(bf16[128,640]{1,0:T(8,128)(2,1)S(1)} %get-tuple-element.56), channel_id=1, source_target_pairs={{0,4},{4,0},{8,12},{12,8},{16,20},{20,16},{24,28},{28,24},{1,5},{5... | collective-permute-start | bytes 491528 | tf_op jit(solution)/shard_map/ppermute | solution.py:329
  13.4 2.8 %collective-permute-start.8 = (bf16[128,640]{1,0:T(8,128)(2,1)S(1)}, bf16[128,640]{1,0:T(8,128)(2,1)S(1)}, u32[]{:S(2)}, u32[]{:S(2)}) collective-permute-start(bf16[128,640]{1,0:T(8,128)(2,1)S(1)} %get-tuple-element.57), channel_id=1, source_target_pairs={{0,4},{4,0},{8,12},{12,8},{16,20},{20,16},{24,28},{28,24},{1,5},{5... | collective-permute-start | bytes 491528 | tf_op jit(solution)/shard_map/ppermute | solution.py:329
  14.7 8.0 %collective-permute-start.6 = (bf16[320,640]{1,0:T(8,128)(2,1)S(1)}, bf16[320,640]{1,0:T(8,128)(2,1)S(1)}, u32[]{:S(2)}, u32[]{:S(2)}) collective-permute-start(bf16[320,640]{1,0:T(8,128)(2,1)S(1)} %get-tuple-element.93), channel_id=1, source_target_pairs={{0,16},{4,12},{8,24},{12,4},{16,0},{20,28},{24,8},{28,20},{1,17},{... | collective-permute-start | bytes 1228808 | tf_op jit(solution)/shard_map/ppermute | solution.py:333
  15.5 8.3 %collective-permute-start.4 = (bf16[320,512]{1,0:T(8,128)(2,1)S(1)}, bf16[320,512]{1,0:T(8,128)(2,1)S(1)}, u32[]{:S(2)}, u32[]{:S(2)}) collective-permute-start(bf16[320,512]{1,0:T(8,128)(2,1)S(1)} %collective-permute-done.1.refs_1_.near_ref), channel_id=1, source_target_pairs={{1,2},{2,1},{0,4},{3,7},{5,6},{6,5},{4,0},{7,3},{9,10},{10,9},{8,1... | collective-permute-start | bytes 983048 | tf_op jit(solution)/shard_map/ppermute | solution.py:343
  18.4 9.1 %collective-permute-start.10 = (bf16[320,512]{1,0:T(8,128)(2,1)S(1)}, bf16[320,512]{1,0:T(8,128)(2,1)S(1)}, u32[]{:S(2)}, u32[]{:S(2)}) collective-permute-start(bf16[320,512]{1,0:T(8,128)(2,1)S(1)} %shard_map.117), channel_id=1, source_target_pairs={{0,1},{1,0},{2,3},{3,2},{4,5},{5,4},{6,7},{7,6},{8,9},{9,8},{10,11... | collective-permute-start | bytes 983048 | tf_op jit(solution)/shard_map/ppermute | solution.py:336
  24.3 9.9 %collective-permute-start.9 = (bf16[320,512]{1,0:T(8,128)(2,1)S(1)}, bf16[320,512]{1,0:T(8,128)(2,1)S(1)}, u32[]{:S(2)}, u32[]{:S(2)}) collective-permute-start(bf16[320,512]{1,0:T(8,128)(2,1)S(1)} %shard_map.116), channel_id=1, source_target_pairs={{0,1},{1,0},{2,3},{3,2},{4,5},{5,4},{6,7},{7,6},{8,9},{9,8},{10,11... | collective-permute-start | bytes 983048 | tf_op jit(solution)/shard_map/ppermute | solution.py:336
  27.9 7.8 %collective-permute-start.13 = (bf16[320,512]{1,0:T(8,128)(2,1)S(1)}, bf16[320,512]{1,0:T(8,128)(2,1)S(1)}, u32[]{:S(2)}, u32[]{:S(2)}) collective-permute-start(bf16[320,512]{1,0:T(8,128)(2,1)S(1)} %shard_map.119), channel_id=1, source_target_pairs={{1,2},{2,1},{0,4},{3,7},{5,6},{6,5},{4,0},{7,3},{9,10},{10,9},{8,1... | collective-permute-start | bytes 983048 | tf_op jit(solution)/shard_map/ppermute | solution.py:343
  28.5 9.2 %collective-permute-start.11 = (bf16[160,640]{1,0:T(8,128)(2,1)S(1)}, bf16[160,640]{1,0:T(8,128)(2,1)S(1)}, u32[]{:S(2)}, u32[]{:S(2)}) collective-permute-start(bf16[160,640]{1,0:T(8,128)(2,1)S(1)} %get-tuple-element.67), channel_id=1, source_target_pairs={{0,8},{4,20},{8,0},{12,28},{16,24},{20,4},{24,16},{28,12},{1,9},{5... | collective-permute-start | bytes 614408 | tf_op jit(solution)/shard_map/ppermute | solution.py:333
  29.5 8.2 %collective-permute-start.12 = (bf16[160,640]{1,0:T(8,128)(2,1)S(1)}, bf16[160,640]{1,0:T(8,128)(2,1)S(1)}, u32[]{:S(2)}, u32[]{:S(2)}) collective-permute-start(bf16[160,640]{1,0:T(8,128)(2,1)S(1)} %get-tuple-element.68), channel_id=1, source_target_pairs={{0,8},{4,20},{8,0},{12,28},{16,24},{20,4},{24,16},{28,12},{1,9},{5... | collective-permute-start | bytes 614408 | tf_op jit(solution)/shard_map/ppermute | solution.py:333
  34.6 8.0 %collective-permute-start.14 = (bf16[320,640]{1,0:T(8,128)(2,1)S(1)}, bf16[320,640]{1,0:T(8,128)(2,1)S(1)}, u32[]{:S(2)}, u32[]{:S(2)}) collective-permute-start(bf16[320,640]{1,0:T(8,128)(2,1)S(1)} %get-tuple-element.69), channel_id=1, source_target_pairs={{0,8},{4,20},{8,0},{12,28},{16,24},{20,4},{24,16},{28,12},{1,9},{5... | collective-permute-start | bytes 1228808 | tf_op jit(solution)/shard_map/ppermute | solution.py:333
  36.2 8.9 %collective-permute-start.15 = (bf16[320,512]{1,0:T(8,128)(2,1)S(1)}, bf16[320,512]{1,0:T(8,128)(2,1)S(1)}, u32[]{:S(2)}, u32[]{:S(2)}) collective-permute-start(bf16[320,512]{1,0:T(8,128)(2,1)S(1)} %shard_map.121), channel_id=1, source_target_pairs={{0,1},{1,0},{2,3},{3,2},{4,5},{5,4},{6,7},{7,6},{8,9},{9,8},{10,11... | collective-permute-start | bytes 983048 | tf_op jit(solution)/shard_map/ppermute | solution.py:336
  38.2 6.9 %collective-permute-start.16 = (bf16[320,512]{1,0:T(8,128)(2,1)S(1)}, bf16[320,512]{1,0:T(8,128)(2,1)S(1)}, u32[]{:S(2)}, u32[]{:S(2)}) collective-permute-start(bf16[320,512]{1,0:T(8,128)(2,1)S(1)} %shard_map.123), channel_id=1, source_target_pairs={{1,2},{2,1},{0,4},{3,7},{5,6},{6,5},{4,0},{7,3},{9,10},{10,9},{8,1... | collective-permute-start | bytes 983048 | tf_op jit(solution)/shard_map/ppermute | solution.py:343
  42.9 8.0 %collective-permute-start.18 = (bf16[320,640]{1,0:T(8,128)(2,1)S(1)}, bf16[320,640]{1,0:T(8,128)(2,1)S(1)}, u32[]{:S(2)}, u32[]{:S(2)}) collective-permute-start(bf16[320,640]{1,0:T(8,128)(2,1)S(1)} %get-tuple-element.86), channel_id=1, source_target_pairs={{0,16},{4,12},{8,24},{12,4},{16,0},{20,28},{24,8},{28,20},{1,17},{... | collective-permute-start | bytes 1228808 | tf_op jit(solution)/shard_map/ppermute | solution.py:333
  45.0 1.7 %collective-permute-start.19 = (bf16[256,640]{1,0:T(8,128)(2,1)S(1)}, bf16[256,640]{1,0:T(8,128)(2,1)S(1)}, u32[]{:S(2)}, u32[]{:S(2)}) collective-permute-start(bf16[256,640]{1,0:T(8,128)(2,1)S(1)} %get-tuple-element.89), channel_id=1, source_target_pairs={{0,4},{4,0},{8,12},{12,8},{16,20},{20,16},{24,28},{28,24},{1,5},{5... | collective-permute-start | bytes 983048 | tf_op jit(solution)/shard_map/ppermute | solution.py:329
  45.6 3.7 %collective-permute-start.17 = (f32[320,256]{1,0:T(8,128)S(1)}, f32[320,256]{1,0:T(8,128)S(1)}, u32[]{:S(2)}, u32[]{:S(2)}) collective-permute-start(f32[320,256]{1,0:T(8,128)S(1)} %get-tuple-element.83), channel_id=1, source_target_pairs={{0,4},{4,0},{8,12},{12,8},{16,20},{20,16},{24,28},{28,24},{1,5},{5... | collective-permute-start | bytes 983048 | tf_op jit(solution)/shard_map/ppermute | solution.py:329
  46.7 2.5 %copy-start.4 = (bf16[256,640]{1,0:T(8,128)(2,1)S(1)}, bf16[256,640]{1,0:T(8,128)(2,1)}, u32[]{:S(2)}) copy-start(bf16[256,640]{1,0:T(8,128)(2,1)} %residual_ref.1) | copy-start | bytes 983044

commit v8 on v7

--- a/solution.py
+++ b/solution.py
@@ -286,12 +286,21 @@
 def weight_late_kernel(group, inner_ref, outer_ref, own_ref, other_ref, near, beyond, send, keep):
     late, first = late_slot(group), own_bits()[0]
     sends = (late & first) == first
-    rest = jnp.where(first_pair(group)[1], beyond[...], near[...])
+    with_near = first_pair(group)[1]
+
+    def send_part(part, rest):
+        send[...] = part.astype(BF16)
+        keep[...] = rest[...]
+
+    def send_rest(part, rest):
+        send[...] = rest[...].astype(BF16)
+        keep[...] = part
 
     def body(plane, unit_ref):
         part = weight_part(unit_ref, own_ref, other_ref)
-        send[...] = jnp.where(sends, part, rest).astype(BF16)
-        keep[...] = jnp.where(sends, rest, part)
+        for rest, chosen in ((beyond, with_near), (near, ~with_near)):
+            pl.when(chosen & sends)(lambda rest=rest: send_part(part, rest))
+            pl.when(chosen & ~sends)(lambda rest=rest: send_rest(part, rest))
 
     late_plane(inner_ref, outer_ref, body)
 

time: 52 us -> 52.1 us (level)
  no operation moved by 1% of the time
where the time goes in v8:
time: 52.1 us; the launch traced here: 51.9 us
  starting transfers between devices  19.7 us (38%)
  waiting for transfers between devices  17.5 us (34%)
  Pallas kernels  12.7 us (24%)
  local copies, waits for them, and re-layouts  1.04 us (2%)
  between operations  0.9 us (2%)
    pallas_call x19, Pallas kernels, call(): pl.pallas_call(kernel, out_shape=tuple(outs), in_specs=[pl.BlockSpec(memo...  12.7 us
    ppermute x7, waiting for transfers between devices, core_swap(): lax.ppermute(value, 'blk', [(i, i ^ group * bits[i % 2]) for i in range(b...  11.2 us
    ppermute x7, starting transfers between devices, core_swap(): lax.ppermute(value, 'blk', [(i, i ^ group * bits[i % 2]) for i in range(b...  9.55 us
    ppermute x4, starting transfers between devices, pair_swap(): return lax.ppermute(value, 'shard', [(0, 1), (1, 0), (2, 3), (3, 2)])  8.12 us
    ppermute x4, waiting for transfers between devices, pair_swap(): return lax.ppermute(value, 'shard', [(0, 1), (1, 0), (2, 3), (3, 2)])  4.19 us
    ppermute x5, waiting for transfers between devices, swap(): return lax.ppermute(value, 'blk', [(i, i ^ bit) for i in range(blk)])  2.11 us
    ppermute x5, starting transfers between devices, swap(): return lax.ppermute(value, 'blk', [(i, i ^ bit) for i in range(blk)])  1.19 us
  transfers between devices with their start and end apart: 20, of which 10 were waited for; matrix products, arithmetic and copies ran while one was open for 0% of the time, Pallas kernels for 23%

profile of v8, /device:TPU:0, one launch (start us, length us, event | category | flops | bytes accessed | tf_op | source)
XLA Modules:
  0.0 51.9 jit_solution(9465826072732089397)
XLA Ops:
  0.6 3.0 %collective-permute-start.3 = (bf16[320,640]{1,0:T(8,128)(2,1)}, bf16[320,640]{1,0:T(8,128)(2,1)S(1)}, u32[]{:S(2)}, u32[]{:S(2)}) collective-permute-start(bf16[320,640]{1,0:T(8,128)(2,1)} %bitcast.3), channel_id=1, source_target_pairs={{0,8},{4,20},{8,0},{12,28},{16,24},{20,4},{24,16},{28,12},{1,9},{5... | collective-permute-start | bytes 1228808 | tf_op jit(solution)/shard_map/ppermute | solution.py:342
  3.6 0.0 collective-permute-start
  3.7 1.0 %copy-done.5 = bf16[256,640]{1,0:T(8,128)(2,1)S(1)} copy-done((bf16[256,640]{1,0:T(8,128)(2,1)S(1)}, bf16[256,640]{1,0:T(8,128)(2,1)}, u32[]{:S(2)}) %copy-start.5) | copy-done | bytes 327704
  4.6 0.1 shard_map.110.own_ref
  4.8 0.0 copy-start.1
  4.8 0.0 copy-start.2
  4.8 0.0 copy-start.3
  4.8 0.0 copy-start.6
  4.8 0.6 %collective-permute-done.other_ref = bf16[256,640]{1,0:T(8,128)(2,1)S(1)} collective-permute-done((bf16[256,640]{1,0:T(8,128)(2,1)}, bf16[256,640]{1,0:T(8,128)(2,1)S(1)}, u32[]{:S(2)}, u32[]{:S(2)}) %collective-permute-start) | collective-permute-done | bytes 327712 | tf_op jit(solution)/shard_map/ppermute | solution.py:338
  5.5 0.1 shard_map.111.refs_0_.unit_ref
  5.6 1.6 %collective-permute-start.1 = (bf16[320,512]{1,0:T(8,128)(2,1)S(1)}, bf16[320,512]{1,0:T(8,128)(2,1)S(1)}, u32[]{:S(2)}, u32[]{:S(2)}) collective-permute-start(bf16[320,512]{1,0:T(8,128)(2,1)S(1)} %shard_map.111.refs_0_.unit_ref), channel_id=1, source_target_pairs={{0,1},{1,0},{2,3},{3,2},{4,5},{5,4},{6,7},{7,6},{8,9},{9,8},{10,11... | collective-permute-start | bytes 983048 | tf_op jit(solution)/shard_map/ppermute | solution.py:345
  7.3 0.0 collective-permute-start.2
  7.3 2.5 %collective-permute-done.3.refs_1_ = bf16[320,640]{1,0:T(8,128)(2,1)S(1)} collective-permute-done((bf16[320,640]{1,0:T(8,128)(2,1)}, bf16[320,640]{1,0:T(8,128)(2,1)S(1)}, u32[]{:S(2)}, u32[]{:S(2)}) %collective-permute-start.3) | collective-permute-done | bytes 409632 | tf_op jit(solution)/shard_map/ppermute | solution.py:342
  9.8 0.1 broadcast_select_fusion
  9.9 2.1 %collective-permute-start.5 = (bf16[320,640]{1,0:T(8,128)(2,1)S(1)}, bf16[320,640]{1,0:T(8,128)(2,1)S(1)}, u32[]{:S(2)}, u32[]{:S(2)}) collective-permute-start(bf16[320,640]{1,0:T(8,128)(2,1)S(1)} %get-tuple-element.94), channel_id=1, source_target_pairs={{0,16},{4,12},{8,24},{12,4},{16,0},{20,28},{24,8},{28,20},{1,17},{... | collective-permute-start | bytes 1228808 | tf_op jit(solution)/shard_map/ppermute | solution.py:342
  12.0 1.3 %shard_map.112 = (bf16[256,640]{1,0:T(8,128)(2,1)S(1)}, bf16[128,640]{1,0:T(8,128)(2,1)S(1)}, bf16[128,640]{1,0:T(8,128)(2,1)S(1)}, f32[5,256,256]{2,1,0:T(8,128)S(1)}) custom-call(bf16[256,640]{1,0:T(8,128)(2,1)S(1)} %copy-done.1, bf16[256,640]{1,0:T(8,128)(2,1)S(1)} %copy-done.2, bf16[256,640]{1,0:T(8,128)(2,1)S(1)} %copy-done.3, s32[1,256]{1,0:T(1,128)S(1)} %copy-done.6), custom_call_target="tpu_custom_call" | custom-call | flops 167772160 | bytes 2950144 | tf_op jit(solution)/shard_map/pallas_call | solution.py:25
  13.3 0.1 collective-permute-start.7
  13.4 0.5 collective-permute-start.8
  13.9 0.9 %collective-permute-done.7 = bf16[128,640]{1,0:T(8,128)(2,1)S(1)} collective-permute-done((bf16[128,640]{1,0:T(8,128)(2,1)S(1)}, bf16[128,640]{1,0:T(8,128)(2,1)S(1)}, u32[]{:S(2)}, u32[]{:S(2)}) %collective-permute-start.7) | collective-permute-done | bytes 163872 | tf_op jit(solution)/shard_map/ppermute | solution.py:338
  14.7 0.0 collective-permute-start.6
  14.8 0.7 %collective-permute-done.1.refs_1_.near_ref = bf16[320,512]{1,0:T(8,128)(2,1)S(1)} collective-permute-done((bf16[320,512]{1,0:T(8,128)(2,1)S(1)}, bf16[320,512]{1,0:T(8,128)(2,1)S(1)}, u32[]{:S(2)}, u32[]{:S(2)}) %collective-permute-start.1) | collective-permute-done | bytes 327712 | tf_op jit(solution)/shard_map/ppermute | solution.py:345
  15.5 0.0 collective-permute-done.2.refs_5_.refs_0_.refs_2_
  15.5 0.7 %collective-permute-start.4 = (bf16[320,512]{1,0:T(8,128)(2,1)S(1)}, bf16[320,512]{1,0:T(8,128)(2,1)S(1)}, u32[]{:S(2)}, u32[]{:S(2)}) collective-permute-start(bf16[320,512]{1,0:T(8,128)(2,1)S(1)} %collective-permute-done.1.refs_1_.near_ref), channel_id=1, source_target_pairs={{1,2},{2,1},{0,4},{3,7},{5,6},{6,5},{4,0},{7,3},{9,10},{10,9},{8,1... | collective-permute-start | bytes 983048 | tf_op jit(solution)/shard_map/ppermute | solution.py:352
  16.2 0.0 collective-permute-done.8
  16.2 1.7 %collective-permute-done.5.refs_2_ = bf16[320,640]{1,0:T(8,128)(2,1)S(1)} collective-permute-done((bf16[320,640]{1,0:T(8,128)(2,1)S(1)}, bf16[320,640]{1,0:T(8,128)(2,1)S(1)}, u32[]{:S(2)}, u32[]{:S(2)}) %collective-permute-start.5) | collective-permute-done | bytes 409632 | tf_op jit(solution)/shard_map/ppermute | solution.py:342
  17.9 0.4 shard_map.117
  18.4 1.7 %collective-permute-start.10 = (bf16[320,512]{1,0:T(8,128)(2,1)S(1)}, bf16[320,512]{1,0:T(8,128)(2,1)S(1)}, u32[]{:S(2)}, u32[]{:S(2)}) collective-permute-start(bf16[320,512]{1,0:T(8,128)(2,1)S(1)} %shard_map.117), channel_id=1, source_target_pairs={{0,1},{1,0},{2,3},{3,2},{4,5},{5,4},{6,7},{7,6},{8,9},{9,8},{10,11... | collective-permute-start | bytes 983048 | tf_op jit(solution)/shard_map/ppermute | solution.py:345
  20.1 0.7 %shard_map.115 = (f32[320,640]{1,0:T(8,128)S(1)}, f32[320,640]{1,0:T(8,128)S(1)}) custom-call(bf16[320,512]{1,0:T(8,128)(2,1)S(1)} %shard_map.111.refs_0_.unit_ref, bf16[320,512]{1,0:T(8,128)(2,1)S(1)} %collective-permute-done.1.refs_1_.near_ref, bf16[256,640]{1,0:T(8,128)(2,1)S(1)} %get-tuple-element.55.own_ref.refs_1_.refs_3_.refs_2_, ...), custom_call_target="tpu_custom_call" | custom-call | flops 419430400 | bytes 2949120 | tf_op jit(solution)/shard_map/pallas_call | solution.py:25
  20.8 1.9 %collective-permute-done.6.refs_3_ = bf16[320,640]{1,0:T(8,128)(2,1)S(1)} collective-permute-done((bf16[320,640]{1,0:T(8,128)(2,1)S(1)}, bf16[320,640]{1,0:T(8,128)(2,1)S(1)}, u32[]{:S(2)}, u32[]{:S(2)}) %collective-permute-start.6) | collective-permute-done | bytes 409632 | tf_op jit(solution)/shard_map/ppermute | solution.py:342
  22.7 0.1 shard_map.113.refs_2_.refs_0_.refs_4_
  22.8 0.9 %shard_map.114.refs_5_ = f32[512,640]{1,0:T(8,128)S(1)} custom-call(bf16[320,512]{1,0:T(8,128)(2,1)S(1)} %shard_map.111.refs_0_.unit_ref, bf16[320,512]{1,0:T(8,128)(2,1)S(1)} %collective-permute-done.1.refs_1_.near_ref, bf16[4,320,640]{2,1,0:T(8,128)(2,1)S(1)} %shard_map.113.refs_2_.refs_0_.refs_4_), custom_call_target="tpu_custom_call" | custom-call | flops 419430400 | bytes 3604480 | tf_op jit(solution)/shard_map/pallas_call | solution.py:25
  23.8 0.0 collective-permute-done.4.refs_3_.refs_1_
  23.8 0.5 shard_map.116
  24.3 3.2 %collective-permute-start.9 = (bf16[320,512]{1,0:T(8,128)(2,1)S(1)}, bf16[320,512]{1,0:T(8,128)(2,1)S(1)}, u32[]{:S(2)}, u32[]{:S(2)}) collective-permute-start(bf16[320,512]{1,0:T(8,128)(2,1)S(1)} %shard_map.116), channel_id=1, source_target_pairs={{0,1},{1,0},{2,3},{3,2},{4,5},{5,4},{6,7},{7,6},{8,9},{9,8},{10,11... | collective-permute-start | bytes 983048 | tf_op jit(solution)/shard_map/ppermute | solution.py:345
  27.5 0.0 collective-permute-done.10.refs_0_.refs_3_
  27.5 0.4 shard_map.119
  27.9 0.1 collective-permute-start.13
  28.0 0.5 shard_map.118
  28.5 1.0 %collective-permute-start.11 = (bf16[160,640]{1,0:T(8,128)(2,1)S(1)}, bf16[160,640]{1,0:T(8,128)(2,1)S(1)}, u32[]{:S(2)}, u32[]{:S(2)}) collective-permute-start(bf16[160,640]{1,0:T(8,128)(2,1)S(1)} %get-tuple-element.67), channel_id=1, source_target_pairs={{0,8},{4,20},{8,0},{12,28},{16,24},{20,4},{24,16},{28,12},{1,9},{5... | collective-permute-start | bytes 614408 | tf_op jit(solution)/shard_map/ppermute | solution.py:342
  29.5 1.1 %collective-permute-start.12 = (bf16[160,640]{1,0:T(8,128)(2,1)S(1)}, bf16[160,640]{1,0:T(8,128)(2,1)S(1)}, u32[]{:S(2)}, u32[]{:S(2)}) collective-permute-start(bf16[160,640]{1,0:T(8,128)(2,1)S(1)} %get-tuple-element.68), channel_id=1, source_target_pairs={{0,8},{4,20},{8,0},{12,28},{16,24},{20,4},{24,16},{28,12},{1,9},{5... | collective-permute-start | bytes 614408 | tf_op jit(solution)/shard_map/ppermute | solution.py:342
  30.6 3.5 %collective-permute-done.9.refs_1_.refs_3_ = bf16[320,512]{1,0:T(8,128)(2,1)S(1)} collective-permute-done((bf16[320,512]{1,0:T(8,128)(2,1)S(1)}, bf16[320,512]{1,0:T(8,128)(2,1)S(1)}, u32[]{:S(2)}, u32[]{:S(2)}) %collective-permute-start.9) | collective-permute-done | bytes 327712 | tf_op jit(solution)/shard_map/ppermute | solution.py:345
  34.1 0.5 %shard_map.120 = (bf16[320,640]{1,0:T(8,128)(2,1)S(1)}, f32[320,640]{1,0:T(8,128)S(1)}) custom-call(bf16[320,512]{1,0:T(8,128)(2,1)S(1)} %collective-permute-done.2.refs_5_.refs_0_.refs_2_, bf16[320,512]{1,0:T(8,128)(2,1)S(1)} %collective-permute-done.9.refs_1_.refs_3_, bf16[256,640]{1,0:T(8,128)(2,1)S(1)} %get-tuple-element.55.own_ref.refs_1_.refs_3_.refs_2_, ...), custom_call_target="tpu_custom_call" | custom-call | flops 209715200 | bytes 4177920 | tf_op jit(solution)/shard_map/pallas_call | solution.py:25
  34.7 1.1 %collective-permute-start.14 = (bf16[320,640]{1,0:T(8,128)(2,1)S(1)}, bf16[320,640]{1,0:T(8,128)(2,1)S(1)}, u32[]{:S(2)}, u32[]{:S(2)}) collective-permute-start(bf16[320,640]{1,0:T(8,128)(2,1)S(1)} %get-tuple-element.69), channel_id=1, source_target_pairs={{0,8},{4,20},{8,0},{12,28},{16,24},{20,4},{24,16},{28,12},{1,9},{5... | collective-permute-start | bytes 1228808 | tf_op jit(solution)/shard_map/ppermute | solution.py:342
  35.8 0.0 collective-permute-done.13.refs_3_
  35.8 0.4 shard_map.121
  36.3 1.5 %collective-permute-start.15 = (bf16[320,512]{1,0:T(8,128)(2,1)S(1)}, bf16[320,512]{1,0:T(8,128)(2,1)S(1)}, u32[]{:S(2)}, u32[]{:S(2)}) collective-permute-start(bf16[320,512]{1,0:T(8,128)(2,1)S(1)} %shard_map.121), channel_id=1, source_target_pairs={{0,1},{1,0},{2,3},{3,2},{4,5},{5,4},{6,7},{7,6},{8,9},{9,8},{10,11... | collective-permute-start | bytes 983048 | tf_op jit(solution)/shard_map/ppermute | solution.py:345
  37.8 0.0 collective-permute-done.11.refs_3_
  37.8 0.0 collective-permute-done.12.refs_4_
  37.8 0.4 shard_map.123
  38.2 0.1 collective-permute-start.16
  38.3 4.4 %collective-permute-done.14.refs_6_ = bf16[320,640]{1,0:T(8,128)(2,1)S(1)} collective-permute-done((bf16[320,640]{1,0:T(8,128)(2,1)S(1)}, bf16[320,640]{1,0:T(8,128)(2,1)S(1)}, u32[]{:S(2)}, u32[]{:S(2)}) %collective-permute-start.14) | collective-permute-done | bytes 409632 | tf_op jit(solution)/shard_map/ppermute | solution.py:342
  42.7 0.2 shard_map.122
  42.9 1.2 %collective-permute-start.18 = (bf16[320,640]{1,0:T(8,128)(2,1)S(1)}, bf16[320,640]{1,0:T(8,128)(2,1)S(1)}, u32[]{:S(2)}, u32[]{:S(2)}) collective-permute-start(bf16[320,640]{1,0:T(8,128)(2,1)S(1)} %get-tuple-element.86), channel_id=1, source_target_pairs={{0,16},{4,12},{8,24},{12,4},{16,0},{20,28},{24,8},{28,20},{1,17},{... | collective-permute-start | bytes 1228808 | tf_op jit(solution)/shard_map/ppermute | solution.py:342
  44.1 0.9 %shard_map.124 = (f32[256,640]{1,0:T(8,128)S(1)}, bf16[256,640]{1,0:T(8,128)(2,1)S(1)}) custom-call(bf16[320,512]{1,0:T(8,128)(2,1)S(1)} %collective-permute-done.10.refs_0_.refs_3_, bf16[320,512]{1,0:T(8,128)(2,1)S(1)} %collective-permute-done.4.refs_3_.refs_1_, bf16[320,512]{1,0:T(8,128)(2,1)S(1)} %collective-permute-done.2.refs_5_.refs_0_.refs_2_, ...), custom_call_target="tpu_custom_call" | custom-call | flops 419430400 | bytes 5242880 | tf_op jit(solution)/shard_map/pallas_call | solution.py:25
  45.0 0.1 collective-permute-start.19
  45.1 0.0 collective-permute-done.15.refs_3_
  45.1 0.0 collective-permute-done.16.refs_4_
  45.1 0.5 shard_map.125
  45.6 0.5 %collective-permute-start.17 = (f32[320,256]{1,0:T(8,128)S(1)}, f32[320,256]{1,0:T(8,128)S(1)}, u32[]{:S(2)}, u32[]{:S(2)}) collective-permute-start(f32[320,256]{1,0:T(8,128)S(1)} %get-tuple-element.83), channel_id=1, source_target_pairs={{0,4},{4,0},{8,12},{12,8},{16,20},{20,16},{24,28},{28,24},{1,5},{5... | collective-permute-start | bytes 983048 | tf_op jit(solution)/shard_map/ppermute | solution.py:338
  46.2 0.6 %collective-permute-done.19.other_ref = bf16[256,640]{1,0:T(8,128)(2,1)S(1)} collective-permute-done((bf16[256,640]{1,0:T(8,128)(2,1)S(1)}, bf16[256,640]{1,0:T(8,128)(2,1)S(1)}, u32[]{:S(2)}, u32[]{:S(2)}) %collective-permute-start.19) | collective-permute-done | bytes 327712 | tf_op jit(solution)/shard_map/ppermute | solution.py:338
  46.7 2.5 %shard_map.128 = (bf16[256,640]{1,0:T(8,128)(2,1)}, bf16[256,640]{1,0:T(8,128)(2,1)}, bf16[256,640]{1,0:T(8,128)(2,1)}) custom-call(bf16[256,640]{1,0:T(8,128)(2,1)S(1)} %copy-done.1, bf16[256,640]{1,0:T(8,128)(2,1)S(1)} %copy-done.2, bf16[256,640]{1,0:T(8,128)(2,1)S(1)} %copy-done.3, f32[5,256,256]{2,1,0:T(8,128)S(1)} %get-tuple-element.87.probs_ref, ...), custom_call_target="tpu_custom_call" | custom-call | flops 419430400 | bytes 4259840 | tf_op jit(solution)/shard_map/pallas_call | solution.py:25
  49.3 1.0 %shard_map.126 = bf16[256,640]{1,0:T(8,128)(2,1)} custom-call(bf16[256,640]{1,0:T(8,128)(2,1)S(1)} %copy-done.4, f32[320,256]{1,0:T(8,128)S(1)} %get-tuple-element.82.keep_ref, f32[320,256]{1,0:T(8,128)S(1)} %collective-permute-done.17.other_ref), custom_call_target="tpu_custom_call" | custom-call | bytes 1310720 | tf_op jit(solution)/shard_map/pallas_call | solution.py:25
  50.2 0.7 %collective-permute-done.18.refs_1_ = bf16[320,640]{1,0:T(8,128)(2,1)S(1)} collective-permute-done((bf16[320,640]{1,0:T(8,128)(2,1)S(1)}, bf16[320,640]{1,0:T(8,128)(2,1)S(1)}, u32[]{:S(2)}, u32[]{:S(2)}) %collective-permute-start.18) | collective-permute-done | bytes 409632 | tf_op jit(solution)/shard_map/ppermute | solution.py:342
  50.9 1.0 %shard_map.127 = f32[320,640]{1,0:T(8,128)} custom-call(f32[320,640]{1,0:T(8,128)S(1)} %get-tuple-element.85.refs_0_, bf16[320,640]{1,0:T(8,128)(2,1)S(1)} %collective-permute-done.18.refs_1_), custom_call_target="tpu_custom_call" | custom-call | bytes 2048000 | tf_op jit(solution)/shard_map/pallas_call | solution.py:25
  (12 shorter events, 0.1 us)
Async XLA Ops:
  0.6 9.2 %copy-start = (bf16[640,320]{0,1:T(8,128)(2,1)S(1)}, bf16[640,320]{0,1:T(8,128)(2,1)}, u32[]{:S(2)}) copy-start(bf16[640,320]{0,1:T(8,128)(2,1)} %param.12) | copy-start | bytes 1228804
  0.6 9.1 %collective-permute-start.3 = (bf16[320,640]{1,0:T(8,128)(2,1)}, bf16[320,640]{1,0:T(8,128)(2,1)S(1)}, u32[]{:S(2)}, u32[]{:S(2)}) collective-permute-start(bf16[320,640]{1,0:T(8,128)(2,1)} %bitcast.3), channel_id=1, source_target_pairs={{0,8},{4,20},{8,0},{12,28},{16,24},{20,4},{24,16},{28,12},{1,9},{5... | collective-permute-start | bytes 1228808 | tf_op jit(solution)/shard_map/ppermute | solution.py:342
  3.6 1.8 %collective-permute-start = (bf16[256,640]{1,0:T(8,128)(2,1)}, bf16[256,640]{1,0:T(8,128)(2,1)S(1)}, u32[]{:S(2)}, u32[]{:S(2)}) collective-permute-start(bf16[256,640]{1,0:T(8,128)(2,1)} %own_ref.1), channel_id=1, source_target_pairs={{0,4},{4,0},{8,12},{12,8},{16,20},{20,16},{24,28},{28,24},{1,5},{5... | collective-permute-start | bytes 983048 | tf_op jit(solution)/shard_map/ppermute | solution.py:338
  3.6 1.0 %copy-start.5 = (bf16[256,640]{1,0:T(8,128)(2,1)S(1)}, bf16[256,640]{1,0:T(8,128)(2,1)}, u32[]{:S(2)}) copy-start(bf16[256,640]{1,0:T(8,128)(2,1)} %own_ref.1) | copy-start | bytes 983044
  4.8 7.2 %copy-start.1 = (bf16[256,640]{1,0:T(8,128)(2,1)S(1)}, bf16[256,640]{1,0:T(8,128)(2,1)}, u32[]{:S(2)}) copy-start(bf16[256,640]{1,0:T(8,128)(2,1)} %q_ref.2) | copy-start | bytes 983044
  4.8 7.2 %copy-start.2 = (bf16[256,640]{1,0:T(8,128)(2,1)S(1)}, bf16[256,640]{1,0:T(8,128)(2,1)}, u32[]{:S(2)}) copy-start(bf16[256,640]{1,0:T(8,128)(2,1)} %k_ref.3) | copy-start | bytes 983044
  4.8 7.2 %copy-start.3 = (bf16[256,640]{1,0:T(8,128)(2,1)S(1)}, bf16[256,640]{1,0:T(8,128)(2,1)}, u32[]{:S(2)}) copy-start(bf16[256,640]{1,0:T(8,128)(2,1)} %v_ref.3) | copy-start | bytes 983044
  4.8 7.2 %copy-start.6 = (s32[1,256]{1,0:T(1,128)S(1)}, s32[1,256]{1,0:T(1,128)}, u32[]{:S(2)}) copy-start(s32[1,256]{1,0:T(1,128)} %seg_ref.1) | copy-start | bytes 3076
  5.6 9.8 %collective-permute-start.1 = (bf16[320,512]{1,0:T(8,128)(2,1)S(1)}, bf16[320,512]{1,0:T(8,128)(2,1)S(1)}, u32[]{:S(2)}, u32[]{:S(2)}) collective-permute-start(bf16[320,512]{1,0:T(8,128)(2,1)S(1)} %shard_map.111.refs_0_.unit_ref), channel_id=1, source_target_pairs={{0,1},{1,0},{2,3},{3,2},{4,5},{5,4},{6,7},{7,6},{8,9},{9,8},{10,11... | collective-permute-start | bytes 983048 | tf_op jit(solution)/shard_map/ppermute | solution.py:345
  7.3 8.2 %collective-permute-start.2 = (bf16[320,512]{1,0:T(8,128)(2,1)S(1)}, bf16[320,512]{1,0:T(8,128)(2,1)S(1)}, u32[]{:S(2)}, u32[]{:S(2)}) collective-permute-start(bf16[320,512]{1,0:T(8,128)(2,1)S(1)} %shard_map.111.refs_0_.unit_ref), channel_id=1, source_target_pairs={{1,2},{2,1},{0,4},{3,7},{5,6},{6,5},{4,0},{7,3},{9,10},{10,9},{8,1... | collective-permute-start | bytes 983048 | tf_op jit(solution)/shard_map/ppermute | solution.py:352
  9.9 8.0 %collective-permute-start.5 = (bf16[320,640]{1,0:T(8,128)(2,1)S(1)}, bf16[320,640]{1,0:T(8,128)(2,1)S(1)}, u32[]{:S(2)}, u32[]{:S(2)}) collective-permute-start(bf16[320,640]{1,0:T(8,128)(2,1)S(1)} %get-tuple-element.94), channel_id=1, source_target_pairs={{0,16},{4,12},{8,24},{12,4},{16,0},{20,28},{24,8},{28,20},{1,17},{... | collective-permute-start | bytes 1228808 | tf_op jit(solution)/shard_map/ppermute | solution.py:342
  13.3 1.5 %collective-permute-start.7 = (bf16[128,640]{1,0:T(8,128)(2,1)S(1)}, bf16[128,640]{1,0:T(8,128)(2,1)S(1)}, u32[]{:S(2)}, u32[]{:S(2)}) collective-permute-start(bf16[128,640]{1,0:T(8,128)(2,1)S(1)} %get-tuple-element.56), channel_id=1, source_target_pairs={{0,4},{4,0},{8,12},{12,8},{16,20},{20,16},{24,28},{28,24},{1,5},{5... | collective-permute-start | bytes 491528 | tf_op jit(solution)/shard_map/ppermute | solution.py:338
  13.4 2.8 %collective-permute-start.8 = (bf16[128,640]{1,0:T(8,128)(2,1)S(1)}, bf16[128,640]{1,0:T(8,128)(2,1)S(1)}, u32[]{:S(2)}, u32[]{:S(2)}) collective-permute-start(bf16[128,640]{1,0:T(8,128)(2,1)S(1)} %get-tuple-element.57), channel_id=1, source_target_pairs={{0,4},{4,0},{8,12},{12,8},{16,20},{20,16},{24,28},{28,24},{1,5},{5... | collective-permute-start | bytes 491528 | tf_op jit(solution)/shard_map/ppermute | solution.py:338
  14.7 8.0 %collective-permute-start.6 = (bf16[320,640]{1,0:T(8,128)(2,1)S(1)}, bf16[320,640]{1,0:T(8,128)(2,1)S(1)}, u32[]{:S(2)}, u32[]{:S(2)}) collective-permute-start(bf16[320,640]{1,0:T(8,128)(2,1)S(1)} %get-tuple-element.93), channel_id=1, source_target_pairs={{0,16},{4,12},{8,24},{12,4},{16,0},{20,28},{24,8},{28,20},{1,17},{... | collective-permute-start | bytes 1228808 | tf_op jit(solution)/shard_map/ppermute | solution.py:342
  15.5 8.3 %collective-permute-start.4 = (bf16[320,512]{1,0:T(8,128)(2,1)S(1)}, bf16[320,512]{1,0:T(8,128)(2,1)S(1)}, u32[]{:S(2)}, u32[]{:S(2)}) collective-permute-start(bf16[320,512]{1,0:T(8,128)(2,1)S(1)} %collective-permute-done.1.refs_1_.near_ref), channel_id=1, source_target_pairs={{1,2},{2,1},{0,4},{3,7},{5,6},{6,5},{4,0},{7,3},{9,10},{10,9},{8,1... | collective-permute-start | bytes 983048 | tf_op jit(solution)/shard_map/ppermute | solution.py:352
  18.4 9.1 %collective-permute-start.10 = (bf16[320,512]{1,0:T(8,128)(2,1)S(1)}, bf16[320,512]{1,0:T(8,128)(2,1)S(1)}, u32[]{:S(2)}, u32[]{:S(2)}) collective-permute-start(bf16[320,512]{1,0:T(8,128)(2,1)S(1)} %shard_map.117), channel_id=1, source_target_pairs={{0,1},{1,0},{2,3},{3,2},{4,5},{5,4},{6,7},{7,6},{8,9},{9,8},{10,11... | collective-permute-start | bytes 983048 | tf_op jit(solution)/shard_map/ppermute | solution.py:345
  24.3 9.9 %collective-permute-start.9 = (bf16[320,512]{1,0:T(8,128)(2,1)S(1)}, bf16[320,512]{1,0:T(8,128)(2,1)S(1)}, u32[]{:S(2)}, u32[]{:S(2)}) collective-permute-start(bf16[320,512]{1,0:T(8,128)(2,1)S(1)} %shard_map.116), channel_id=1, source_target_pairs={{0,1},{1,0},{2,3},{3,2},{4,5},{5,4},{6,7},{7,6},{8,9},{9,8},{10,11... | collective-permute-start | bytes 983048 | tf_op jit(solution)/shard_map/ppermute | solution.py:345
  27.9 7.9 %collective-permute-start.13 = (bf16[320,512]{1,0:T(8,128)(2,1)S(1)}, bf16[320,512]{1,0:T(8,128)(2,1)S(1)}, u32[]{:S(2)}, u32[]{:S(2)}) collective-permute-start(bf16[320,512]{1,0:T(8,128)(2,1)S(1)} %shard_map.119), channel_id=1, source_target_pairs={{1,2},{2,1},{0,4},{3,7},{5,6},{6,5},{4,0},{7,3},{9,10},{10,9},{8,1... | collective-permute-start | bytes 983048 | tf_op jit(solution)/shard_map/ppermute | solution.py:352
  28.5 9.3 %collective-permute-start.11 = (bf16[160,640]{1,0:T(8,128)(2,1)S(1)}, bf16[160,640]{1,0:T(8,128)(2,1)S(1)}, u32[]{:S(2)}, u32[]{:S(2)}) collective-permute-start(bf16[160,640]{1,0:T(8,128)(2,1)S(1)} %get-tuple-element.67), channel_id=1, source_target_pairs={{0,8},{4,20},{8,0},{12,28},{16,24},{20,4},{24,16},{28,12},{1,9},{5... | collective-permute-start | bytes 614408 | tf_op jit(solution)/shard_map/ppermute | solution.py:342
  29.5 8.3 %collective-permute-start.12 = (bf16[160,640]{1,0:T(8,128)(2,1)S(1)}, bf16[160,640]{1,0:T(8,128)(2,1)S(1)}, u32[]{:S(2)}, u32[]{:S(2)}) collective-permute-start(bf16[160,640]{1,0:T(8,128)(2,1)S(1)} %get-tuple-element.68), channel_id=1, source_target_pairs={{0,8},{4,20},{8,0},{12,28},{16,24},{20,4},{24,16},{28,12},{1,9},{5... | collective-permute-start | bytes 614408 | tf_op jit(solution)/shard_map/ppermute | solution.py:342
  34.7 8.0 %collective-permute-start.14 = (bf16[320,640]{1,0:T(8,128)(2,1)S(1)}, bf16[320,640]{1,0:T(8,128)(2,1)S(1)}, u32[]{:S(2)}, u32[]{:S(2)}) collective-permute-start(bf16[320,640]{1,0:T(8,128)(2,1)S(1)} %get-tuple-element.69), channel_id=1, source_target_pairs={{0,8},{4,20},{8,0},{12,28},{16,24},{20,4},{24,16},{28,12},{1,9},{5... | collective-permute-start | bytes 1228808 | tf_op jit(solution)/shard_map/ppermute | solution.py:342
  36.3 8.9 %collective-permute-start.15 = (bf16[320,512]{1,0:T(8,128)(2,1)S(1)}, bf16[320,512]{1,0:T(8,128)(2,1)S(1)}, u32[]{:S(2)}, u32[]{:S(2)}) collective-permute-start(bf16[320,512]{1,0:T(8,128)(2,1)S(1)} %shard_map.121), channel_id=1, source_target_pairs={{0,1},{1,0},{2,3},{3,2},{4,5},{5,4},{6,7},{7,6},{8,9},{9,8},{10,11... | collective-permute-start | bytes 983048 | tf_op jit(solution)/shard_map/ppermute | solution.py:345
  38.2 6.9 %collective-permute-start.16 = (bf16[320,512]{1,0:T(8,128)(2,1)S(1)}, bf16[320,512]{1,0:T(8,128)(2,1)S(1)}, u32[]{:S(2)}, u32[]{:S(2)}) collective-permute-start(bf16[320,512]{1,0:T(8,128)(2,1)S(1)} %shard_map.123), channel_id=1, source_target_pairs={{1,2},{2,1},{0,4},{3,7},{5,6},{6,5},{4,0},{7,3},{9,10},{10,9},{8,1... | collective-permute-start | bytes 983048 | tf_op jit(solution)/shard_map/ppermute | solution.py:352
  42.9 8.0 %collective-permute-start.18 = (bf16[320,640]{1,0:T(8,128)(2,1)S(1)}, bf16[320,640]{1,0:T(8,128)(2,1)S(1)}, u32[]{:S(2)}, u32[]{:S(2)}) collective-permute-start(bf16[320,640]{1,0:T(8,128)(2,1)S(1)} %get-tuple-element.86), channel_id=1, source_target_pairs={{0,16},{4,12},{8,24},{12,4},{16,0},{20,28},{24,8},{28,20},{1,17},{... | collective-permute-start | bytes 1228808 | tf_op jit(solution)/shard_map/ppermute | solution.py:342
  45.0 1.7 %collective-permute-start.19 = (bf16[256,640]{1,0:T(8,128)(2,1)S(1)}, bf16[256,640]{1,0:T(8,128)(2,1)S(1)}, u32[]{:S(2)}, u32[]{:S(2)}) collective-permute-start(bf16[256,640]{1,0:T(8,128)(2,1)S(1)} %get-tuple-element.89), channel_id=1, source_target_pairs={{0,4},{4,0},{8,12},{12,8},{16,20},{20,16},{24,28},{28,24},{1,5},{5... | collective-permute-start | bytes 983048 | tf_op jit(solution)/shard_map/ppermute | solution.py:338
  45.6 3.7 %collective-permute-start.17 = (f32[320,256]{1,0:T(8,128)S(1)}, f32[320,256]{1,0:T(8,128)S(1)}, u32[]{:S(2)}, u32[]{:S(2)}) collective-permute-start(f32[320,256]{1,0:T(8,128)S(1)} %get-tuple-element.83), channel_id=1, source_target_pairs={{0,4},{4,0},{8,12},{12,8},{16,20},{20,16},{24,28},{28,24},{1,5},{5... | collective-permute-start | bytes 983048 | tf_op jit(solution)/shard_map/ppermute | solution.py:338
  46.7 2.5 %copy-start.4 = (bf16[256,640]{1,0:T(8,128)(2,1)S(1)}, bf16[256,640]{1,0:T(8,128)(2,1)}, u32[]{:S(2)}) copy-start(bf16[256,640]{1,0:T(8,128)(2,1)} %residual_ref.1) | copy-start | bytes 983044
